TPU v7x, 128 devices: a whole 4x4x4 slice. The times are simulated.
128 devices in a mesh: lat: 16 (over y, x), chan: 8 (over z, core).
Axes of the slice: x: 4, y: 4, z: 4, core: 2. Of those that a mesh axis runs over, the one named last changes fastest.
Arguments:
- atmos: bfloat16 [384, 720, 1440], P('chan', 'lat'), may hold values from -6 to 6
- sea_temp_gain: bfloat16 [384], P('chan'), may hold values from -4 to 4
- legendre_analysis: bfloat16 [256, 256, 720], P(('lat', 'chan')), may hold values from -0.21875 to 0.21875
- legendre_synthesis: bfloat16 [256, 720, 256], P(('lat', 'chan')), may hold values from -0.375 to 0.375
- spectral_mixing_weight: bfloat16 [2, 384, 384], replicated, may hold values from -0.21875 to 0.21875
- surface_flux_weight: bfloat16 [4, 384], P(None, 'chan'), may hold values from -0.3125 to 0.3125
- flux_ocean_forcing: float32 [76, 4], replicated, may hold values from -3 to 3
- ocean: bfloat16 [76, 720, 1440], P(None, 'lat', 'chan'), may hold values from -6 to 6
- ocean_tile_mask: int32 [80, 40], P('lat', 'chan'), may hold values 0 or 1
- depthwise_filter: bfloat16 [76, 1, 7, 7], replicated, may hold values from -0.875 to 0.875
- norm_gain_vector: float32 [76], replicated, may hold values from 0.5 to 1.5
- expand_matrix: bfloat16 [304, 76], replicated, may hold values from -0.625 to 0.625
- contract_matrix: bfloat16 [76, 304], replicated, may hold values from -0.3125 to 0.3125
Outputs:
- atmos_next: bfloat16 [384, 720, 1440], P('chan', 'lat')
- ocean_next: bfloat16 [76, 720, 1440], P(None, 'lat', 'chan')
All inputs are finite; a program needn't handle non-finite values. No bound on the sum of `ocean_tile_mask` on one device may be relied on, other than what follows from the above.
Results may differ from a plain program's by a relative error of at most 0.015.
Values may be sent and summed in bfloat16 or wider, within the bound.
No kernel may reach another device: no remote copies, remote signals or barrier semaphores. Data moves between devices by JAX's collectives and lax.ppermute only.
A program may use at most 128 MiB of HBM per device.

v0:
```python
import math

import jax
import jax.numpy as jnp
from jax import lax
from jax.sharding import PartitionSpec as P


def with_halo(block, sides, width):
    for axis, dim in sides:
        count = lax.axis_size(axis)
        forward = [(i, i + 1) for i in range(count - 1)]
        backward = [(target, source) for source, target in forward]
        low = lax.ppermute(
            lax.slice_in_dim(block, block.shape[dim] - width, None, axis=dim), axis, forward
        )
        high = lax.ppermute(lax.slice_in_dim(block, 0, width, axis=dim), axis, backward)
        block = jnp.concatenate([low, block, high], axis=dim)
    return block


def forward_table(lon_len, total_modes):
    product = (
        jnp.arange(lon_len, dtype=jnp.int32)[:, None]
        * jnp.arange(total_modes, dtype=jnp.int32)[None, :]
    )
    angle = 2.0 * math.pi / lon_len * (product % lon_len).astype(jnp.float32)
    factor = math.sqrt(2.0 / lon_len)
    return jnp.stack([factor * jnp.cos(angle), -factor * jnp.sin(angle)], axis=2).astype(
        jnp.bfloat16
    )


def inverse_table(lon_len, mode_ids, total_modes):
    product = mode_ids[:, None] * jnp.arange(lon_len, dtype=jnp.int32)[None, :]
    angle = 2.0 * math.pi / lon_len * (product % lon_len).astype(jnp.float32)
    factor = 1.0 / math.sqrt(total_modes)
    return jnp.stack([factor * jnp.cos(angle), -factor * jnp.sin(angle)], axis=1).astype(
        jnp.bfloat16
    )


def body(
    atmos,
    sea_temp_gain,
    legendre_analysis,
    legendre_synthesis,
    spectral_mixing_weight,
    surface_flux_weight,
    flux_ocean_forcing,
    ocean,
    ocean_tile_mask,
    depthwise_filter,
    norm_gain_vector,
    expand_matrix,
    contract_matrix,
):
    lat_parts = lax.axis_size("lat")
    chan_parts = lax.axis_size("chan")
    local_ch = atmos.shape[0]
    local_rows = atmos.shape[1]
    lon_len = atmos.shape[2]
    per_dev = legendre_analysis.shape[0]
    total_modes = per_dev * lat_parts * chan_parts
    ocean_ch = ocean.shape[0]
    ocean_cols = ocean.shape[2]
    sea_temp_line = lax.all_gather(ocean[0], "chan", axis=1, tiled=True)
    forced_ocean = (
        atmos.astype(jnp.float32)
        + sea_temp_gain.astype(jnp.float32)[:, None, None] * sea_temp_line.astype(jnp.float32)[None]
    )
    rounded = forced_ocean.astype(jnp.bfloat16)
    forward_flat = forward_table(lon_len, total_modes).reshape(lon_len, total_modes * 2)
    fourier_flat = lax.dot_general(
        forward_flat,
        rounded.reshape(local_ch * local_rows, lon_len),
        (((0,), (1,)), ((), ())),
        preferred_element_type=jnp.float32,
    )
    fourier = fourier_flat.reshape(total_modes, 2, local_ch, local_rows).astype(jnp.bfloat16)
    gathered = lax.all_to_all(
        lax.all_to_all(fourier, "lat", split_axis=0, concat_axis=3, tiled=True),
        "chan",
        split_axis=0,
        concat_axis=2,
        tiled=True,
    )
    spectrum = jnp.einsum(
        "mkcr,mlr->mkcl", gathered, legendre_analysis, preferred_element_type=jnp.float32
    ).astype(jnp.bfloat16)
    real_part = spectral_mixing_weight[0]
    imag_part = spectral_mixing_weight[1]
    coupling = jnp.stack([jnp.stack([real_part, -imag_part]), jnp.stack([imag_part, real_part])])
    mixed = jnp.einsum(
        "jkdc,mkcl->mjdl", coupling, spectrum, preferred_element_type=jnp.float32
    ).astype(jnp.bfloat16)
    synthesis = jnp.einsum(
        "mkcl,mrl->mkcr", mixed, legendre_synthesis, preferred_element_type=jnp.float32
    ).astype(jnp.bfloat16)
    returned = lax.all_to_all(
        lax.all_to_all(synthesis, "lat", split_axis=3, concat_axis=0, tiled=True),
        "chan",
        split_axis=2,
        concat_axis=0,
        tiled=True,
    )
    position = jnp.arange(total_modes, dtype=jnp.int32)
    band_index = position // per_dev % lat_parts
    group_index = position // (lat_parts * per_dev)
    mode_ids = band_index * (chan_parts * per_dev) + group_index * per_dev + position % per_dev
    inverse_flat = inverse_table(lon_len, mode_ids, total_modes).reshape(total_modes * 2, lon_len)
    wave_flat = lax.dot_general(
        returned.reshape(total_modes * 2, local_ch * local_rows),
        inverse_flat,
        (((0,), (0,)), ((), ())),
        preferred_element_type=jnp.float32,
    )
    wave_field = wave_flat.reshape(local_ch, local_rows, lon_len)
    atmos_next = (forced_ocean + wave_field).astype(jnp.bfloat16)
    flux_terms = jnp.dot(
        surface_flux_weight,
        atmos.reshape(local_ch, local_rows * lon_len),
        preferred_element_type=jnp.float32,
    )
    flux = lax.psum_scatter(
        flux_terms.reshape(surface_flux_weight.shape[0], local_rows, lon_len).astype(jnp.bfloat16),
        "chan",
        scatter_dimension=2,
        tiled=True,
    ).astype(jnp.float32)
    forcing = jnp.dot(
        flux_ocean_forcing, flux.reshape(flux.shape[0], -1), precision=lax.Precision.HIGHEST
    ).reshape(ocean.shape)
    ocean_in = (ocean.astype(jnp.float32) + forcing).astype(jnp.bfloat16)
    reach = depthwise_filter.shape[2] // 2
    padded = with_halo(ocean_in, (("lat", 1), ("chan", 2)), reach)
    smooth = lax.conv_general_dilated(
        padded[None],
        depthwise_filter,
        (1, 1),
        "VALID",
        feature_group_count=ocean_ch,
        preferred_element_type=jnp.float32,
    )[0]
    center = jnp.mean(smooth, axis=0, keepdims=True)
    spread_var = jnp.mean((smooth - center) ** 2, axis=0, keepdims=True)
    normed = (
        (smooth - center) * lax.rsqrt(spread_var + 1e-06) * norm_gain_vector[:, None, None]
    ).astype(jnp.bfloat16)
    hidden = jax.nn.gelu(
        jnp.dot(expand_matrix, normed.reshape(ocean_ch, -1), preferred_element_type=jnp.float32)
    ).astype(jnp.bfloat16)
    branch = jnp.dot(contract_matrix, hidden, preferred_element_type=jnp.float32).reshape(
        ocean.shape
    )
    tile_rows = ocean_tile_mask.shape[0]
    tile_cols = ocean_tile_mask.shape[1]
    flag = (
        jnp.broadcast_to(
            ocean_tile_mask[:, None, :, None],
            (tile_rows, local_rows // tile_rows, tile_cols, ocean_cols // tile_cols),
        )
        .reshape(local_rows, ocean_cols)
        .astype(jnp.float32)
    )
    ocean_next = (ocean.astype(jnp.float32) + flag[None] * (forcing + branch)).astype(jnp.bfloat16)
    return (atmos_next, ocean_next)


def solution(mesh):
    in_specs = (
        P("chan", "lat", None),
        P("chan"),
        P(("lat", "chan"), None, None),
        P(("lat", "chan"), None, None),
        P(),
        P(None, "chan"),
        P(),
        P(None, "lat", "chan"),
        P("lat", "chan"),
        P(),
        P(),
        P(),
        P(),
    )
    out_specs = (P("chan", "lat", None), P(None, "lat", "chan"))
    return jax.shard_map(body, mesh=mesh, in_specs=in_specs, out_specs=out_specs, check_vma=False)
```

profile of v0, /device:TPU:1, one launch (start us, length us, event | category | flops | bytes accessed | tf_op | source)
XLA Modules:
  0.0 467.8 jit_solution(11826882137912593306)
XLA Ops:
  26.4 15.9 %all-gather = bf16[1,45,1440]{1,0,2:T(2,128)(2,1)S(1)} all-gather(bf16[1,45,180]{1,0,2:T(2,128)(2,1)S(1)} %copy.159), channel_id=2, replica_groups=mesh['lat'=16,'chan'=8] {'chan'}, dimensions={2}, use_global_device_ids=true | all-gather | bytes 145800 | tf_op jit(solution)/shard_map/all_gather | solution.py:67
  43.8 7.1 %fusion.32 = bf16[256,2,48,45]{0,2,3,1:T(8,128)(2,1)S(1)} fusion(bf16[48,45,1440]{2,0,1:T(8,128)(2,1)} %param.13, f32[45,1440]{1,0:T(8,128)S(1)} %bitcast_convert_fusion.1, f32[48]{0:T(128)S(1)} %convert_element_type.111, bf16[256,2,1440,1]{2,1,0,3:T(2,128)(2,1)} %bitcast.139), kind=kOutput, calls=%fused_computation.47 | convolution fusion | flops 3198597120 | bytes 10166592 | tf_op jit(solution)/shard_map/dot_general | solution.py:74
  50.9 8.7 %copy.111 = bf16[256,2,48,45]{2,1,3,0:T(2,128)(2,1)} copy(bf16[256,2,48,45]{0,2,3,1:T(8,128)(2,1)S(1)} %fusion.32) | data formatting | bytes 4423680 | tf_op jit(solution)/shard_map/convert_element_type | solution.py:80
  59.7 10.1 %reshape.297 = bf16[16,2,34560]{2,1,0:T(2,128)(2,1)} reshape(bf16[256,45,2,48]{3,2,1,0:T(2,128)(2,1)} %bitcast.130) | data formatting | bytes 4423680
  76.9 9.5 %copy.128 = bf16[48,45,1440]{2,1,0:T(8,128)(2,1)} copy(bf16[48,45,1440]{2,0,1:T(8,128)(2,1)} %param.13) | data formatting | bytes 12441600 | tf_op args[0]
  86.3 12.2 %reshape.266 = bf16[48,64800]{1,0:T(8,128)(2,1)} reshape(bf16[48,45,1440]{2,1,0:T(8,128)(2,1)} %copy.128) | data formatting | bytes 12441600 | tf_op jit(solution)/shard_map/reshape | solution.py:122
  98.6 12.8 %dot_general.55 = bf16[45,1440,48]{1,0,2:T(8,128)(2,1)} reshape(bf16[64800,48]{0,1:T(8,128)(2,1)} %bitcast.129) | data formatting | bytes 12441600 | tf_op jit(solution)/shard_map/dot_general | solution.py:120
  111.4 11.0 %fusion.28 = bf16[4,45,1440]{2,0,1:T(4,128)(2,1)} fusion(bf16[45,1440,48]{1,0,2:T(8,128)(2,1)} %dot_general.55, bf16[4,48]{1,0:T(4,128)(2,1)S(1)} %copy-done.16), kind=kOutput, calls=%fused_computation.39 | convolution fusion | flops 25142400 | bytes 6739584 | tf_op jit(solution)/shard_map/dot_general | solution.py:120
  123.7 15.2 %multiply_convert_fusion.2 = (bf16[256,1,1440]{0,2,1:T(8,128)(2,1)S(1)}, bf16[256,1,1440]{0,2,1:T(8,128)(2,1)S(1)}) fusion(s32[256]{0:T(256)S(1)} %fusion.67), kind=kLoop, calls=%fused_computation.59 | loop fusion | flops 4792320 | bytes 1475584 | tf_op jit(solution)/shard_map/convert
  140.2 42.3 %all-reduce.3.cloned.1.call-done = bf16[4,45,1440]{2,0,1:T(4,128)(2,1)} async-done(((bf16[4,45,1440]{2,0,1:T(4,128)(2,1)}), bf16[4,45,1440]{2,0,1:T(4,128)(2,1)}) %all-reduce.3.cloned.1.call-update) | async-done | bytes 518416
  183.8 7.3 %reshape.298 = bf16[256,45,2,48]{3,2,1,0:T(2,128)(2,1)} reshape(bf16[16,2,34560]{2,1,0:T(2,128)(2,1)S(1)} %all-to-all-done) | data formatting | bytes 4423680
  197.9 11.6 %copy.113 = bf16[16,2,48,16,45]{4,3,2,1,0:T(8,128)(2,1)} copy(bf16[16,2,48,16,45]{2,0,3,4,1:T(8,128)(2,1)} %bitcast.132) | data formatting | bytes 4423680 | tf_op jit(solution)/shard_map/all_to_all | solution.py:82
  209.5 9.9 %all_to_all.53 = bf16[16,2,48,720]{3,2,1,0:T(8,128)(2,1)} reshape(bf16[16,2,48,16,45]{4,3,2,1,0:T(8,128)(2,1)} %copy.113) | data formatting | bytes 4423680 | tf_op jit(solution)/shard_map/all_to_all | solution.py:82
  219.3 7.6 %all-to-all-start.1 = ((bf16[16,2,48,720]{3,2,1,0:T(8,128)(2,1)}), bf16[16,2,48,720]{3,2,1,0:T(8,128)(2,1)}, u32[]{:S(2)}, u32[]{:S(2)}) async-start(bf16[16,2,48,720]{3,2,1,0:T(8,128)(2,1)} %all_to_all.53), calls=%async_computation.1 | async-start | bytes 4718592 | tf_op jit(solution)/shard_map/all_to_all | solution.py:81
  302.3 8.6 %all-to-all-start.2 = ((bf16[2,2,384,720]{2,1,0,3:T(2,128)(2,1)}), bf16[2,2,384,720]{2,1,0,3:T(2,128)(2,1)S(1)}, u32[]{:S(2)}, u32[]{:S(2)}) async-start(bf16[2,2,384,720]{2,1,0,3:T(2,128)(2,1)} %copy.118), calls=%async_computation.2 | async-start | bytes 4423680 | tf_op jit(solution)/shard_map/all_to_all | solution.py:101
  310.9 16.8 %broadcast_select_fusion = f32[45,8,24,76]{3,1,2,0:T(8,128)S(1)} fusion(pred[8,24]{0,1:T(8,128)(4,1)S(1)} %copy-done.24, bf16[76,51,1,7,6]{0,3,4,1,2:T(8,128)(2,1)S(1)} %copy-done.4, bf16[76,51,1,8,24]{0,3,4,1,2:T(8,128)(2,1)} %copy-done.3, bf16[76,1,7,7]{0,3,2,1:T(8,128)(2,1)S(1)} %copy-done.20), kind=kOutput, calls=%fused_computation.41 | convolution fusion | flops 70588800 | bytes 4448168 | tf_op jit(solution)/shard_map/conv_general_dilated | solution.py:137
  333.7 10.1 %all-to-all-done.2 = bf16[2,2,384,720]{2,1,0,3:T(2,128)(2,1)S(1)} async-done(((bf16[2,2,384,720]{2,1,0,3:T(2,128)(2,1)}), bf16[2,2,384,720]{2,1,0,3:T(2,128)(2,1)S(1)}, u32[]{:S(2)}, u32[]{:S(2)}) %all-to-all-start.2) | async-done | bytes 2211872 | tf_op jit(solution)/shard_map/all_to_all | solution.py:101
  346.6 10.6 %copy.121 = bf16[32,2,384,45]{3,0,1,2:T(8,128)(2,1)} copy(bf16[32,2,384,45]{2,1,3,0:T(2,128)(2,1)} %bitcast.136) | data formatting | bytes 4423680 | tf_op jit(solution)/shard_map/all_to_all | solution.py:101
  357.2 12.6 %reshape.299 = bf16[8,2,69120]{2,1,0:T(2,128)(2,1)} reshape(bf16[384,2,32,45]{3,2,1,0:T(8,128)(2,1)} %bitcast.128) | data formatting | bytes 4423680
  396.0 7.1 %reshape.269 = f32[76,45,180]{2,1,0:T(8,128)} reshape(f32[76,8100]{1,0:T(8,128)} %convolution_bitcast_fusion.1) | data formatting | bytes 4924800 | tf_op jit(solution)/shard_map/reshape | solution.py:153
  410.0 18.9 %reshape.300 = bf16[384,2,32,45]{3,2,1,0:T(8,128)(2,1)} reshape(bf16[8,2,69120]{2,1,0:T(2,128)(2,1)S(1)} %all-to-all-done.3) | data formatting | bytes 4423680
  428.9 9.5 %copy.175 = bf16[32,2,8,48,45]{4,3,1,0,2:T(8,128)(2,1)} copy(bf16[32,2,8,48,45]{4,0,1,3,2:T(8,128)(2,1)} %bitcast.126) | data formatting | bytes 4423680 | tf_op jit(solution)/shard_map/all_to_all | solution.py:100
  438.4 8.1 %reshape.265 = bf16[512,2160]{1,0:T(8,128)(2,1)S(1)} reshape(bf16[8,32,2,48,45]{4,3,2,1,0:T(8,128)(2,1)} %bitcast.127) | data formatting | bytes 4423680 | tf_op jit(solution)/shard_map/reshape | solution.py:113
  451.7 8.9 %add_convert_fusion = bf16[48,45,1440]{2,0,1:T(8,128)(2,1)} fusion(bf16[48,45,1440]{2,0,1:T(8,128)(2,1)} %param.13, f32[45,1440]{1,0:T(8,128)S(1)} %copy-done.12, f32[48]{0:T(128)S(1)} %convert_element_type.111, bf16[48,45,512]{2,1,0:T(8,128)(2,1)S(1)} %dot_general.52, bf16[512,1440]{1,0:T(8,128)(2,1)} %convert_element_type.122), kind=kOutput, calls=%fused_computation.1 | convolution fusion | flops 3200601600 | bytes 16387392 | tf_op jit(solution)/shard_map/dot_general | solution.py:112
  (124 shorter events, 160.0 us)
Async XLA Ops:
  7.2 289.2 %copy-start = (bf16[2,720,256]{2,1,0:T(8,128)(2,1)S(1)}, bf16[2,720,256]{2,1,0:T(8,128)(2,1)}, u32[]{:S(2)}) copy-start(bf16[2,720,256]{2,1,0:T(8,128)(2,1)} %param.16) | copy-start | bytes 2211844
  20.7 22.3 %copy-start.21 = (bf16[48]{0:T(256)(128)(2,1)S(1)}, bf16[48]{0:T(256)(128)(2,1)}, u32[]{:S(2)}) copy-start(bf16[48]{0:T(256)(128)(2,1)} %param.14) | copy-start | bytes 292
  69.8 114.0 %all-to-all-start = ((bf16[16,2,34560]{2,1,0:T(2,128)(2,1)}), bf16[16,2,34560]{2,1,0:T(2,128)(2,1)S(1)}, u32[]{:S(2)}, u32[]{:S(2)}) async-start(bf16[16,2,34560]{2,1,0:T(2,128)(2,1)} %reshape.297), calls=%async_computation | async-start | bytes 4423680 | tf_op jit(solution)/shard_map/all_to_all | solution.py:82
  76.6 106.0 %all-reduce.3.cloned.1.call-start = ((), (), s32[]{:S(2)}) async-start(), calls=%async_computation.4 | async-start | bytes 1105920
  98.6 12.9 %copy-start.16 = (bf16[4,48]{1,0:T(4,128)(2,1)S(1)}, bf16[4,48]{1,0:T(4,128)(2,1)}, u32[]{:S(2)}) copy-start(bf16[4,48]{1,0:T(4,128)(2,1)} %param.18) | copy-start | bytes 1156
  111.4 11.0 %copy-start.23 = (u32[128]{0:T(128)S(1)}, u32[128]{0:T(128)}, u32[]{:S(2)}) copy-start(u32[128]{0:T(128)} %constant.113) | copy-start | bytes 1540
  219.3 7.6 %copy-start.15 = (f32[76,4]{0,1:T(4,128)S(1)}, f32[76,4]{0,1:T(4,128)}, u32[]{:S(2)}) copy-start(f32[76,4]{0,1:T(4,128)} %param.19) | copy-start | bytes 3652
  219.3 73.5 %all-to-all-start.1 = ((bf16[16,2,48,720]{3,2,1,0:T(8,128)(2,1)}), bf16[16,2,48,720]{3,2,1,0:T(8,128)(2,1)}, u32[]{:S(2)}, u32[]{:S(2)}) async-start(bf16[16,2,48,720]{3,2,1,0:T(8,128)(2,1)} %all_to_all.53), calls=%async_computation.1 | async-start | bytes 4718592 | tf_op jit(solution)/shard_map/all_to_all | solution.py:81
  234.9 8.0 %copy-start.9 = (bf16[2,384,384]{2,1,0:T(8,128)(2,1)S(1)}, bf16[2,384,384]{2,1,0:T(8,128)(2,1)}, u32[]{:S(2)}) copy-start(bf16[2,384,384]{2,1,0:T(8,128)(2,1)} %param.17) | copy-start | bytes 1769476
  238.5 6.4 %collective-permute-start = (bf16[76,3,180]{2,1,0:T(4,128)(2,1)S(1)}, bf16[76,3,180]{2,1,0:T(4,128)(2,1)S(1)}, u32[]{:S(2)}, u32[]{:S(2)}) collective-permute-start(bf16[76,3,180]{2,1,0:T(4,128)(2,1)S(1)} %get-tuple-element.12), channel_id=1, source_target_pairs={{0,8},{8,16},{16,24},{24,32},{32,40},{40,48},{48,56},{56,64},{64,7... | collective-permute-start | bytes 246248 | tf_op jit(solution)/shard_map/ppermute | solution.py:14
  241.6 7.2 %collective-permute-start.1 = (bf16[76,3,180]{2,1,0:T(4,128)(2,1)S(1)}, bf16[76,3,180]{2,1,0:T(4,128)(2,1)S(1)}, u32[]{:S(2)}, u32[]{:S(2)}) collective-permute-start(bf16[76,3,180]{2,1,0:T(4,128)(2,1)S(1)} %get-tuple-element.13), channel_id=1, source_target_pairs={{8,0},{16,8},{24,16},{32,24},{40,32},{48,40},{56,48},{64,56},{72,6... | collective-permute-start | bytes 246248 | tf_op jit(solution)/shard_map/ppermute | solution.py:17
  244.9 7.2 %copy-start.5 = (bf16[76,3,180]{2,1,0:T(4,128)(2,1)}, bf16[76,3,180]{2,1,0:T(4,128)(2,1)S(1)}, u32[]{:S(2)}) copy-start(bf16[76,3,180]{2,1,0:T(4,128)(2,1)S(1)} %collective-permute-done) | copy-start | bytes 246244
  252.1 12.0 %copy-start.14 = (s32[5,5]{1,0:T(8,128)S(1)}, s32[5,5]{1,0:T(8,128)}, u32[]{:S(2)}) copy-start(s32[5,5]{1,0:T(8,128)} %param.21) | copy-start | bytes 304
  254.0 20.5 %collective-permute-start.2 = (bf16[76,51,3]{0,1,2:T(8,128)(2,1)S(1)}, bf16[76,51,3]{0,1,2:T(8,128)(2,1)}, u32[]{:S(2)}, u32[]{:S(2)}) collective-permute-start(bf16[76,51,3]{0,1,2:T(8,128)(2,1)S(1)} %copy.131), channel_id=1, source_target_pairs={{0,1},{1,2},{2,3},{3,4},{4,5},{5,6},{6,7},{8,9},{9,10},{10,11},{11... | collective-permute-start | bytes 69776 | tf_op jit(solution)/shard_map/ppermute | solution.py:14
  261.0 15.9 %collective-permute-start.3 = (bf16[76,51,3]{0,1,2:T(8,128)(2,1)}, bf16[76,51,3]{0,1,2:T(8,128)(2,1)}, u32[]{:S(2)}, u32[]{:S(2)}) collective-permute-start(bf16[76,51,3]{0,1,2:T(8,128)(2,1)} %copy.132), channel_id=1, source_target_pairs={{1,0},{2,1},{3,2},{4,3},{5,4},{6,5},{7,6},{9,8},{10,9},{11,10},{12... | collective-permute-start | bytes 69776 | tf_op jit(solution)/shard_map/ppermute | solution.py:17
  269.8 9.5 %copy-start.6 = (bf16[76,3,180]{2,1,0:T(4,128)(2,1)S(1)}, bf16[76,3,180]{2,1,0:T(4,128)(2,1)}, u32[]{:S(2)}) copy-start(bf16[76,3,180]{2,1,0:T(4,128)(2,1)} %copy-done.5) | copy-start | bytes 246244
  269.8 9.5 %copy-start.8 = (bf16[76,3,180]{2,1,0:T(4,128)(2,1)S(1)}, bf16[76,3,180]{2,1,0:T(4,128)(2,1)}, u32[]{:S(2)}) copy-start(bf16[76,3,180]{2,1,0:T(4,128)(2,1)} %copy-done.7) | copy-start | bytes 246244
  302.3 8.6 %copy-start.4 = (bf16[76,51,1,7,6]{0,3,4,1,2:T(8,128)(2,1)S(1)}, bf16[76,51,1,7,6]{0,3,4,1,2:T(8,128)(2,1)}, u32[]{:S(2)}) copy-start(bf16[76,51,1,7,6]{0,3,4,1,2:T(8,128)(2,1)} %slice.34) | copy-start | bytes 976756
  302.3 8.6 %copy-start.20 = (bf16[76,1,7,7]{0,3,2,1:T(8,128)(2,1)S(1)}, bf16[76,1,7,7]{0,3,2,1:T(8,128)(2,1)}, u32[]{:S(2)}) copy-start(bf16[76,1,7,7]{0,3,2,1:T(8,128)(2,1)} %param.22) | copy-start | bytes 22348
  302.3 8.6 %copy-start.24 = (pred[8,24]{0,1:T(8,128)(4,1)S(1)}, pred[8,24]{0,1:T(8,128)(4,1)}, u32[]{:S(2)}) copy-start(pred[8,24]{0,1:T(8,128)(4,1)} %constant.110) | copy-start | bytes 580
  302.3 41.4 %all-to-all-start.2 = ((bf16[2,2,384,720]{2,1,0,3:T(2,128)(2,1)}), bf16[2,2,384,720]{2,1,0,3:T(2,128)(2,1)S(1)}, u32[]{:S(2)}, u32[]{:S(2)}) async-start(bf16[2,2,384,720]{2,1,0,3:T(2,128)(2,1)} %copy.118), calls=%async_computation.2 | async-start | bytes 4423680 | tf_op jit(solution)/shard_map/all_to_all | solution.py:101
  369.8 40.2 %all-to-all-start.3 = ((bf16[8,2,69120]{2,1,0:T(2,128)(2,1)}), bf16[8,2,69120]{2,1,0:T(2,128)(2,1)S(1)}, u32[]{:S(2)}, u32[]{:S(2)}) async-start(bf16[8,2,69120]{2,1,0:T(2,128)(2,1)} %reshape.299), calls=%async_computation.3 | async-start | bytes 4423680 | tf_op jit(solution)/shard_map/all_to_all | solution.py:100
  396.0 7.1 %copy-start.13 = (f32[45,180]{1,0:T(8,128)S(1)}, f32[45,180]{1,0:T(8,128)}, u32[]{:S(2)}) copy-start(f32[45,180]{1,0:T(8,128)} %convert_element_type.126) | copy-start | bytes 97204
  451.7 8.9 %copy-start.1 = (bf16[2,720,256]{2,1,0:T(8,128)(2,1)S(1)}, bf16[2,720,256]{2,1,0:T(8,128)(2,1)}, u32[]{:S(2)}) copy-start(bf16[2,720,256]{2,1,0:T(8,128)(2,1)} %param.16) | copy-start | bytes 2211844
  (10 other events, 29.4 us)
Sparse Core Ops, SparseCore 0:
  122.5 59.9 all-reduce.2
where the time goes:
time: 477 us; the launch traced here: 468 us
  local copies, waits for them, and re-layouts  238 us (50%)
  waiting for transfers between devices  58.2 us (12%)
  matrix products  56 us (12%)
  other arithmetic  45.1 us (9%)
  starting transfers between devices  38.8 us (8%)
  blocking collectives  15.9 us (3%)
  between operations  15.6 us (3%)
    unnamed x60, local copies, waits for them, and re-layouts  69.4 us
    unnamed x2, waiting for transfers between devices  42.4 us
    all_to_all x3, local copies, waits for them, and re-layouts, body(): lax.all_to_all(fourier, 'lat', split_axis=0, concat_axis=3, tiled=True)  28.2 us
    another operation x2, other arithmetic  21.7 us
    conv_general_dilated x1, matrix products, body(): lax.conv_general_dilated(padded[None], depthwise_filter, (1, 1), 'VALID',...  16.8 us
    all_gather x1, blocking collectives, body(): sea_temp_line = lax.all_gather(ocean[0], 'chan', axis=1, tiled=True)  15.9 us
    all_to_all x2, local copies, waits for them, and re-layouts, body(): lax.all_to_all(synthesis, 'lat', split_axis=3, concat_axis=0, tiled=True)  13.5 us
    dot_general x1, local copies, waits for them, and re-layouts, body(): jnp.dot(surface_flux_weight, atmos.reshape(local_ch, local_rows * lon_len...  12.8 us
  transfers between devices with their start and end apart: 9, of which 4 were waited for; matrix products, arithmetic and copies ran while one was open for 36% of the time, Pallas kernels for 0%

commit v1 on v0

v1 whole, which is shorter than its diff:
```python
import functools
import math

import jax
import jax.numpy as jnp
import ml_dtypes
import numpy as np
from jax import lax
from jax.experimental import pallas as pl
from jax.experimental.pallas import tpu as pltpu
from jax.sharding import PartitionSpec as P

BF = jnp.bfloat16
F32 = jnp.float32
VMEM = pl.BlockSpec(memory_space=pltpu.VMEM)
NT = (((1,), (1,)), ((), ()))

HALF = 24


def peer_modes(lat_parts, chan_parts, per_dev):
    j, i, mm = np.meshgrid(np.arange(chan_parts), np.arange(lat_parts), np.arange(per_dev), indexing="ij")
    return ((i * chan_parts + j) * per_dev + mm).reshape(lat_parts * chan_parts, per_dev)


def dft_tables(lon_len, modes):
    total = modes.size
    product = np.arange(lon_len)[:, None, None] * modes.T[None]
    angle = np.float32(2.0 * math.pi / lon_len) * (product % lon_len).astype(np.float32)
    cos, sin = np.cos(angle), np.sin(angle)
    factor = np.float32(math.sqrt(2.0 / lon_len))
    forward = np.stack([factor * cos, -factor * sin], axis=2).reshape(lon_len, total * 2)
    back = np.float32(1.0 / math.sqrt(total))
    inverse = np.stack([back * cos, -back * sin], axis=2).reshape(lon_len, total * 2).T
    return forward.astype(ml_dtypes.bfloat16), np.ascontiguousarray(inverse).astype(ml_dtypes.bfloat16)


def row_swap(outer, inner):
    n = outer * inner
    swap = np.zeros((n, n), np.float32)
    o, k = np.meshgrid(np.arange(outer), np.arange(inner), indexing="ij")
    swap[(o * inner + k).ravel(), (k * outer + o).ravel()] = 1.0
    return swap.astype(ml_dtypes.bfloat16)


def dot(a, b, dims=(((1,), (0,)), ((), ()))):
    return lax.dot_general(a, b, dims, preferred_element_type=F32)


def forward_kernel(rows, x_ref, table_ref, swap_ref, out_ref, held):
    step = pl.program_id(0)
    block, ch, lon = x_ref.shape
    peers = held.shape[1]
    y = dot(x_ref[...].reshape(block * ch, lon), table_ref[...])
    row = lax.broadcasted_iota(jnp.int32, (block * ch, 1), 0)
    y = jnp.where(row < (rows - block * step) * ch, y, 0.0).astype(BF)
    for a in range(block // 2):
        pieces = [
            y[(2 * a + rh) * ch : (2 * a + rh + 1) * ch, q * peers : (q + 1) * peers]
            for rh in range(2)
            for q in range(4)
        ]
        held[step * (block // 2) + a] = jnp.concatenate(pieces, axis=0).T

    @pl.when(step == pl.num_programs(0) - 1)
    def _():
        swap = swap_ref[...]
        for at in range(0, peers, 16):
            part = held[:, at : at + 16, :].reshape(HALF * 16, held.shape[2])
            out_ref[at * HALF : (at + 16) * HALF, :] = dot(swap, part).astype(BF)


def forward(x, table, swap):
    rows, ch, lon = x.shape
    peers = table.shape[1] // 4
    block = 6
    return pl.pallas_call(
        functools.partial(forward_kernel, rows),
        out_shape=jax.ShapeDtypeStruct((peers * HALF, 8 * ch), BF),
        grid=(2 * HALF // block,),
        in_specs=[
            pl.BlockSpec((block, ch, lon), lambda g: (g, 0, 0)),
            pl.BlockSpec(table.shape, lambda g: (0, 0)),
            pl.BlockSpec(swap.shape, lambda g: (0, 0)),
        ],
        out_specs=pl.BlockSpec((peers * HALF, 8 * ch), lambda g: (0, 0)),
        scratch_shapes=[pltpu.VMEM((HALF, peers, 8 * ch), BF)],
        compiler_params=pltpu.CompilerParams(vmem_limit_bytes=40 << 20),
        cost_estimate=pl.CostEstimate(
            flops=2 * rows * ch * lon * peers * 4, bytes_accessed=14 << 20, transcendentals=0
        ),
        name="dft_forward",
    )(x, table, swap)


def spectral_kernel(
    wire_ref, analysis_ref, synthesis_ref, mix_ref, gain_ref, surface_ref, out_ref, spec, mixed
):
    size = analysis_ref.shape[2]
    wide = wire_ref.shape[1]
    pair = wide // 4
    groups = wire_ref.shape[0] // size
    surface = [
        sum(dot(surface_ref[m, rh], analysis_ref[m, rh]) for rh in range(2)) for m in range(2)
    ]
    for j in range(groups):
        turned = wire_ref[j * size : (j + 1) * size, :].T
        for m in range(2):
            total = sum(
                dot(turned[(2 * rh + m) * pair : (2 * rh + m + 1) * pair, :], analysis_ref[m, rh])
                for rh in range(2)
            )
            half = pair // 2
            gain = gain_ref[j * half : (j + 1) * half, :]
            extra = jnp.concatenate([gain * surface[m][k : k + 1, :] for k in range(2)], axis=0)
            spec[m, j * pair : (j + 1) * pair, :] = (total + extra).astype(BF)
    for m in range(2):
        mixed[m] = dot(mix_ref[...], spec[m]).astype(BF)
    for j in range(groups):
        pieces = [
            dot(synthesis_ref[m, rh], mixed[m, j * pair : (j + 1) * pair, :], NT).astype(BF)
            for rh in range(2)
            for m in range(2)
        ]
        out_ref[j * size : (j + 1) * size, :] = jnp.concatenate(pieces, axis=1)


def spectral(wire, analysis, synthesis, mix, gain, surface):
    degrees = analysis.shape[3]
    return pl.pallas_call(
        spectral_kernel,
        out_shape=jax.ShapeDtypeStruct(wire.shape, BF),
        in_specs=[VMEM] * 6,
        out_specs=VMEM,
        scratch_shapes=[pltpu.VMEM((2, mix.shape[0], degrees), BF)] * 2,
        compiler_params=pltpu.CompilerParams(vmem_limit_bytes=40 << 20),
        cost_estimate=pl.CostEstimate(flops=2 << 30, bytes_accessed=9 << 20, transcendentals=0),
        name="spectral",
    )(wire, analysis, synthesis, mix, gain, surface)


def inverse_kernel(wire_ref, table_ref, swap_ref, x_ref, gain_ref, line_ref, out_ref, held):
    step = pl.program_id(0)
    block, ch, lon = x_ref.shape
    peers = held.shape[1]

    @pl.when(step == 0)
    def _():
        swap = swap_ref[...]
        for at in range(0, peers, 16):
            part = wire_ref[at * HALF : (at + 16) * HALF, :]
            held[:, at : at + 16, :] = dot(swap, part).astype(BF).reshape(HALF, 16, held.shape[2])

    rows = []
    for a in range(block // 2):
        turned = held[step * (block // 2) + a].T
        for rh in range(2):
            rows.append(
                jnp.concatenate(
                    [turned[(4 * rh + q) * ch : (4 * rh + q + 1) * ch, :] for q in range(4)], axis=1
                )
            )
    wave = dot(jnp.concatenate(rows, axis=0), table_ref[...])
    gain = gain_ref[...]
    for a in range(block):
        forced = x_ref[a].astype(F32) + gain * line_ref[a].astype(F32)
        out_ref[a] = (forced + wave[a * ch : (a + 1) * ch, :]).astype(BF)


def inverse(wire, table, swap, x, gain, line):
    rows, ch, lon = x.shape
    peers = table.shape[0] // 4
    block = 6
    return pl.pallas_call(
        inverse_kernel,
        out_shape=jax.ShapeDtypeStruct(x.shape, BF),
        grid=(2 * HALF // block,),
        in_specs=[
            pl.BlockSpec(wire.shape, lambda g: (0, 0)),
            pl.BlockSpec(table.shape, lambda g: (0, 0)),
            pl.BlockSpec(swap.shape, lambda g: (0, 0)),
            pl.BlockSpec((block, ch, lon), lambda g: (g, 0, 0)),
            pl.BlockSpec(gain.shape, lambda g: (0, 0)),
            pl.BlockSpec((block, 1, lon), lambda g: (g, 0, 0)),
        ],
        out_specs=pl.BlockSpec((block, ch, lon), lambda g: (g, 0, 0)),
        scratch_shapes=[pltpu.VMEM((HALF, peers, 8 * ch), BF)],
        compiler_params=pltpu.CompilerParams(vmem_limit_bytes=40 << 20),
        cost_estimate=pl.CostEstimate(
            flops=2 * rows * ch * lon * peers * 4, bytes_accessed=20 << 20, transcendentals=0
        ),
        name="dft_inverse",
    )(wire, table, swap, x, gain, line)


def flux_kernel(rows, reach, x_ref, weight_ref, out_ref):
    step = pl.program_id(0)
    block, ch, lon = x_ref.shape
    peers, _, wide = out_ref.shape
    tile = lon // peers
    row = lax.broadcasted_iota(jnp.int32, (block * ch, 1), 0)
    x = x_ref[...].reshape(block * ch, lon)
    x = jnp.where(row < (rows - block * step) * ch, x, jnp.zeros_like(x))
    y = dot(weight_ref[...], x)
    zeros = jnp.zeros((y.shape[0], reach), F32)
    y = jnp.concatenate([zeros, y, zeros], axis=1)
    half = y.shape[0] // 2
    for j in range(peers):
        part = y[:, tile * j : tile * j + tile + 2 * reach]
        out_ref[j] = jnp.concatenate([part[:half], part[half:]], axis=1).astype(BF)


def flux_parts(x, weight, reach, peers):
    rows, ch, lon = x.shape
    block = 8
    steps = pl.cdiv(rows, block)
    eye = jnp.eye(block, dtype=BF)
    spread = weight.reshape(2, 1, 2, 1, ch) * eye[None, :, None, :, None]
    spread = spread.reshape(4 * block, block * ch)
    wide = 2 * (lon // peers + 2 * reach)
    return pl.pallas_call(
        functools.partial(flux_kernel, rows, reach),
        out_shape=jax.ShapeDtypeStruct((peers, steps * 2 * block, wide), BF),
        grid=(steps,),
        in_specs=[
            pl.BlockSpec((block, ch, lon), lambda g: (g, 0, 0)),
            pl.BlockSpec(spread.shape, lambda g: (0, 0)),
        ],
        out_specs=pl.BlockSpec((peers, 2 * block, wide), lambda g: (0, g, 0)),
        compiler_params=pltpu.CompilerParams(vmem_limit_bytes=24 << 20),
        cost_estimate=pl.CostEstimate(flops=1 << 30, bytes_accessed=7 << 20, transcendentals=0),
        name="flux_parts",
    )(x, spread)


def ocean_kernel(
    reach, padded_ref, flux_ref, force_ref, taps_ref, gain_ref, expand_ref, contract_ref, flag_ref,
    center_ref, out_ref, wet, taps, smooth
):
    step = pl.program_id(0)
    block, ch, cols = center_ref.shape
    total_rows, high, wide = wet.shape
    side = 2 * reach + 1
    force = [force_ref[:, f : f + 1] for f in range(4)]

    @pl.when(step == 0)
    def _():
        def fill(r, carry):
            flux = flux_ref[r]
            forcing = sum(force[f] * flux[f : f + 1, : padded_ref.shape[2]] for f in range(4))
            value = (padded_ref[r].astype(F32) + forcing).astype(BF).astype(F32)
            wet[r, :ch, : padded_ref.shape[2]] = value
            return carry

        lax.fori_loop(0, total_rows, fill, 0)
        for k in range(side * side):
            taps[k] = jnp.broadcast_to(taps_ref[:, k : k + 1], taps.shape[1:])

    start = step * block

    def channels(t, carry):
        at = pl.multiple_of(t * 8, 8)
        rows = [wet[start + d, pl.ds(at, 8), :] for d in range(block + side - 1)]
        total = [None] * block
        for dx in range(side):
            part = [None] * block
            for dy in range(side):
                tap = taps[dy * side + dx, pl.ds(at, 8), :]
                tap = jnp.concatenate([tap] * (wide // 128), axis=1)
                for b in range(block):
                    term = tap * rows[b + dy]
                    part[b] = term if part[b] is None else part[b] + term
            for b in range(block):
                moved = part[b] if dx == 0 else pltpu.roll(part[b], wide - dx, 1)
                total[b] = moved if total[b] is None else total[b] + moved
        for b in range(block):
            smooth[b, pl.ds(at, 8), :] = total[b]
        return carry

    lax.fori_loop(0, high // 8, channels, 0)
    normed = []
    for b in range(block):
        value = smooth[b, :ch, :]
        value = value - jnp.mean(value, axis=0, keepdims=True)
        spread = jnp.mean(value * value, axis=0, keepdims=True)
        normed.append((value * lax.rsqrt(spread + 1e-06) * gain_ref[...]).astype(BF))
    for b in range(block):
        hidden = jax.nn.gelu(dot(expand_ref[...], normed[b])).astype(BF)
        branch = dot(contract_ref[...], hidden)[:, :cols]
        flux = flux_ref[start + reach + b][:, reach : reach + cols]
        forcing = sum(force[f] * flux[f : f + 1, :] for f in range(4))
        flag = flag_ref[b]
        out_ref[b] = (center_ref[b].astype(F32) + flag * (forcing + branch)).astype(BF)


def ocean_block(padded, flux, force, taps, gain, expand, contract, flag, center, reach):
    rows, ch, cols = center.shape
    block = 5
    high = pl.cdiv(ch, 8) * 8
    wide = pl.cdiv(cols + 2 * reach, 128) * 128
    whole = lambda a: pl.BlockSpec(a.shape, lambda g: (0,) * a.ndim)
    return pl.pallas_call(
        functools.partial(ocean_kernel, reach),
        out_shape=jax.ShapeDtypeStruct(center.shape, BF),
        grid=(rows // block,),
        in_specs=[whole(a) for a in (padded, flux, force, taps, gain, expand, contract)]
        + [
            pl.BlockSpec((block, 1, cols), lambda g: (g, 0, 0)),
            pl.BlockSpec((block, ch, cols), lambda g: (g, 0, 0)),
        ],
        out_specs=pl.BlockSpec((block, ch, cols), lambda g: (g, 0, 0)),
        scratch_shapes=[
            pltpu.VMEM((rows + 2 * reach, high, wide), F32),
            pltpu.VMEM((taps.shape[1], high, 128), F32),
            pltpu.VMEM((block, high, wide), F32),
        ],
        compiler_params=pltpu.CompilerParams(vmem_limit_bytes=32 << 20),
        cost_estimate=pl.CostEstimate(
            flops=20 << 30, bytes_accessed=8 << 20, transcendentals=3 << 20
        ),
        name="ocean_block",
    )(padded, flux, force, taps, gain, expand, contract, flag, center)


def halo(block, axis, dim, width):
    count = lax.axis_size(axis)
    forward = [(i, i + 1) for i in range(count - 1)]
    backward = [(target, source) for source, target in forward]
    size = block.shape[dim]
    low = lax.ppermute(lax.slice_in_dim(block, size - width, size, axis=dim), axis, forward)
    high = lax.ppermute(lax.slice_in_dim(block, 0, width, axis=dim), axis, backward)
    return jnp.concatenate([low, block, high], axis=dim)


def body(
    atmos,
    sea_temp_gain,
    legendre_analysis,
    legendre_synthesis,
    spectral_mixing_weight,
    surface_flux_weight,
    flux_ocean_forcing,
    ocean,
    ocean_tile_mask,
    depthwise_filter,
    norm_gain_vector,
    expand_matrix,
    contract_matrix,
):
    lat_parts = lax.axis_size("lat")
    chan_parts = lax.axis_size("chan")
    chan_at = lax.axis_index("chan")
    ch, rows, lon = atmos.shape
    per_dev, degrees, _ = legendre_analysis.shape
    all_ch = ch * chan_parts
    ocean_ch, _, cols = ocean.shape
    reach = depthwise_filter.shape[2] // 2
    peers = lat_parts * chan_parts
    padded_rows = 2 * HALF

    table_fwd, table_inv = dft_tables(lon, peer_modes(lat_parts, chan_parts, per_dev))
    table_fwd, table_inv = jnp.asarray(table_fwd), jnp.asarray(table_inv)
    swap_out = jnp.asarray(row_swap(16, HALF))
    swap_in = jnp.asarray(row_swap(HALF, 16))

    x = jnp.transpose(atmos, (1, 0, 2))
    sea = jnp.transpose(ocean, (1, 0, 2))

    def exchange(wire):
        return lax.all_to_all(
            wire.reshape(peers, HALF, 8 * ch), ("chan", "lat"), 0, 0, tiled=True
        ).reshape(wire.shape)

    own = jnp.pad(sea[:, 0, :], ((0, 3), (0, 0)))
    own = own.at[rows, :ch].set(sea_temp_gain)
    lines = lax.all_to_all(
        jnp.broadcast_to(own[None], (chan_parts,) + own.shape), "chan", 0, 0, tiled=True
    )
    all_gain = lines[:, rows, :ch].reshape(all_ch)
    line = jnp.transpose(lines[:, :rows], (1, 0, 2)).reshape(rows, lon)

    wire = forward(x, table_fwd, swap_out)
    gathered = exchange(wire)

    surface = dot(line, table_fwd).reshape(rows, 4, chan_parts, lat_parts)
    surface = lax.dynamic_index_in_dim(surface, chan_at, axis=2, keepdims=False).astype(BF)
    surface = jnp.pad(jnp.transpose(surface, (2, 1, 0)), ((0, 0), (0, 0), (0, padded_rows - rows)))
    surface = lax.all_to_all(surface, "lat", 0, 0, tiled=True)
    surface = surface.reshape(lat_parts, 2, 2, HALF, 2).transpose(1, 4, 2, 0, 3)
    surface = surface.reshape(2, 2, 2, lat_parts * HALF)

    def banded(table):
        table = table.reshape(per_dev, lat_parts, rows, degrees)
        table = jnp.pad(table, ((0, 0), (0, 0), (0, padded_rows - rows), (0, 0)))
        table = table.reshape(per_dev, lat_parts, HALF, 2, degrees).transpose(0, 3, 1, 2, 4)
        return table.reshape(per_dev, 2, lat_parts * HALF, degrees)

    analysis = banded(jnp.transpose(legendre_analysis, (0, 2, 1)))
    synthesis = banded(legendre_synthesis)
    real_part, imag_part = spectral_mixing_weight[0], spectral_mixing_weight[1]
    mix = jnp.stack([jnp.stack([real_part, -imag_part]), jnp.stack([imag_part, real_part])])
    mix = mix.reshape(2, 2, chan_parts, ch, chan_parts, ch).transpose(2, 0, 3, 4, 1, 5)
    mix = mix.reshape(2 * all_ch, 2 * all_ch)
    returned = exchange(
        spectral(gathered, analysis, synthesis, mix, all_gain.astype(F32)[:, None], surface)
    )

    parts = lax.all_to_all(
        flux_parts(x, surface_flux_weight, reach, chan_parts), "chan", 0, 0, tiled=True
    )
    flux = jnp.sum(parts.astype(F32), axis=0)[: 2 * rows]
    flux = halo(flux, "lat", 0, 2 * reach)
    flux = flux.reshape(rows + 2 * reach, 2, 2, cols + 2 * reach).transpose(0, 2, 1, 3)
    flux = flux.reshape(rows + 2 * reach, 4, cols + 2 * reach)
    padded = halo(halo(sea, "lat", 0, reach), "chan", 2, reach)
    tile_rows, tile_cols = ocean_tile_mask.shape
    flag = jnp.repeat(jnp.repeat(ocean_tile_mask, rows // tile_rows, 0), cols // tile_cols, 1)
    taps = depthwise_filter.reshape(ocean_ch, -1).astype(F32)
    taps = jnp.pad(taps, ((0, -ocean_ch % 8), (0, 0)))
    ocean_next = ocean_block(
        padded,
        flux,
        flux_ocean_forcing,
        taps,
        norm_gain_vector[:, None],
        expand_matrix,
        contract_matrix,
        flag.astype(F32)[:, None, :],
        sea,
        reach,
    )

    atmos_next = inverse(
        returned, table_inv, swap_in, x, sea_temp_gain.astype(F32)[:, None], line[:, None, :]
    )
    return (jnp.transpose(atmos_next, (1, 0, 2)), jnp.transpose(ocean_next, (1, 0, 2)))


def solution(mesh):
    in_specs = (
        P("chan", "lat", None),
        P("chan"),
        P(("lat", "chan"), None, None),
        P(("lat", "chan"), None, None),
        P(),
        P(None, "chan"),
        P(),
        P(None, "lat", "chan"),
        P("lat", "chan"),
        P(),
        P(),
        P(),
        P(),
    )
    out_specs = (P("chan", "lat", None), P(None, "lat", "chan"))
    return jax.shard_map(body, mesh=mesh, in_specs=in_specs, out_specs=out_specs, check_vma=False)
```

time: 477 us -> 197 us (0.41); the launches traced: 468 us -> 196 us
  local copies, waits for them, and re-layouts: 238 us -> 49.3 us
  Pallas kernels: 0 us -> 63.3 us
  matrix products: 56 us -> 0.54 us
  waiting for transfers between devices: 58.2 us -> 7.93 us
  other arithmetic: 45.1 us -> 17.5 us
  starting transfers between devices: 38.8 us -> 56.3 us
  blocking collectives: 15.9 us -> 0 us
  between operations: 15.6 us -> 1.24 us
    pallas_call x0 -> x5, Pallas kernels: none -> 63.3 us  [the longest x1 38.5 us: ocean_block(): pl.pallas_call(functools.partial(ocean_kernel, reach), out_shape=jax.Shap...]
    all_to_all x7 -> x1, local copies, waits for them, and re-layouts: 53.1 us -> 0.11 us  [body(): surface = lax.all_to_all(surface, 'lat', 0, 0, tiled=True)]
    unnamed x60 -> x67, local copies, waits for them, and re-layouts: 69.4 us -> 18.4 us
    unnamed x2 -> x0, waiting for transfers between devices: 42.4 us -> none
    dot_general x7 -> x1, matrix products: 39.3 us -> 0.54 us  [dot(): return lax.dot_general(a, b, dims, preferred_element_type=F32)]
    reshape x5, local copies, waits for them, and re-layouts: 34.3 us -> 7.3 us  [the longest x1 4.73 us: body(): mix = mix.reshape(2 * all_ch, 2 * all_ch)]
    another operation x5 -> x1, other arithmetic: 25.4 us -> 1.14 us  [body(): jnp.stack([real_part, -imag_part])]
    dot_general x4 -> x0, local copies, waits for them, and re-layouts: 22.6 us -> none  [the longest x1 12.8 us: body(): jnp.dot(surface_flux_weight, atmos.reshape(local_ch, local_rows * lon_len...]
  transfers between devices with their start and end apart: 9 -> 11, of which waited for: 4 -> 2; matrix products, arithmetic and copies ran while one was open for 36% -> 23% of each run, Pallas kernels for 0% -> 28%
where the time goes in v1:
time: 197 us; the launch traced here: 196 us
  Pallas kernels  63.3 us (32%)
  starting transfers between devices  56.3 us (29%)
  local copies, waits for them, and re-layouts  49.3 us (25%)
  other arithmetic  17.5 us (9%)
  waiting for transfers between devices  7.93 us (4%)
    pallas_call x1, Pallas kernels, ocean_block(): pl.pallas_call(functools.partial(ocean_kernel, reach), out_shape=jax.Shap...  38.5 us
    all_to_all x2, starting transfers between devices, exchange(): lax.all_to_all(wire.reshape(peers, HALF, 8 * ch), ('chan', 'lat'), 0, 0,...  20 us
    unnamed x67, local copies, waits for them, and re-layouts  18.4 us
    ppermute x3, starting transfers between devices, halo(): lax.ppermute(lax.slice_in_dim(block, size - width, size, axis=dim), axis,...  12 us
    another operation x4, local copies, waits for them, and re-layouts, body(): jnp.stack([jnp.stack([real_part, -imag_part]), jnp.stack([imag_part, real...  11.2 us
    pallas_call x1, Pallas kernels, inverse(): pl.pallas_call(inverse_kernel, out_shape=jax.ShapeDtypeStruct(x.shape, BF...  8.44 us
    pallas_call x1, Pallas kernels, forward(): pl.pallas_call(functools.partial(forward_kernel, rows), out_shape=jax.Sha...  7.18 us
    transpose x1, other arithmetic, body(): mix.reshape(2, 2, chan_parts, ch, chan_parts, ch)  6.87 us
  transfers between devices with their start and end apart: 11, of which 2 were waited for; matrix products, arithmetic and copies ran while one was open for 23% of the time, Pallas kernels for 28%

profile of v1, /device:TPU:1, one launch (start us, length us, event | category | flops | bytes accessed | tf_op | source)
XLA Modules:
  0.0 196.2 jit_solution(6552072200551202870)
XLA Ops:
  3.2 6.8 %all-to-all-start.1 = ((bf16[8,48,180]{2,1,0:T(8,128)(2,1)}), bf16[8,48,180]{2,1,0:T(8,128)(2,1)S(1)}, u32[]{:S(2)}, u32[]{:S(2)}) async-start(bf16[8,48,180]{2,1,0:T(8,128)(2,1)} %broadcast_in_dim.26), calls=%async_computation.1 | async-start | bytes 393216 | tf_op jit(solution)/shard_map/all_to_all | solution.py:376
  10.9 5.0 %all-to-all-done.1 = bf16[8,48,180]{2,1,0:T(8,128)(2,1)S(1)} async-done(((bf16[8,48,180]{2,1,0:T(8,128)(2,1)}), bf16[8,48,180]{2,1,0:T(8,128)(2,1)S(1)}, u32[]{:S(2)}, u32[]{:S(2)}) %all-to-all-start.1) | async-done | bytes 138272 | tf_op jit(solution)/shard_map/all_to_all | solution.py:376
  17.5 6.8 %all-to-all-start.2 = ((bf16[16,4,48]{2,1,0:T(4,128)(2,1)}), bf16[16,4,48]{2,1,0:T(4,128)(2,1)S(1)}, u32[]{:S(2)}, u32[]{:S(2)}) async-start(bf16[16,4,48]{2,1,0:T(4,128)(2,1)} %pad.27.clone), calls=%async_computation.2 | async-start | bytes 32768 | tf_op jit(solution)/shard_map/all_to_all | solution.py:388
  24.3 2.9 %copy-done = bf16[48,45,1440]{2,0,1:T(8,128)(2,1)S(1)} copy-done((bf16[48,45,1440]{2,0,1:T(8,128)(2,1)S(1)}, bf16[48,45,1440]{2,0,1:T(8,128)(2,1)}, u32[]{:S(2)}) %copy-start) | copy-done | bytes 6220824
  27.2 3.8 %flux_parts.1 = bf16[8,96,372]{2,1,0:T(8,128)(2,1)} custom-call(bf16[45,48,1440]{2,1,0:T(8,128)(2,1)S(1)} %bitcast.55, bf16[32,384]{1,0:T(8,128)(2,1)S(1)} %mul.23.weight_ref), custom_call_target="tpu_custom_call" | custom-call | flops 1073741824 | bytes 7340032 | tf_op jit(solution)/shard_map/flux_parts/pallas_call | solution.py:221
  31.0 5.5 %all-to-all-start.4 = ((bf16[8,96,372]{2,1,0:T(8,128)(2,1)}), bf16[8,96,372]{2,1,0:T(8,128)(2,1)S(1)}, u32[]{:S(2)}, u32[]{:S(2)}) async-start(bf16[8,96,372]{2,1,0:T(8,128)(2,1)} %flux_parts.1), calls=%async_computation.4 | async-start | bytes 1179648 | tf_op jit(solution)/shard_map/all_to_all | solution.py:408
  36.5 2.9 %copy-done.1 = bf16[48,45,1440]{2,0,1:T(8,128)(2,1)S(1)} copy-done((bf16[48,45,1440]{2,0,1:T(8,128)(2,1)S(1)}, bf16[48,45,1440]{2,0,1:T(8,128)(2,1)}, u32[]{:S(2)}) %copy-start.1) | copy-done | bytes 6220824
  39.4 7.2 %dft_forward.1 = bf16[3072,384]{1,0:T(8,128)(2,1)S(1)} custom-call(bf16[45,48,1440]{2,1,0:T(8,128)(2,1)S(1)} %bitcast.56, bf16[1440,512]{1,0:T(8,128)(2,1)S(1)} %copy-done.11, bf16[384,384]{1,0:T(8,128)(2,1)S(1)} %copy-done.12), custom_call_target="tpu_custom_call" | custom-call | flops 3185049600 | bytes 14680064 | tf_op jit(solution)/shard_map/dft_forward/pallas_call | solution.py:77
  48.9 9.2 %all-to-all-start = ((bf16[128,24,384]{2,1,0:T(8,128)(2,1)}), bf16[128,24,384]{2,1,0:T(8,128)(2,1)}, u32[]{:S(2)}, u32[]{:S(2)}) async-start(bf16[128,24,384]{2,1,0:T(8,128)(2,1)} %bitcast.64), calls=%async_computation | async-start | bytes 4718592 | tf_op jit(solution)/shard_map/all_to_all | solution.py:370
  60.1 4.6 %collective-permute-start = (bf16[3,76,180]{2,1,0:T(8,128)(2,1)}, bf16[3,76,180]{2,1,0:T(8,128)(2,1)}, u32[]{:S(2)}, u32[]{:S(2)}) collective-permute-start(bf16[3,76,180]{2,1,0:T(8,128)(2,1)} %get-tuple-element.16), channel_id=1, source_target_pairs={{0,8},{8,16},{16,24},{24,32},{32,40},{40,48},{48,56},{56,64},{64,7... | collective-permute-start | bytes 246248 | tf_op jit(solution)/shard_map/ppermute | solution.py:330
  68.5 3.6 %copy.54 = bf16[1,2,8,48,8,48]{5,1,4,3,0,2:T(2,128)(2,1)} copy(bf16[1,2,8,48,8,48]{5,4,3,2,1,0:T(8,128)(2,1)S(1)} %stack.19) | data formatting | bytes 1179648 | tf_op jit(solution)/shard_map/stack | solution.py:401
  72.1 2.7 %stack.17 = bf16[1,2,8,48,8,48]{5,4,3,2,1,0:T(8,128)(2,1)S(1)} reshape(bf16[2,384,384]{2,1,0:T(8,128)(2,1)} %get-tuple-element.21) | data formatting | bytes 1179648 | tf_op jit(solution)/shard_map/stack | solution.py:401
  77.3 6.9 %maximum_bitcast_fusion = bf16[8,2,48,8,2,48]{5,4,3,2,1,0:T(2,128)(2,1)} fusion(bf16[1,2,8,48,8,48]{5,1,4,3,0,2:T(2,128)(2,1)S(1)} %copy-done.13, bf16[1,2,8,48,8,48]{5,1,4,3,0,2:T(2,128)(2,1)S(1)} %copy.53), kind=kLoop, calls=%fused_computation | loop fusion | flops 589824 | bytes 2359296 | tf_op jit(solution)/shard_map/transpose | solution.py:402
  84.3 2.9 %collective-permute-done.1 = bf16[3,76,180]{2,1,0:T(8,128)(2,1)S(1)} collective-permute-done((bf16[3,76,180]{2,1,0:T(8,128)(2,1)}, bf16[3,76,180]{2,1,0:T(8,128)(2,1)S(1)}, u32[]{:S(2)}, u32[]{:S(2)}) %collective-permute-start.1) | collective-permute-done | bytes 82112 | tf_op jit(solution)/shard_map/ppermute | solution.py:331
  89.6 2.7 %collective-permute-start.3 = (bf16[51,76,3]{1,0,2:T(8,128)(2,1)S(1)}, bf16[51,76,3]{1,0,2:T(8,128)(2,1)S(1)}, u32[]{:S(2)}, u32[]{:S(2)}) collective-permute-start(bf16[51,76,3]{1,0,2:T(8,128)(2,1)S(1)} %copy.64), channel_id=1, source_target_pairs={{1,0},{2,1},{3,2},{4,3},{5,4},{6,5},{7,6},{9,8},{10,9},{11,10},{12... | collective-permute-start | bytes 69776 | tf_op jit(solution)/shard_map/ppermute | solution.py:331
  92.8 3.3 %collective-permute-start.2 = (bf16[51,76,3]{1,0,2:T(8,128)(2,1)S(1)}, bf16[51,76,3]{1,0,2:T(8,128)(2,1)S(1)}, u32[]{:S(2)}, u32[]{:S(2)}) collective-permute-start(bf16[51,76,3]{1,0,2:T(8,128)(2,1)S(1)} %copy.63), channel_id=1, source_target_pairs={{0,1},{1,2},{2,3},{3,4},{4,5},{5,6},{6,7},{8,9},{9,10},{10,11},{11... | collective-permute-start | bytes 69776 | tf_op jit(solution)/shard_map/ppermute | solution.py:330
  99.2 4.7 %reshape.146.mix_ref = bf16[768,768]{1,0:T(8,128)(2,1)S(1)} reshape(bf16[8,2,48,8,2,48]{5,4,3,2,1,0:T(2,128)(2,1)} %maximum_bitcast_fusion) | data formatting | bytes 2359296 | tf_op jit(solution)/shard_map/reshape | solution.py:403
  111.5 4.0 %collective-permute-start.4 = (f32[6,372]{1,0:T(8,128)S(1)}, f32[6,372]{1,0:T(8,128)S(1)}, u32[]{:S(2)}, u32[]{:S(2)}) collective-permute-start(f32[6,372]{1,0:T(8,128)S(1)} %get-tuple-element.23), channel_id=1, source_target_pairs={{0,8},{8,16},{16,24},{24,32},{32,40},{40,48},{48,56},{56,64},{64,7... | collective-permute-start | bytes 26792 | tf_op jit(solution)/shard_map/ppermute | solution.py:330
  115.5 5.4 %spectral.1 = bf16[3072,384]{1,0:T(8,128)(2,1)S(1)} custom-call(bf16[3072,384]{1,0:T(8,128)(2,1)} %bitcast.2.wire_ref, bf16[2,2,384,256]{3,2,1,0:T(8,128)(2,1)S(1)} %bitcast.66, bf16[2,2,384,256]{3,2,1,0:T(8,128)(2,1)S(1)} %bitcast.67, bf16[768,768]{1,0:T(8,128)(2,1)S(1)} %reshape.146.mix_ref, f32[384,1]{1,0:T(8,128)S(1)} %reshape.157.gain_ref, ...), custom_call_target="tpu_custom_call" | custom-call | flops 2147483648 | bytes 9437184 | tf_op jit(solution)/shard_map/spectral/pallas_call | solution.py:130
  122.3 10.7 %all-to-all-start.3 = ((bf16[128,24,384]{2,1,0:T(8,128)(2,1)}), bf16[128,24,384]{2,1,0:T(8,128)(2,1)S(1)}, u32[]{:S(2)}, u32[]{:S(2)}) async-start(bf16[128,24,384]{2,1,0:T(8,128)(2,1)} %bitcast.65), calls=%async_computation.3 | async-start | bytes 4718592 | tf_op jit(solution)/shard_map/all_to_all | solution.py:370
  133.0 4.7 %pad_maximum_fusion.1.padded_ref = bf16[51,76,186]{2,1,0:T(8,128)(2,1)} fusion(bf16[51,76,3]{2,1,0:T(8,128)(2,1)} %copy.66, bf16[3,76,180]{2,1,0:T(8,128)(2,1)S(1)} %copy-done.23, bf16[45,76,180]{2,1,0:T(8,128)(2,1)} %bitcast.60, bf16[3,76,180]{2,1,0:T(8,128)(2,1)} %collective-permute-done, bf16[51,76,3]{2,1,0:T(8,128)(2,1)} %copy.65), kind=kLoop, calls=%fused_computation.2 | loop fusion | flops 7209360 | bytes 2883744 | tf_op jit(solution)/shard_map/concatenate | solution.py:332
  144.9 38.5 %ocean_block.1 = bf16[45,76,180]{2,1,0:T(8,128)(2,1)} custom-call(bf16[51,76,186]{2,1,0:T(8,128)(2,1)S(1)} %copy-done.7, f32[51,4,186]{2,1,0:T(4,128)S(1)} %reshape.153.flux_ref, f32[76,4]{1,0:T(8,128)S(1)} %copy.70.force_ref, f32[80,49]{1,0:T(8,128)S(1)} %pad_convert_fusion.taps_ref, f32[76,1]{1,0:T(8,128)S(1)} %copy.71.gain_ref, ...), custom_call_target="tpu_custom_call" | custom-call | flops 21474836480 | bytes 8388608 | tf_op jit(solution)/shard_map/ocean_block/pallas_call | solution.py:302
  183.4 2.9 %copy-done.2 = bf16[48,45,1440]{2,0,1:T(8,128)(2,1)S(1)} copy-done((bf16[48,45,1440]{2,0,1:T(8,128)(2,1)S(1)}, bf16[48,45,1440]{2,0,1:T(8,128)(2,1)}, u32[]{:S(2)}) %copy-start.2) | copy-done | bytes 6220824
  187.7 8.4 %dft_inverse.1 = bf16[45,48,1440]{2,1,0:T(8,128)(2,1)} custom-call(bf16[3072,384]{1,0:T(8,128)(2,1)S(1)} %bitcast.58, bf16[512,1440]{1,0:T(8,128)(2,1)S(1)} %copy-done.8, bf16[384,384]{1,0:T(8,128)(2,1)S(1)} %copy-done.9, bf16[45,48,1440]{2,1,0:T(8,128)(2,1)S(1)} %bitcast.57, f32[48,1]{1,0:T(8,128)S(1)} %copy.61.gain_ref, ...), custom_call_target="tpu_custom_call" | custom-call | flops 3185049600 | bytes 20971520 | tf_op jit(solution)/shard_map/dft_inverse/pallas_call | solution.py:174
  (129 shorter events, 38.8 us)
Async XLA Ops:
  0.6 15.6 %copy-start.17 = (bf16[4,8,16,1440]{3,2,1,0:T(8,128)(2,1)S(1)}, bf16[4,8,16,1440]{3,2,1,0:T(8,128)(2,1)}, u32[]{:S(2)}) copy-start(bf16[4,8,16,1440]{3,2,1,0:T(8,128)(2,1)} %constant.75) | copy-start | bytes 4423684
  3.2 12.7 %all-to-all-start.1 = ((bf16[8,48,180]{2,1,0:T(8,128)(2,1)}), bf16[8,48,180]{2,1,0:T(8,128)(2,1)S(1)}, u32[]{:S(2)}, u32[]{:S(2)}) async-start(bf16[8,48,180]{2,1,0:T(8,128)(2,1)} %broadcast_in_dim.26), calls=%async_computation.1 | async-start | bytes 393216 | tf_op jit(solution)/shard_map/all_to_all | solution.py:376
  15.9 8.3 %copy-start.18 = (bf16[8,48,180]{2,1,0:T(8,128)(2,1)}, bf16[8,48,180]{2,1,0:T(8,128)(2,1)S(1)}, u32[]{:S(2)}) copy-start(bf16[8,48,180]{2,1,0:T(8,128)(2,1)S(1)} %all-to-all-done.1) | copy-start | bytes 414724
  16.0 8.2 %copy-start.15 = (bf16[45,8,180]{2,1,0:T(8,128)(2,1)}, bf16[45,8,180]{2,1,0:T(8,128)(2,1)S(1)}, u32[]{:S(2)}) copy-start(bf16[45,8,180]{2,1,0:T(8,128)(2,1)S(1)} %copy.55) | copy-start | bytes 388804
  17.5 13.5 %all-to-all-start.2 = ((bf16[16,4,48]{2,1,0:T(4,128)(2,1)}), bf16[16,4,48]{2,1,0:T(4,128)(2,1)S(1)}, u32[]{:S(2)}, u32[]{:S(2)}) async-start(bf16[16,4,48]{2,1,0:T(4,128)(2,1)} %pad.27.clone), calls=%async_computation.2 | async-start | bytes 32768 | tf_op jit(solution)/shard_map/all_to_all | solution.py:388
  27.2 9.4 %copy-start.11 = (bf16[1440,512]{1,0:T(8,128)(2,1)S(1)}, bf16[1440,512]{1,0:T(8,128)(2,1)}, u32[]{:S(2)}) copy-start(bf16[1440,512]{1,0:T(8,128)(2,1)} %constant.55.clone.table_ref) | copy-start | bytes 4423684
  27.2 9.4 %copy-start.12 = (bf16[384,384]{1,0:T(8,128)(2,1)S(1)}, bf16[384,384]{1,0:T(8,128)(2,1)}, u32[]{:S(2)}) copy-start(bf16[384,384]{1,0:T(8,128)(2,1)} %constant.57.clone.swap_ref) | copy-start | bytes 884740
  31.0 17.1 %all-to-all-start.4 = ((bf16[8,96,372]{2,1,0:T(8,128)(2,1)}), bf16[8,96,372]{2,1,0:T(8,128)(2,1)S(1)}, u32[]{:S(2)}, u32[]{:S(2)}) async-start(bf16[8,96,372]{2,1,0:T(8,128)(2,1)} %flux_parts.1), calls=%async_computation.4 | async-start | bytes 1179648 | tf_op jit(solution)/shard_map/all_to_all | solution.py:408
  48.9 9.3 %copy-start.3 = (bf16[76,45,180]{2,0,1:T(8,128)(2,1)S(1)}, bf16[76,45,180]{2,0,1:T(8,128)(2,1)}, u32[]{:S(2)}) copy-start(bf16[76,45,180]{2,0,1:T(8,128)(2,1)} %param.26) | copy-start | bytes 3693604
  48.9 15.9 %copy-start.21 = (bf16[2,384,384]{2,1,0:T(8,128)(2,1)S(1)}, bf16[2,384,384]{2,1,0:T(8,128)(2,1)}, u32[]{:S(2)}) copy-start(bf16[2,384,384]{2,1,0:T(8,128)(2,1)} %param.23) | copy-start | bytes 1769476
  48.9 66.6 %all-to-all-start = ((bf16[128,24,384]{2,1,0:T(8,128)(2,1)}), bf16[128,24,384]{2,1,0:T(8,128)(2,1)}, u32[]{:S(2)}, u32[]{:S(2)}) async-start(bf16[128,24,384]{2,1,0:T(8,128)(2,1)} %bitcast.64), calls=%async_computation | async-start | bytes 4718592 | tf_op jit(solution)/shard_map/all_to_all | solution.py:370
  58.9 28.4 %collective-permute-start.1 = (bf16[3,76,180]{2,1,0:T(8,128)(2,1)}, bf16[3,76,180]{2,1,0:T(8,128)(2,1)S(1)}, u32[]{:S(2)}, u32[]{:S(2)}) collective-permute-start(bf16[3,76,180]{2,1,0:T(8,128)(2,1)} %get-tuple-element.17), channel_id=1, source_target_pairs={{8,0},{16,8},{24,16},{32,24},{40,32},{48,40},{56,48},{64,56},{72,6... | collective-permute-start | bytes 246248 | tf_op jit(solution)/shard_map/ppermute | solution.py:331
  60.1 27.1 %collective-permute-start = (bf16[3,76,180]{2,1,0:T(8,128)(2,1)}, bf16[3,76,180]{2,1,0:T(8,128)(2,1)}, u32[]{:S(2)}, u32[]{:S(2)}) collective-permute-start(bf16[3,76,180]{2,1,0:T(8,128)(2,1)} %get-tuple-element.16), channel_id=1, source_target_pairs={{0,8},{8,16},{16,24},{24,32},{32,40},{40,48},{48,56},{56,64},{64,7... | collective-permute-start | bytes 246248 | tf_op jit(solution)/shard_map/ppermute | solution.py:330
  77.3 6.9 %copy-start.28 = (bf16[48]{0:T(256)(128)(2,1)S(1)}, bf16[48]{0:T(256)(128)(2,1)}, u32[]{:S(2)}) copy-start(bf16[48]{0:T(256)(128)(2,1)} %param.20) | copy-start | bytes 292
  77.3 6.9 %copy-start.25 = (bf16[76,1,7,7]{0,3,2,1:T(8,128)(2,1)S(1)}, bf16[76,1,7,7]{0,3,2,1:T(8,128)(2,1)}, u32[]{:S(2)}) copy-start(bf16[76,1,7,7]{0,3,2,1:T(8,128)(2,1)} %param.28) | copy-start | bytes 22348
  89.1 7.1 %copy-start.19 = (bf16[2,256,720]{1,2,0:T(8,128)(2,1)S(1)}, bf16[2,256,720]{1,2,0:T(8,128)(2,1)}, u32[]{:S(2)}) copy-start(bf16[2,256,720]{1,2,0:T(8,128)(2,1)} %param.21) | copy-start | bytes 2211844
  89.6 15.1 %collective-permute-start.3 = (bf16[51,76,3]{1,0,2:T(8,128)(2,1)S(1)}, bf16[51,76,3]{1,0,2:T(8,128)(2,1)S(1)}, u32[]{:S(2)}, u32[]{:S(2)}) collective-permute-start(bf16[51,76,3]{1,0,2:T(8,128)(2,1)S(1)} %copy.64), channel_id=1, source_target_pairs={{1,0},{2,1},{3,2},{4,3},{5,4},{6,5},{7,6},{9,8},{10,9},{11,10},{12... | collective-permute-start | bytes 69776 | tf_op jit(solution)/shard_map/ppermute | solution.py:331
  92.8 13.4 %collective-permute-start.2 = (bf16[51,76,3]{1,0,2:T(8,128)(2,1)S(1)}, bf16[51,76,3]{1,0,2:T(8,128)(2,1)S(1)}, u32[]{:S(2)}, u32[]{:S(2)}) collective-permute-start(bf16[51,76,3]{1,0,2:T(8,128)(2,1)S(1)} %copy.63), channel_id=1, source_target_pairs={{0,1},{1,2},{2,3},{3,4},{4,5},{5,6},{6,7},{8,9},{9,10},{10,11},{11... | collective-permute-start | bytes 69776 | tf_op jit(solution)/shard_map/ppermute | solution.py:330
  110.2 27.9 %collective-permute-start.5 = (f32[6,372]{1,0:T(8,128)S(1)}, f32[6,372]{1,0:T(8,128)S(1)}, u32[]{:S(2)}, u32[]{:S(2)}) collective-permute-start(f32[6,372]{1,0:T(8,128)S(1)} %get-tuple-element.24), channel_id=1, source_target_pairs={{8,0},{16,8},{24,16},{32,24},{40,32},{48,40},{56,48},{64,56},{72,6... | collective-permute-start | bytes 26792 | tf_op jit(solution)/shard_map/ppermute | solution.py:331
  111.5 26.6 %collective-permute-start.4 = (f32[6,372]{1,0:T(8,128)S(1)}, f32[6,372]{1,0:T(8,128)S(1)}, u32[]{:S(2)}, u32[]{:S(2)}) collective-permute-start(f32[6,372]{1,0:T(8,128)S(1)} %get-tuple-element.23), channel_id=1, source_target_pairs={{0,8},{8,16},{16,24},{24,32},{32,40},{40,48},{48,56},{56,64},{64,7... | collective-permute-start | bytes 26792 | tf_op jit(solution)/shard_map/ppermute | solution.py:330
  122.3 10.7 %copy-start.23 = (bf16[3,76,180]{2,1,0:T(8,128)(2,1)S(1)}, bf16[3,76,180]{2,1,0:T(8,128)(2,1)}, u32[]{:S(2)}) copy-start(bf16[3,76,180]{2,1,0:T(8,128)(2,1)} %copy-done.22) | copy-start | bytes 246244
  122.3 61.2 %all-to-all-start.3 = ((bf16[128,24,384]{2,1,0:T(8,128)(2,1)}), bf16[128,24,384]{2,1,0:T(8,128)(2,1)S(1)}, u32[]{:S(2)}, u32[]{:S(2)}) async-start(bf16[128,24,384]{2,1,0:T(8,128)(2,1)} %bitcast.65), calls=%async_computation.3 | async-start | bytes 4718592 | tf_op jit(solution)/shard_map/all_to_all | solution.py:370
  133.0 8.8 %copy-start.10 = (bf16[76,304]{1,0:T(8,128)(2,1)S(1)}, bf16[76,304]{1,0:T(8,128)(2,1)}, u32[]{:S(2)}) copy-start(bf16[76,304]{1,0:T(8,128)(2,1)} %contract_ref.1) | copy-start | bytes 138628
  144.9 38.5 %copy-start.9 = (bf16[384,384]{1,0:T(8,128)(2,1)S(1)}, bf16[384,384]{1,0:T(8,128)(2,1)}, u32[]{:S(2)}) copy-start(bf16[384,384]{1,0:T(8,128)(2,1)} %constant.58.clone.swap_ref) | copy-start | bytes 884740
  (17 other events, 47.1 us)

commit v2 on v1

v2 whole, which is shorter than its diff:
```python
import functools
import math

import jax
import jax.numpy as jnp
import ml_dtypes
import numpy as np
from jax import lax
from jax.experimental import pallas as pl
from jax.experimental.pallas import tpu as pltpu
from jax.sharding import PartitionSpec as P

BF = jnp.bfloat16
F32 = jnp.float32
VMEM = pl.BlockSpec(memory_space=pltpu.VMEM)
NT = (((1,), (1,)), ((), ()))

HALF = 24


def peer_modes(lat_parts, chan_parts, per_dev):
    j, i, mm = np.meshgrid(np.arange(chan_parts), np.arange(lat_parts), np.arange(per_dev), indexing="ij")
    return ((i * chan_parts + j) * per_dev + mm).reshape(lat_parts * chan_parts, per_dev)


def dft_tables(lon_len, modes):
    total = modes.size
    product = np.arange(lon_len)[:, None, None] * modes.T[None]
    angle = np.float32(2.0 * math.pi / lon_len) * (product % lon_len).astype(np.float32)
    cos, sin = np.cos(angle), np.sin(angle)
    factor = np.float32(math.sqrt(2.0 / lon_len))
    forward = np.stack([factor * cos, -factor * sin], axis=2).reshape(lon_len, total * 2)
    back = np.float32(1.0 / math.sqrt(total))
    inverse = np.stack([back * cos, -back * sin], axis=2).reshape(lon_len, total * 2).T
    return forward.astype(ml_dtypes.bfloat16), np.ascontiguousarray(inverse).astype(ml_dtypes.bfloat16)


def row_swap(outer, inner):
    n = outer * inner
    swap = np.zeros((n, n), np.float32)
    o, k = np.meshgrid(np.arange(outer), np.arange(inner), indexing="ij")
    swap[(o * inner + k).ravel(), (k * outer + o).ravel()] = 1.0
    return swap.astype(ml_dtypes.bfloat16)


def dot(a, b, dims=(((1,), (0,)), ((), ()))):
    return lax.dot_general(a, b, dims, preferred_element_type=F32)


ANY = pl.BlockSpec(memory_space=pl.ANY)
SMEM = pl.BlockSpec(memory_space=pltpu.SMEM)
HBM = pl.BlockSpec(memory_space=pltpu.HBM)
BLOCK = 6


def row_groups(rows):
    return [(at, min(BLOCK, rows - at)) for at in range(0, rows, BLOCK)]


def column(row_ref):
    n = row_ref.shape[1]
    rows = jnp.broadcast_to(row_ref[...].astype(F32), (16, n))
    first = lax.broadcasted_iota(jnp.int32, (16, 128), 0) == 0
    return dot(rows.astype(BF), first.astype(F32).astype(BF), (((0,), (0,)), ((), ())))


def forward_kernel(
    at_ref, x, sea_ref, gain_ref, table, swap_ref, out_ref, sea, held, out, out_sems, sems
):
    rows, ch, lon = x.shape
    peers = held.shape[1]
    groups = row_groups(rows)
    sea_copy = pltpu.make_async_copy(sea_ref.at[:, pl.ds(0, 16), :], sea, sems.at[0])
    sea_copy.start()
    for at, size in groups:
        y = dot(x[at : at + size].reshape(size * ch, lon), table[...]).astype(BF)
        for a in range(0, size, 2):
            pieces = []
            for rh in range(2):
                for q in range(4):
                    if a + rh < size:
                        pieces.append(y[(a + rh) * ch : (a + rh + 1) * ch, q * peers : (q + 1) * peers])
                    else:
                        pieces.append(jnp.zeros((ch, peers), BF))
            held[(at + a) // 2] = jnp.concatenate(pieces, axis=0).T

    sea_copy.wait()
    own = sea[:, 0, :].astype(F32)
    own = jnp.concatenate([own, jnp.zeros((ch - rows, own.shape[1]), F32)], axis=0)
    wide = pl.cdiv(lon, 128) * 128
    own = jnp.concatenate([own, jnp.zeros((ch, wide - own.shape[1]), F32)], axis=1)
    own = pltpu.roll(own, at_ref[0], 1)[:, :lon].astype(BF)
    y = dot(own, table[...]).astype(BF)
    pieces = [y[:, q * peers : (q + 1) * peers] for q in range(4)]
    pieces.append(column(gain_ref).astype(BF))
    pieces.append(jnp.zeros((3 * ch, peers), BF))
    held[HALF - 1] = jnp.concatenate(pieces, axis=0).T

    out_copies = []
    for b in range(peers // 16):
        part = held[:, b * 16 : (b + 1) * 16, :].reshape(HALF * 16, held.shape[2])
        span = pl.ds(b * 16 * HALF, 16 * HALF)
        out[span, :] = dot(swap_ref[...], part).astype(BF)
        out_copies.append(pltpu.make_async_copy(out.at[span], out_ref.at[span], out_sems.at[b]))
        out_copies[-1].start()
    for copy in out_copies:
        copy.wait()


def forward(at, x, sea, gain, table, swap):
    rows, ch, lon = x.shape
    peers = table.shape[1] // 4
    return pl.pallas_call(
        forward_kernel,
        out_shape=pltpu.HBM((peers * HALF, 8 * ch), BF),
        in_specs=[SMEM, VMEM, HBM, VMEM, VMEM, VMEM],
        out_specs=ANY,
        scratch_shapes=[
            pltpu.VMEM((rows, 16, sea.shape[2]), BF),
            pltpu.VMEM((HALF, peers, 8 * ch), BF),
            pltpu.VMEM((peers * HALF, 8 * ch), BF),
            pltpu.SemaphoreType.DMA((peers // 16,)),
            pltpu.SemaphoreType.DMA((1,)),
        ],
        compiler_params=pltpu.CompilerParams(vmem_limit_bytes=24 << 20),
        cost_estimate=pl.CostEstimate(
            flops=2 * rows * ch * lon * peers * 4, bytes_accessed=14 << 20, transcendentals=0
        ),
        name="dft_forward",
    )(at, x, sea, gain, table, swap)


def spread_last(lat_parts):
    n = lat_parts * HALF
    col = np.arange(n)
    spread = np.zeros((n, n), np.float32)
    spread[col // HALF * HALF + HALF - 1, col] = 1.0
    return spread.astype(ml_dtypes.bfloat16)


def spectral_kernel(
    wire_hbm, analysis_hbm, synthesis_hbm, mix_hbm, spread_hbm, out_ref,
    wire_ref, analysis_ref, synthesis_ref, mix_ref, spread_ref, spec, mixed, gains, out,
    wire_sems, in_sems, sems
):
    size = analysis_ref.shape[2]
    ch = wire_ref.shape[1] // 8
    groups = wire_ref.shape[0] // size
    pairs = (
        (analysis_hbm, analysis_ref), (spread_hbm, spread_ref), (mix_hbm, mix_ref), (synthesis_hbm, synthesis_ref)
    )
    tables = [pltpu.make_async_copy(a, b, in_sems.at[k]) for k, (a, b) in enumerate(pairs)]
    wires = []
    for j in range(groups):
        span = pl.ds(j * size, size)
        wires.append(pltpu.make_async_copy(wire_hbm.at[span], wire_ref.at[span], wire_sems.at[j]))
    wires[0].start()
    tables[0].start()
    for copy in wires[1:] + tables[1:]:
        copy.start()
    tables[0].wait()
    lines = 0.0
    for j in range(groups):
        wires[j].wait()
        turned = wire_ref[j * size : (j + 1) * size, :].T
        for m in range(2):
            total = sum(
                dot(turned[(4 * rh + 2 * m) * ch : (4 * rh + 2 * m + 2) * ch, :], analysis_ref[m, rh])
                for rh in range(2)
            ).astype(BF)
            for k in range(2):
                spec[m, k, j * ch : (j + 1) * ch, :] = total[k * ch : (k + 1) * ch, :]
        gains[j * ch : (j + 1) * ch, :] = turned[4 * ch : 5 * ch, :128]
        lines = lines + turned[: 4 * ch, :].astype(F32)

    for copy in tables[1:]:
        copy.wait()
    lines = dot(lines.astype(BF), spread_ref[...])
    own_row = lax.broadcasted_iota(jnp.int32, (ch, size), 0)
    rr = lax.rem(lax.broadcasted_iota(jnp.int32, (ch, size), 1), HALF)
    real, imag = mix_ref[0], mix_ref[1]
    gain_real = dot(real, gains[...])[:, HALF - 1 : HALF]
    gain_imag = dot(imag, gains[...])[:, HALF - 1 : HALF]
    for m in range(2):
        surface = 0.0
        for rh in range(2):
            both = [
                jnp.sum(
                    jnp.where(own_row == 2 * rr + rh, lines[q * ch : (q + 1) * ch, :], 0.0),
                    axis=0,
                    keepdims=True,
                )
                for q in (2 * m, 2 * m + 1)
            ]
            both.append(jnp.zeros((6, size), F32))
            both = jnp.concatenate(both, axis=0).astype(BF)
            surface = surface + dot(both, analysis_ref[m, rh])
        sr, si = surface[0:1, :], surface[1:2, :]
        value = dot(real, spec[m, 0]) - dot(imag, spec[m, 1])
        mixed[m, 0] = (value + (gain_real * sr - gain_imag * si)).astype(BF)
        value = dot(imag, spec[m, 0]) + dot(real, spec[m, 1])
        mixed[m, 1] = (value + (gain_imag * sr + gain_real * si)).astype(BF)

    copies = []
    for j in range(groups):
        pieces = []
        for rh in range(2):
            for m in range(2):
                both = [mixed[m, k, j * ch : (j + 1) * ch, :] for k in range(2)]
                pieces.append(dot(synthesis_ref[m, rh], jnp.concatenate(both, axis=0), NT).astype(BF))
        span = pl.ds(j * size, size)
        out[span, :] = jnp.concatenate(pieces, axis=1)
        copies.append(pltpu.make_async_copy(out.at[span], out_ref.at[span], sems.at[j]))
        copies[-1].start()
    for copy in copies:
        copy.wait()


def spectral(wire, analysis, synthesis, mix, spread):
    _, _, size, degrees = analysis.shape
    groups = wire.shape[0] // size
    all_ch = mix.shape[1]
    return pl.pallas_call(
        spectral_kernel,
        out_shape=pltpu.HBM(wire.shape, BF),
        in_specs=[ANY] * 5,
        out_specs=ANY,
        scratch_shapes=[
            *(pltpu.VMEM(a.shape, BF) for a in (wire, analysis, synthesis, mix, spread)),
            pltpu.VMEM((2, 2, all_ch, degrees), BF),
            pltpu.VMEM((2, 2, all_ch, degrees), BF),
            pltpu.VMEM((all_ch, 128), BF),
            pltpu.VMEM(wire.shape, BF),
            pltpu.SemaphoreType.DMA((groups,)),
            pltpu.SemaphoreType.DMA((4,)),
            pltpu.SemaphoreType.DMA((groups,)),
        ],
        compiler_params=pltpu.CompilerParams(vmem_limit_bytes=56 << 20),
        cost_estimate=pl.CostEstimate(flops=2 << 30, bytes_accessed=9 << 20, transcendentals=0),
        name="spectral",
    )(wire, analysis, synthesis, mix, spread)


def inverse_kernel(
    wire_ref, table_ref, swap_ref, x_ref, gain_ref, parts_ref, out_ref,
    wire, table, held, x, out, lines, wire_sems, x_sems, out_sems, sems
):
    rows, ch, lon = x.shape
    peers = held.shape[1]
    groups = row_groups(rows)
    wire_copies = []
    for b in range(peers // 16):
        span = pl.ds(b * 16 * HALF, 16 * HALF)
        wire_copies.append(pltpu.make_async_copy(wire_ref.at[span], wire.at[span], wire_sems.at[b]))
        wire_copies[-1].start()
    table_copy = pltpu.make_async_copy(table_ref, table, sems.at[0])
    table_copy.start()
    x_copies = []
    for g, (at, size) in enumerate(groups):
        span = pl.ds(at, size)
        x_copies.append(pltpu.make_async_copy(x_ref.at[span], x.at[span], x_sems.at[g]))
        x_copies[-1].start()
    for b in range(peers // 16):
        wire_copies[b].wait()
        part = dot(swap_ref[...], wire[b * 16 * HALF : (b + 1) * 16 * HALF, :]).astype(BF)
        held[:, b * 16 : (b + 1) * 16, :] = part.reshape(HALF, 16, held.shape[2])
    chans, end, _ = parts_ref.shape
    for half in range(2):
        lines[half] = jnp.concatenate(
            [
                parts_ref[j, end - 32 :, half * PITCH : half * PITCH + lon // chans].astype(F32)
                for j in range(chans)
            ],
            axis=1,
        )
    gain = column(gain_ref)[:, :1]
    table_copy.wait()

    def wave_of(at, size):
        waves = []
        for a in range(0, size, 2):
            turned = held[(at + a) // 2].T
            for rh in range(min(2, size - a)):
                parts = [turned[(4 * rh + q) * ch : (4 * rh + q + 1) * ch, :] for q in range(4)]
                waves.append(jnp.concatenate(parts, axis=1))
        return dot(jnp.concatenate(waves, axis=0), table[...])

    out_copies = []
    wave = wave_of(*groups[0])
    for g, (at, size) in enumerate(groups):
        x_copies[g].wait()
        later = wave_of(*groups[g + 1]) if g + 1 < len(groups) else None
        for a in range(size):
            line = lines[a % 2, (at + a) // 2 : (at + a) // 2 + 1, :]
            forced = x[at + a].astype(F32) + gain * line
            out[at + a] = (forced + wave[a * ch : (a + 1) * ch, :]).astype(BF)
        span = pl.ds(at, size)
        out_copies.append(pltpu.make_async_copy(out.at[span], out_ref.at[span], out_sems.at[g]))
        out_copies[-1].start()
        wave = later
    for copy in out_copies:
        copy.wait()


def inverse(wire, table, swap, x, gain, parts):
    rows, ch, lon = x.shape
    peers = table.shape[0] // 4
    groups = len(row_groups(rows))
    return pl.pallas_call(
        inverse_kernel,
        out_shape=pltpu.HBM(x.shape, BF),
        in_specs=[ANY, ANY, VMEM, ANY, VMEM, VMEM],
        out_specs=ANY,
        scratch_shapes=[
            pltpu.VMEM(wire.shape, BF),
            pltpu.VMEM(table.shape, BF),
            pltpu.VMEM((HALF, peers, 8 * ch), BF),
            pltpu.VMEM(x.shape, BF),
            pltpu.VMEM(x.shape, BF),
            pltpu.VMEM((2, 32, lon), F32),
            pltpu.SemaphoreType.DMA((peers // 16,)),
            pltpu.SemaphoreType.DMA((groups,)),
            pltpu.SemaphoreType.DMA((groups,)),
            pltpu.SemaphoreType.DMA((1,)),
        ],
        compiler_params=pltpu.CompilerParams(vmem_limit_bytes=56 << 20),
        cost_estimate=pl.CostEstimate(
            flops=2 * rows * ch * lon * peers * 4, bytes_accessed=20 << 20, transcendentals=0
        ),
        name="dft_inverse",
    )(wire, table, swap, x, gain, parts)


PITCH = 192


def flux_kernel(reach, x_ref, sea_ref, weight_ref, out_ref, x, sea, x_sems, sems):
    rows, ch, lon = x.shape
    peers = out_ref.shape[0]
    tile = lon // peers
    block = 8
    groups = [(at, min(block, rows - at)) for at in range(0, rows, block)]
    copies = []
    for g, (at, size) in enumerate(groups):
        span = pl.ds(at, size)
        copies.append(pltpu.make_async_copy(x_ref.at[span], x.at[span], x_sems.at[g]))
        copies[-1].start()
    sea_copy = pltpu.make_async_copy(sea_ref.at[:, pl.ds(0, 16), :], sea, sems.at[0])
    sea_copy.start()
    weight = weight_ref[...].astype(F32)
    weight = jnp.concatenate([weight] * block, axis=1)
    weight = jnp.concatenate([weight] * block, axis=0)
    row = lax.broadcasted_iota(jnp.int32, weight.shape, 0)
    col = lax.broadcasted_iota(jnp.int32, weight.shape, 1)
    keep = col // ch == row % 16 // 4 * 2 + row // 16
    weight = jnp.where(keep, weight, 0.0).astype(BF)
    before = jnp.zeros((4 * block, reach), F32)
    after = jnp.zeros((4 * block, PITCH - tile - reach), F32)
    for g, (at, size) in enumerate(groups):
        copies[g].wait()
        y = dot(weight[:, : size * ch], x[at : at + size].reshape(size * ch, lon))
        y = jnp.concatenate([before, y, after], axis=1)
        for j in range(peers):
            part = y[:, tile * j : tile * j + PITCH]
            part = jnp.concatenate([part[: 2 * block], part[2 * block :]], axis=1)
            out_ref[j, 2 * block * g : 2 * block * (g + 1), :] = part.astype(BF)
    sea_copy.wait()
    own = jnp.concatenate([sea[:, 0, :].astype(F32), jnp.zeros((ch - rows, tile), F32)], axis=0)
    halves = []
    for half in range(2):
        pick = lax.broadcasted_iota(jnp.int32, (32, ch), 1) == (
            2 * lax.broadcasted_iota(jnp.int32, (32, ch), 0) + half
        )
        halves.append(dot(pick.astype(F32).astype(BF), own.astype(BF)))
        halves.append(jnp.zeros((32, PITCH - tile), F32))
    own = jnp.concatenate(halves, axis=1).astype(BF)
    for j in range(peers):
        out_ref[j, out_ref.shape[1] - 32 :, :] = own


def flux_parts(x, sea, weight, reach, peers):
    rows, ch, lon = x.shape
    groups = pl.cdiv(rows, 8)
    return pl.pallas_call(
        functools.partial(flux_kernel, reach),
        out_shape=jax.ShapeDtypeStruct((peers, groups * 16 + 32, 2 * PITCH), BF),
        in_specs=[HBM, HBM, VMEM],
        out_specs=VMEM,
        scratch_shapes=[
            pltpu.VMEM(x.shape, BF),
            pltpu.VMEM((rows, 16, sea.shape[2]), BF),
            pltpu.SemaphoreType.DMA((groups,)),
            pltpu.SemaphoreType.DMA((1,)),
        ],
        compiler_params=pltpu.CompilerParams(vmem_limit_bytes=24 << 20),
        cost_estimate=pl.CostEstimate(flops=1 << 30, bytes_accessed=7 << 20, transcendentals=0),
        name="flux_parts",
    )(x, sea, weight)


def column_kernel(reach, center_ref, first_ref, last_ref):
    rows, ch, cols = center_ref.shape
    shape = (16, cols)
    row = lax.broadcasted_iota(jnp.int32, shape, 0)
    col = lax.broadcasted_iota(jnp.int32, shape, 1)
    want = jnp.where(row % 8 < 2 * reach, row % 8 % reach + row // 8 * (cols - reach), -1)
    picks = []
    for half in range(2):
        pick = (col == want) & (row % 8 // reach == half)
        picks.append(pick.astype(F32).astype(BF))
    for s in range((rows + 1) // 2):
        value = dot(picks[0], center_ref[2 * s], NT)
        if 2 * s + 1 < rows:
            value = value + dot(picks[1], center_ref[2 * s + 1], NT)
        first_ref[s] = value[:8].astype(BF)
        last_ref[s] = value[8:].astype(BF)


def edge_columns(center, reach):
    rows, ch, _ = center.shape
    out = jax.ShapeDtypeStruct(((rows + 1) // 2, 8, ch), BF)
    return pl.pallas_call(
        functools.partial(column_kernel, reach),
        out_shape=(out, out),
        in_specs=[VMEM],
        out_specs=(VMEM, VMEM),
        compiler_params=pltpu.CompilerParams(vmem_limit_bytes=16 << 20),
        cost_estimate=pl.CostEstimate(flops=1 << 20, bytes_accessed=1 << 20, transcendentals=0),
        name="edge_columns",
    )(center)


def edge_picks(reach, span):
    picks = np.zeros((16, 2 * PITCH), np.float32)
    for side in range(2):
        for half in range(2):
            for dx in range(reach):
                picks[8 * side + reach * half + dx, PITCH * half + side * (span - reach) + dx] = 1.0
    return picks.astype(ml_dtypes.bfloat16)


def pair_forcing(s, left_ref, right_ref, picks, flux, force):
    high = flux.astype(BF).astype(F32)
    low = flux - high
    flux = jnp.concatenate([high, low, high, jnp.zeros_like(high)], axis=0).astype(BF)
    edge = jnp.concatenate([left_ref[s].astype(F32), right_ref[s].astype(F32)], axis=0).astype(BF)
    return dot(
        jnp.concatenate([edge, force], axis=0),
        jnp.concatenate([picks, flux], axis=0),
        (((0,), (0,)), ((), ())),
    )


def pair_rows(first, second, reach):
    ch, cols = first.shape
    before = jnp.zeros((ch, reach), F32)
    after = jnp.zeros((ch, PITCH - cols - reach), F32)
    first, second = first.astype(F32), second.astype(F32)
    return jnp.concatenate([before, first, after, before, second, after], axis=1)


def wet_kernel(
    reach, center_ref, left_ref, right_ref, picks_ref, parts_ref, force_ref,
    odd_ref, even_ref, forcing_ref, first_ref, last_ref, flux
):
    rows = center_ref.shape[0]
    own_pairs = odd_ref.shape[0]
    picks, force = picks_ref[...], force_ref[...]
    total = parts_ref[0].astype(F32)
    for j in range(1, parts_ref.shape[0]):
        total = total + parts_ref[j].astype(F32)
    for s in range(own_pairs):
        flux[s] = total[4 * s : 4 * s + 4, :]

    def fill(s, second):
        more = pair_forcing(s, left_ref, right_ref, picks, flux[s], force)
        forcing_ref[s] = pltpu.roll(more, 2 * PITCH - reach, 1)
        odd_ref[s] = (pair_rows(center_ref[2 * s], second, reach) + more).astype(BF)

    def fill_pair(s, carry):
        fill(s, center_ref[2 * s + 1])
        return carry

    def join(s, carry):
        even_ref[s] = jnp.concatenate([odd_ref[s][:, PITCH:], odd_ref[s + 1][:, :PITCH]], axis=1)
        return carry

    lax.fori_loop(0, own_pairs - 1, fill_pair, 0)
    fill(own_pairs - 1, center_ref[rows - 1])
    lax.fori_loop(0, own_pairs - 1, join, 0)
    even_ref[own_pairs - 1] = odd_ref[own_pairs - 1]
    for at, ref in ((0, first_ref), (rows - reach, last_ref)):
        for d in range(reach):
            half = (at + d) % 2
            ref[d] = odd_ref[(at + d) // 2][:, half * PITCH : (half + 1) * PITCH]


def wet_rows(center, left, right, picks, parts, force, reach):
    rows, ch, _ = center.shape
    edge = jax.ShapeDtypeStruct((reach, ch, PITCH), BF)
    pairs = (rows + 1) // 2
    own = jax.ShapeDtypeStruct((pairs, ch, 2 * PITCH), BF)
    return pl.pallas_call(
        functools.partial(wet_kernel, reach),
        out_shape=(own, own, jax.ShapeDtypeStruct(own.shape, F32), edge, edge),
        in_specs=[VMEM] * 6,
        out_specs=(VMEM,) * 5,
        scratch_shapes=[pltpu.VMEM((pairs, 4, 2 * PITCH), F32)],
        compiler_params=pltpu.CompilerParams(vmem_limit_bytes=24 << 20),
        cost_estimate=pl.CostEstimate(flops=1 << 20, bytes_accessed=1 << 20, transcendentals=0),
        name="wet_rows",
    )(center, left, right, picks, parts, force)


def ocean_kernel(
    reach, mask_tiles, center_ref, forcing_ref, odd_ref, even_ref, low_ref, high_ref, taps_ref, gain_ref,
    expand_ref, contract_ref, mask_ref, out_ref, odd, even, taps, gain, flag, smooth
):
    step = pl.program_id(0)
    _, ch, cols = center_ref.shape
    high_ch, wide = even.shape[1:]
    pairs = smooth.shape[0]
    side = 2 * reach + 1
    own_pairs = odd_ref.shape[0]

    @pl.when(step == 0)
    def _():
        def widen(s, carry):
            odd[s + 2, :ch, :] = odd_ref[s].astype(F32)
            even[s + 2, :ch, :] = even_ref[s].astype(F32)
            return carry

        lax.fori_loop(0, own_pairs, widen, 0)
        odd[0, :ch, PITCH:] = low_ref[0].astype(F32)
        odd[1, :ch, :] = jnp.concatenate([low_ref[1].astype(F32), low_ref[2].astype(F32)], axis=1)
        odd[own_pairs + 1, :ch, PITCH:] = high_ref[0].astype(F32)
        odd[own_pairs + 2, :ch, :] = jnp.concatenate(
            [high_ref[1].astype(F32), high_ref[2].astype(F32)], axis=1
        )
        for t in (0, 1, own_pairs + 1, own_pairs + 2):
            even[t] = jnp.concatenate([odd[t][:, PITCH:], odd[t + 1][:, :PITCH]], axis=1)
        for k in range(side * side):
            taps[k] = jnp.broadcast_to(taps_ref[:, k : k + 1], taps.shape[1:])
        gain[...] = jnp.broadcast_to(gain_ref[...], gain.shape)
        tall, across = mask_tiles
        mask = mask_ref[...].astype(F32).astype(BF)
        spread = 0.0
        for half in range(2):
            pair = lax.broadcasted_iota(jnp.int32, (32, 8), 0)
            tile = lax.broadcasted_iota(jnp.int32, (32, 8), 1)
            up = ((2 * pair + half) // tall == tile).astype(F32).astype(BF)
            lane = lax.broadcasted_iota(jnp.int32, (8, wide), 1) - half * PITCH
            tile = lax.broadcasted_iota(jnp.int32, (8, wide), 0)
            side_by = (lane >= 0) & (lane < cols) & (lane // across == tile)
            side_by = side_by.astype(F32).astype(BF)
            spread = spread + dot(dot(up, mask).astype(BF), side_by)
        for s in range(flag.shape[0]):
            flag[s] = jnp.broadcast_to(spread[s : s + 1, :], (8, wide))

    start = step * pairs

    def channels(c, carry):
        at = pl.multiple_of(c * 8, 8)
        total = [None] * pairs
        for dx in range(side):
            part = [None] * pairs
            for dy in range(side):
                tap = taps[dy * side + dx, pl.ds(at, 8), :]
                tap = jnp.concatenate([tap] * (wide // 128), axis=1)
                for p in range(pairs):
                    if dy % 2 == 0:
                        value = even[start + p + dy // 2, pl.ds(at, 8), :]
                    else:
                        value = odd[start + p + dy // 2 + 1, pl.ds(at, 8), :]
                    term = tap * value
                    part[p] = term if part[p] is None else part[p] + term
            for p in range(pairs):
                moved = part[p] if dx == 0 else pltpu.roll(part[p], wide - dx, 1)
                total[p] = moved if total[p] is None else total[p] + moved
        for p in range(pairs):
            smooth[p, pl.ds(at, 8), :] = total[p]
        return carry

    lax.fori_loop(0, high_ch // 8, channels, 0)
    scale = jnp.concatenate([gain[...]] * (wide // 128), axis=1)
    for p in range(pairs):
        value = smooth[p, :ch, :]
        value = value - jnp.mean(value, axis=0, keepdims=True)
        spread = jnp.mean(value * value, axis=0, keepdims=True)
        normed = (value * lax.rsqrt(spread + 1e-06) * scale).astype(BF)
        hidden = dot(expand_ref[...], normed)
        inner = hidden * (0.7978845608028654 + 0.035677408136300125 * (hidden * hidden))
        hidden = (hidden + hidden * jnp.tanh(inner)).astype(BF)
        branch = 0.5 * dot(contract_ref[...], hidden)
        change = flag[start + p][:1] * (forcing_ref[p] + branch)
        for half in range(2):
            moved = change[:, half * PITCH : half * PITCH + cols]
            out_ref[2 * p + half] = (center_ref[2 * p + half].astype(F32) + moved).astype(BF)


def ocean_block(
    center, forcing, odd, even, low, high, taps, gain, expand, contract, mask, mask_tiles, reach
):
    rows, ch, cols = center.shape
    pairs = 6
    steps = pl.cdiv((rows + 1) // 2, pairs)
    high_ch = pl.cdiv(ch, 8) * 8
    deep = steps * pairs + reach + 1
    whole = lambda a: pl.BlockSpec(a.shape, lambda g: (0,) * a.ndim)
    operands = (center, forcing, odd, even, low, high, taps, gain, expand, contract, mask)
    return pl.pallas_call(
        functools.partial(ocean_kernel, reach, mask_tiles),
        out_shape=jax.ShapeDtypeStruct(center.shape, BF),
        grid=(steps,),
        in_specs=[
            pl.BlockSpec((2 * pairs, ch, cols), lambda g: (g, 0, 0)),
            pl.BlockSpec((pairs, ch, 2 * PITCH), lambda g: (g, 0, 0)),
            *(whole(a) for a in operands[2:]),
        ],
        out_specs=pl.BlockSpec((2 * pairs, ch, cols), lambda g: (g, 0, 0)),
        scratch_shapes=[
            pltpu.VMEM((deep, high_ch, 2 * PITCH), F32),
            pltpu.VMEM((deep, high_ch, 2 * PITCH), F32),
            pltpu.VMEM((taps.shape[1], high_ch, 128), F32),
            pltpu.VMEM((ch, 128), F32),
            pltpu.VMEM((steps * pairs, 8, 2 * PITCH), F32),
            pltpu.VMEM((pairs, high_ch, 2 * PITCH), F32),
        ],
        compiler_params=pltpu.CompilerParams(vmem_limit_bytes=32 << 20),
        cost_estimate=pl.CostEstimate(
            flops=30 << 30, bytes_accessed=8 << 20, transcendentals=3 << 20
        ),
        name="ocean_block",
    )(*operands)


def shift(first, last, axis):
    count = lax.axis_size(axis)
    up = [(i, i + 1) for i in range(count - 1)]
    down = [(target, source) for source, target in up]
    return lax.ppermute(last, axis, up), lax.ppermute(first, axis, down)


def body(
    atmos,
    sea_temp_gain,
    legendre_analysis,
    legendre_synthesis,
    spectral_mixing_weight,
    surface_flux_weight,
    flux_ocean_forcing,
    ocean,
    ocean_tile_mask,
    depthwise_filter,
    norm_gain_vector,
    expand_matrix,
    contract_matrix,
):
    lat_parts = lax.axis_size("lat")
    chan_parts = lax.axis_size("chan")
    chan_at = lax.axis_index("chan")
    ch, rows, lon = atmos.shape
    per_dev, degrees, _ = legendre_analysis.shape
    ocean_ch, _, cols = ocean.shape
    reach = depthwise_filter.shape[2] // 2
    peers = lat_parts * chan_parts
    padded_rows = 2 * HALF

    table_fwd, table_inv = dft_tables(lon, peer_modes(lat_parts, chan_parts, per_dev))
    table_fwd, table_inv = jnp.asarray(table_fwd), jnp.asarray(table_inv)
    swap_out = jnp.asarray(row_swap(16, HALF))
    swap_in = jnp.asarray(row_swap(HALF, 16))

    x = jnp.transpose(atmos, (1, 0, 2))
    sea = jnp.transpose(ocean, (1, 0, 2))

    def exchange(wire):
        return lax.all_to_all(
            wire.reshape(peers, HALF, 8 * ch), ("chan", "lat"), 0, 0, tiled=True
        ).reshape(wire.shape)

    parts = flux_parts(x, sea, surface_flux_weight, reach, chan_parts)
    parts = lax.all_to_all(parts, "chan", 0, 0, tiled=True)

    gain = sea_temp_gain[None]
    at = jnp.reshape(chan_at * cols, (1,)).astype(jnp.int32)
    wire = forward(at, x, sea, gain, table_fwd, swap_out)
    gathered = exchange(wire)
    sea, legendre_analysis, legendre_synthesis, wire = lax.optimization_barrier(
        (sea, legendre_analysis, legendre_synthesis, wire)
    )
    left, right = shift(*edge_columns(sea, reach), "chan")
    force = flux_ocean_forcing.T
    force_high = force.astype(BF)
    force_low = (force - force_high.astype(F32)).astype(BF)
    force = jnp.concatenate([force_high, force_high, force_low, jnp.zeros_like(force_low)], axis=0)
    picks = jnp.asarray(edge_picks(reach, cols + 2 * reach))
    odd, even, forcing, first, last = wet_rows(sea, left, right, picks, parts, force, reach)
    low, high = shift(first, last, "lat")

    def banded(table):
        table = table.reshape(per_dev, lat_parts, rows, degrees)
        table = jnp.pad(table, ((0, 0), (0, 0), (0, padded_rows - rows), (0, 0)))
        table = table.reshape(per_dev, lat_parts, HALF, 2, degrees).transpose(0, 3, 1, 2, 4)
        return table.reshape(per_dev, 2, lat_parts * HALF, degrees)

    analysis = banded(jnp.transpose(legendre_analysis, (0, 2, 1)))
    synthesis = banded(legendre_synthesis)
    analysis, first, last = lax.optimization_barrier((analysis, first, last))
    back = spectral(
        gathered, analysis, synthesis, spectral_mixing_weight, jnp.asarray(spread_last(lat_parts))
    )
    back, low, high = lax.optimization_barrier((back, low, high))
    returned = exchange(back)

    tile_rows, tile_cols = ocean_tile_mask.shape
    mask = jnp.pad(ocean_tile_mask, ((0, 8 - tile_rows), (0, 8 - tile_cols)))
    taps = depthwise_filter.reshape(ocean_ch, -1).astype(F32)
    taps = jnp.pad(taps, ((0, -ocean_ch % 8), (0, 0)))
    ocean_next = ocean_block(
        sea,
        forcing,
        odd,
        even,
        low,
        high,
        taps,
        norm_gain_vector[:, None],
        expand_matrix,
        contract_matrix,
        mask,
        (rows // tile_rows, cols // tile_cols),
        reach,
    )

    atmos_next = inverse(returned, table_inv, swap_in, x, gain, parts)
    return (jnp.transpose(atmos_next, (1, 0, 2)), jnp.transpose(ocean_next, (1, 0, 2)))


def solution(mesh):
    in_specs = (
        P("chan", "lat", None),
        P("chan"),
        P(("lat", "chan"), None, None),
        P(("lat", "chan"), None, None),
        P(),
        P(None, "chan"),
        P(),
        P(None, "lat", "chan"),
        P("lat", "chan"),
        P(),
        P(),
        P(),
        P(),
    )
    out_specs = (P("chan", "lat", None), P(None, "lat", "chan"))
    return jax.shard_map(body, mesh=mesh, in_specs=in_specs, out_specs=out_specs, check_vma=False)
```

time: 197 us -> 149 us (0.76)
  local copies, waits for them, and re-layouts: 49.3 us -> 23.4 us
  other arithmetic: 17.5 us -> 0.09 us
  starting transfers between devices: 56.3 us -> 46.6 us
  waiting for transfers between devices: 7.93 us -> 11.6 us
  Pallas kernels: 63.3 us -> 65.6 us
    all_to_all x3 -> x1, starting transfers between devices: 19.1 us -> 6.83 us  [body(): parts = lax.all_to_all(parts, 'chan', 0, 0, tiled=True)]
    another operation x5 -> x0, local copies, waits for them, and re-layouts: 11.6 us -> none  [the longest x4 11.2 us: body(): jnp.stack([jnp.stack([real_part, -imag_part]), jnp.stack([imag_part, real...]
    all_to_all x2, starting transfers between devices: 20 us -> 30.1 us  [exchange(): lax.all_to_all(wire.reshape(peers, HALF, 8 * ch), ('chan', 'lat'), 0, 0,...]
    ppermute x6 -> x4, starting transfers between devices: 17.2 us -> 9.6 us  [shift(): return (lax.ppermute(last, axis, up), lax.ppermute(first, axis, down))]
    reshape x5 -> x0, local copies, waits for them, and re-layouts: 7.3 us -> none  [the longest x1 4.73 us: body(): mix = mix.reshape(2 * all_ch, 2 * all_ch)]
    transpose x1 -> x0, other arithmetic: 6.87 us -> none  [body(): mix.reshape(2, 2, chan_parts, ch, chan_parts, ch)]
    concatenate x3 -> x1, other arithmetic: 6.73 us -> 0.08 us  [body(): jnp.concatenate([force_high, force_high, force_low, jnp.zeros_like(force_...]
    all_to_all x2, waiting for transfers between devices: 0.01 us -> 5.84 us  [exchange(): lax.all_to_all(wire.reshape(peers, HALF, 8 * ch), ('chan', 'lat'), 0, 0,...]
  transfers between devices with their start and end apart: 11 -> 7, of which waited for: 2 -> 3; matrix products, arithmetic and copies ran while one was open for 23% -> 4% of each run, Pallas kernels for 28% -> 31%
where the time goes in v2:
time: 149 us; the launch traced here: 148 us
  Pallas kernels  65.6 us (44%)
  starting transfers between devices  46.6 us (31%)
  local copies, waits for them, and re-layouts  23.4 us (16%)
  waiting for transfers between devices  11.6 us (8%)
    all_to_all x2, starting transfers between devices, exchange(): lax.all_to_all(wire.reshape(peers, HALF, 8 * ch), ('chan', 'lat'), 0, 0,...  30.1 us
    pallas_call x1, Pallas kernels, ocean_block(): pl.pallas_call(functools.partial(ocean_kernel, reach, mask_tiles), out_sh...  21.9 us
    unnamed x49, local copies, waits for them, and re-layouts  18 us
    pallas_call x1, Pallas kernels, inverse(): pl.pallas_call(inverse_kernel, out_shape=pltpu.HBM(x.shape, BF), in_specs...  14.1 us
    ppermute x4, starting transfers between devices, shift(): return (lax.ppermute(last, axis, up), lax.ppermute(first, axis, down))  9.6 us
    pallas_call x1, Pallas kernels, wet_rows(): pl.pallas_call(functools.partial(wet_kernel, reach), out_shape=(own, own,...  8.87 us
    pallas_call x1, Pallas kernels, spectral(): pl.pallas_call(spectral_kernel, out_shape=pltpu.HBM(wire.shape, BF), in_s...  8.21 us
    all_to_all x1, starting transfers between devices, body(): parts = lax.all_to_all(parts, 'chan', 0, 0, tiled=True)  6.83 us
  transfers between devices with their start and end apart: 7, of which 3 were waited for; matrix products, arithmetic and copies ran while one was open for 4% of the time, Pallas kernels for 31%

profile of v2, /device:TPU:1, one launch (start us, length us, event | category | flops | bytes accessed | tf_op | source)
XLA Modules:
  0.0 148.3 jit_solution(3767289461039134632)
XLA Ops:
  0.6 2.9 %copy-done = bf16[48,45,1440]{2,0,1:T(8,128)(2,1)S(1)} copy-done((bf16[48,45,1440]{2,0,1:T(8,128)(2,1)S(1)}, bf16[48,45,1440]{2,0,1:T(8,128)(2,1)}, u32[]{:S(2)}) %copy-start) | copy-done | bytes 6220824
  3.5 1.5 %copy-done.2 = bf16[76,45,180]{2,0,1:T(8,128)(2,1)S(1)} copy-done((bf16[76,45,180]{2,0,1:T(8,128)(2,1)S(1)}, bf16[76,45,180]{2,0,1:T(8,128)(2,1)}, u32[]{:S(2)}) %copy-start.2) | copy-done | bytes 1231224
  5.7 5.5 %flux_parts.1 = bf16[8,128,384]{2,1,0:T(8,128)(2,1)} custom-call(bf16[45,48,1440]{2,1,0:T(8,128)(2,1)S(1)} %bitcast.31, bf16[45,76,180]{2,1,0:T(8,128)(2,1)S(1)} %bitcast.33, bf16[4,48]{1,0:T(4,128)(2,1)S(1)} %copy-done.9), custom_call_target="tpu_custom_call" | custom-call | flops 1073741824 | bytes 7340032 | tf_op jit(solution)/shard_map/flux_parts/pallas_call | solution.py:384
  11.2 6.8 %all-to-all-start.1 = ((bf16[8,128,384]{2,1,0:T(8,128)(2,1)}), bf16[8,128,384]{2,1,0:T(8,128)(2,1)S(1)}, u32[]{:S(2)}, u32[]{:S(2)}) async-start(bf16[8,128,384]{2,1,0:T(8,128)(2,1)} %flux_parts.1), calls=%async_computation.1 | async-start | bytes 1572864 | tf_op jit(solution)/shard_map/all_to_all | solution.py:683
  18.1 2.9 %copy-done.1 = bf16[48,45,1440]{2,0,1:T(8,128)(2,1)S(1)} copy-done((bf16[48,45,1440]{2,0,1:T(8,128)(2,1)S(1)}, bf16[48,45,1440]{2,0,1:T(8,128)(2,1)}, u32[]{:S(2)}) %copy-start.1) | copy-done | bytes 6220824
  20.9 1.4 copy-done.5
  22.3 6.5 %dft_forward.1 = bf16[3072,384]{1,0:T(8,128)(2,1)} custom-call(s32[1]{0:T(128)} %bitcast.at_ref, bf16[45,48,1440]{2,1,0:T(8,128)(2,1)S(1)} %bitcast.32, bf16[45,76,180]{2,1,0:T(8,128)(2,1)S(1)} %bitcast.34, bf16[1,48]{1,0:T(2,128)(2,1)S(1)} %bitcast.39, bf16[1440,512]{1,0:T(8,128)(2,1)S(1)} %copy-done.5, bf16[384,384]{1,0:T(8,128)(2,1)S(1)} %copy-done.6), custom_call_target="tpu_custom_call" | custom-call | flops 3185049600 | bytes 14680064 | tf_op jit(solution)/shard_map/dft_forward/pallas_call | solution.py:113
  28.8 1.5 %all-to-all-done.1.parts_ref = bf16[8,128,384]{2,1,0:T(8,128)(2,1)S(1)} async-done(((bf16[8,128,384]{2,1,0:T(8,128)(2,1)}), bf16[8,128,384]{2,1,0:T(8,128)(2,1)S(1)}, u32[]{:S(2)}, u32[]{:S(2)}) %all-to-all-start.1) | async-done | bytes 786464 | tf_op jit(solution)/shard_map/all_to_all | solution.py:683
  30.3 8.4 %all-to-all-start = ((bf16[128,24,384]{2,1,0:T(8,128)(2,1)}), bf16[128,24,384]{2,1,0:T(8,128)(2,1)}, u32[]{:S(2)}, u32[]{:S(2)}) async-start(bf16[128,24,384]{2,1,0:T(8,128)(2,1)} %bitcast.40), calls=%async_computation | async-start | bytes 4718592 | tf_op jit(solution)/shard_map/all_to_all | solution.py:678
  39.3 3.7 %collective-permute-start = (bf16[23,8,76]{2,1,0:T(8,128)(2,1)S(1)}, bf16[23,8,76]{2,1,0:T(8,128)(2,1)S(1)}, u32[]{:S(2)}, u32[]{:S(2)}) collective-permute-start(bf16[23,8,76]{2,1,0:T(8,128)(2,1)S(1)} %get-tuple-element.18), channel_id=1, source_target_pairs={{0,1},{1,2},{2,3},{3,4},{4,5},{5,6},{6,7},{8,9},{9,10},{10,11},{11... | collective-permute-start | bytes 83912 | tf_op jit(solution)/shard_map/ppermute | solution.py:641
  43.0 1.9 %collective-permute-start.1 = (bf16[23,8,76]{2,1,0:T(8,128)(2,1)S(1)}, bf16[23,8,76]{2,1,0:T(8,128)(2,1)S(1)}, u32[]{:S(2)}, u32[]{:S(2)}) collective-permute-start(bf16[23,8,76]{2,1,0:T(8,128)(2,1)S(1)} %get-tuple-element.19), channel_id=1, source_target_pairs={{1,0},{2,1},{3,2},{4,3},{5,4},{6,5},{7,6},{9,8},{10,9},{11,10},{12... | collective-permute-start | bytes 83912 | tf_op jit(solution)/shard_map/ppermute | solution.py:641
  45.3 1.7 %copy.24 = bf16[2,720,256]{2,0,1:T(2,128)(2,1)S(1)} copy(bf16[2,720,256]{2,1,0:T(8,128)(2,1)} %bitcast.49) | data formatting | bytes 1474560 | tf_op jit(solution)/shard_map/transpose | solution.py:707
  49.3 1.4 copy.29
  50.9 4.2 %collective-permute-done.1.right_ref = bf16[23,8,76]{2,1,0:T(8,128)(2,1)S(1)} collective-permute-done((bf16[23,8,76]{2,1,0:T(8,128)(2,1)S(1)}, bf16[23,8,76]{2,1,0:T(8,128)(2,1)S(1)}, u32[]{:S(2)}, u32[]{:S(2)}) %collective-permute-start.1) | collective-permute-done | bytes 28000 | tf_op jit(solution)/shard_map/ppermute | solution.py:641
  55.2 8.9 %wet_rows.1 = (bf16[23,76,384]{2,1,0:T(8,128)(2,1)S(1)}, bf16[23,76,384]{2,1,0:T(8,128)(2,1)S(1)}, f32[23,76,384]{2,1,0:T(8,128)S(1)}, bf16[3,76,192]{2,1,0:T(8,128)(2,1)S(1)}, bf16[3,76,192]{2,1,0:T(8,128)(2,1)S(1)}) custom-call(bf16[45,76,180]{2,1,0:T(8,128)(2,1)S(1)} %bitcast.36, bf16[23,8,76]{2,1,0:T(8,128)(2,1)S(1)} %collective-permute-done.left_ref, ...), custom_call_target="tpu_custom_call" | custom-call | flops 1048576 | bytes 1048576 | tf_op jit(solution)/shard_map/wet_rows/pallas_call | solution.py:503
  64.0 1.5 %copy-done.10 = f32[23,76,384]{2,1,0:T(8,128)} copy-done((f32[23,76,384]{2,1,0:T(8,128)}, f32[23,76,384]{2,1,0:T(8,128)S(1)}, u32[]{:S(2)}) %copy-start.10) | copy-done | bytes 2684952
  67.8 2.5 %collective-permute-start.2 = (bf16[3,76,192]{2,1,0:T(8,128)(2,1)S(1)}, bf16[3,76,192]{2,1,0:T(8,128)(2,1)S(1)}, u32[]{:S(2)}, u32[]{:S(2)}) collective-permute-start(bf16[3,76,192]{2,1,0:T(8,128)(2,1)S(1)} %get-tuple-element.21), channel_id=1, source_target_pairs={{0,8},{8,16},{16,24},{24,32},{32,40},{40,48},{48,56},{56,64},{64,7... | collective-permute-start | bytes 262664 | tf_op jit(solution)/shard_map/ppermute | solution.py:641
  70.4 1.5 collective-permute-start.3
  71.9 8.2 %spectral.1 = bf16[3072,384]{1,0:T(8,128)(2,1)} custom-call(bf16[3072,384]{1,0:T(8,128)(2,1)} %bitcast.5.wire_hbm, bf16[2,2,384,256]{3,2,1,0:T(8,128)(2,1)} %bitcast.47, bf16[2,2,384,256]{3,2,1,0:T(8,128)(2,1)} %bitcast.48, bf16[2,384,384]{2,1,0:T(8,128)(2,1)} %mix_hbm.1, bf16[384,384]{1,0:T(8,128)(2,1)} %constant.30.clone.spread_hbm), custom_call_target="tpu_custom_call" | custom-call | flops 2147483648 | bytes 9437184 | tf_op jit(solution)/shard_map/spectral/pallas_call | solution.py:223
  80.1 21.7 %all-to-all-start.2 = ((bf16[128,24,384]{2,1,0:T(8,128)(2,1)}), bf16[128,24,384]{2,1,0:T(8,128)(2,1)}, u32[]{:S(2)}, u32[]{:S(2)}) async-start(bf16[128,24,384]{2,1,0:T(8,128)(2,1)} %bitcast.46), calls=%async_computation.2 | async-start | bytes 4718592 | tf_op jit(solution)/shard_map/all_to_all | solution.py:678
  101.9 1.8 %copy-done.11 = f32[23,76,384]{2,1,0:T(8,128)S(1)} copy-done((f32[23,76,384]{2,1,0:T(8,128)S(1)}, f32[23,76,384]{2,1,0:T(8,128)}, u32[]{:S(2)}) %copy-start.11) | copy-done | bytes 2684952
  106.4 21.9 %ocean_block.1 = bf16[45,76,180]{2,1,0:T(8,128)(2,1)} custom-call(bf16[45,76,180]{2,1,0:T(8,128)(2,1)S(1)} %bitcast.37, f32[23,76,384]{2,1,0:T(8,128)S(1)} %copy-done.11, bf16[23,76,384]{2,1,0:T(8,128)(2,1)S(1)} %copy-done.13, bf16[23,76,384]{2,1,0:T(8,128)(2,1)S(1)} %copy-done.15, bf16[3,76,192]{2,1,0:T(8,128)(2,1)S(1)} %collective-permute-done.2.low_ref, ...), custom_call_target="tpu_custom_call" | custom-call | flops 32212254720 | bytes 8388608 | tf_op jit(solution)/shard_map/ocean_block/pallas_call | solution.py:611
  128.3 5.8 %all-to-all-done.2 = bf16[128,24,384]{2,1,0:T(8,128)(2,1)} async-done(((bf16[128,24,384]{2,1,0:T(8,128)(2,1)}), bf16[128,24,384]{2,1,0:T(8,128)(2,1)}, u32[]{:S(2)}, u32[]{:S(2)}) %all-to-all-start.2) | async-done | bytes 2359328 | tf_op jit(solution)/shard_map/all_to_all | solution.py:678
  134.1 14.1 %dft_inverse.1 = bf16[45,48,1440]{2,1,0:T(8,128)(2,1)} custom-call(bf16[3072,384]{1,0:T(8,128)(2,1)} %bitcast.17.wire_ref, bf16[512,1440]{1,0:T(8,128)(2,1)} %constant.26.clone.table_ref, bf16[384,384]{1,0:T(8,128)(2,1)} %constant.28.clone.swap_ref, bf16[45,48,1440]{2,1,0:T(8,128)(2,1)} %bitcast.30, bf16[1,48]{1,0:T(2,128)(2,1)} %bitcast.38, ...), custom_call_target="tpu_custom_call" | custom-call | flops 3185049600 | bytes 20971520 | tf_op jit(solution)/shard_map/dft_inverse/pallas_call | solution.py:309
  (61 shorter events, 9.1 us)
Async XLA Ops:
  0.6 2.9 %copy-start = (bf16[48,45,1440]{2,0,1:T(8,128)(2,1)S(1)}, bf16[48,45,1440]{2,0,1:T(8,128)(2,1)}, u32[]{:S(2)}) copy-start(bf16[48,45,1440]{2,0,1:T(8,128)(2,1)} %param.19) | copy-start | bytes 18662404
  3.5 1.5 %copy-start.2 = (bf16[76,45,180]{2,0,1:T(8,128)(2,1)S(1)}, bf16[76,45,180]{2,0,1:T(8,128)(2,1)}, u32[]{:S(2)}) copy-start(bf16[76,45,180]{2,0,1:T(8,128)(2,1)} %param.26) | copy-start | bytes 3693604
  5.7 12.3 %copy-start.3 = (bf16[76,45,180]{2,0,1:T(8,128)(2,1)S(1)}, bf16[76,45,180]{2,0,1:T(8,128)(2,1)}, u32[]{:S(2)}) copy-start(bf16[76,45,180]{2,0,1:T(8,128)(2,1)} %param.26) | copy-start | bytes 3693604
  5.7 12.3 %copy-start.6 = (bf16[384,384]{1,0:T(8,128)(2,1)S(1)}, bf16[384,384]{1,0:T(8,128)(2,1)}, u32[]{:S(2)}) copy-start(bf16[384,384]{1,0:T(8,128)(2,1)} %constant.27.clone.swap_ref) | copy-start | bytes 884740
  5.7 12.3 %copy-start.8 = (bf16[48]{0:T(256)(128)(2,1)S(1)}, bf16[48]{0:T(256)(128)(2,1)}, u32[]{:S(2)}) copy-start(bf16[48]{0:T(256)(128)(2,1)} %param.20) | copy-start | bytes 292
  11.2 19.1 %all-to-all-start.1 = ((bf16[8,128,384]{2,1,0:T(8,128)(2,1)}), bf16[8,128,384]{2,1,0:T(8,128)(2,1)S(1)}, u32[]{:S(2)}, u32[]{:S(2)}) async-start(bf16[8,128,384]{2,1,0:T(8,128)(2,1)} %flux_parts.1), calls=%async_computation.1 | async-start | bytes 1572864 | tf_op jit(solution)/shard_map/all_to_all | solution.py:683
  18.1 2.9 %copy-start.1 = (bf16[48,45,1440]{2,0,1:T(8,128)(2,1)S(1)}, bf16[48,45,1440]{2,0,1:T(8,128)(2,1)}, u32[]{:S(2)}) copy-start(bf16[48,45,1440]{2,0,1:T(8,128)(2,1)} %param.19) | copy-start | bytes 18662404
  30.3 24.8 %copy-start.4 = (bf16[8,128,384]{2,1,0:T(8,128)(2,1)}, bf16[8,128,384]{2,1,0:T(8,128)(2,1)S(1)}, u32[]{:S(2)}) copy-start(bf16[8,128,384]{2,1,0:T(8,128)(2,1)S(1)} %all-to-all-done.1.parts_ref) | copy-start | bytes 2359300
  30.3 14.6 %copy-start.19 = (bf16[76,1,7,7]{0,3,2,1:T(8,128)(2,1)S(1)}, bf16[76,1,7,7]{0,3,2,1:T(8,128)(2,1)}, u32[]{:S(2)}) copy-start(bf16[76,1,7,7]{0,3,2,1:T(8,128)(2,1)} %param.28) | copy-start | bytes 22348
  30.3 14.8 %copy-start.21 = (f32[76,4]{0,1:T(4,128)S(1)}, f32[76,4]{0,1:T(4,128)}, u32[]{:S(2)}) copy-start(f32[76,4]{0,1:T(4,128)} %param.25) | copy-start | bytes 3652
  30.3 41.5 %all-to-all-start = ((bf16[128,24,384]{2,1,0:T(8,128)(2,1)}), bf16[128,24,384]{2,1,0:T(8,128)(2,1)}, u32[]{:S(2)}, u32[]{:S(2)}) async-start(bf16[128,24,384]{2,1,0:T(8,128)(2,1)} %bitcast.40), calls=%async_computation | async-start | bytes 4718592 | tf_op jit(solution)/shard_map/all_to_all | solution.py:678
  39.3 11.6 %collective-permute-start = (bf16[23,8,76]{2,1,0:T(8,128)(2,1)S(1)}, bf16[23,8,76]{2,1,0:T(8,128)(2,1)S(1)}, u32[]{:S(2)}, u32[]{:S(2)}) collective-permute-start(bf16[23,8,76]{2,1,0:T(8,128)(2,1)S(1)} %get-tuple-element.18), channel_id=1, source_target_pairs={{0,1},{1,2},{2,3},{3,4},{4,5},{5,6},{6,7},{8,9},{9,10},{10,11},{11... | collective-permute-start | bytes 83912 | tf_op jit(solution)/shard_map/ppermute | solution.py:641
  43.0 12.2 %collective-permute-start.1 = (bf16[23,8,76]{2,1,0:T(8,128)(2,1)S(1)}, bf16[23,8,76]{2,1,0:T(8,128)(2,1)S(1)}, u32[]{:S(2)}, u32[]{:S(2)}) collective-permute-start(bf16[23,8,76]{2,1,0:T(8,128)(2,1)S(1)} %get-tuple-element.19), channel_id=1, source_target_pairs={{1,0},{2,1},{3,2},{4,3},{5,4},{6,5},{7,6},{9,8},{10,9},{11,10},{12... | collective-permute-start | bytes 83912 | tf_op jit(solution)/shard_map/ppermute | solution.py:641
  47.0 1.5 %copy-start.17 = (bf16[2,720,256]{2,1,0:T(8,128)(2,1)S(1)}, bf16[2,720,256]{2,1,0:T(8,128)(2,1)}, u32[]{:S(2)}) copy-start(bf16[2,720,256]{2,1,0:T(8,128)(2,1)} %param.22) | copy-start | bytes 2211844
  49.0 1.6 %copy-start.18 = (bf16[304,76]{0,1:T(8,128)(2,1)S(1)}, bf16[304,76]{0,1:T(8,128)(2,1)}, u32[]{:S(2)}) copy-start(bf16[304,76]{0,1:T(8,128)(2,1)} %param.30) | copy-start | bytes 138628
  49.1 1.7 %copy-start.22 = (f32[76]{0:T(128)S(1)}, f32[76]{0:T(128)}, u32[]{:S(2)}) copy-start(f32[76]{0:T(128)} %param.29) | copy-start | bytes 916
  49.1 1.9 %copy-start.20 = (s32[5,5]{1,0:T(8,128)S(1)}, s32[5,5]{1,0:T(8,128)}, u32[]{:S(2)}) copy-start(s32[5,5]{1,0:T(8,128)} %param.27) | copy-start | bytes 304
  49.1 6.1 %copy-start.7 = (bf16[16,384]{1,0:T(8,128)(2,1)S(1)}, bf16[16,384]{1,0:T(8,128)(2,1)}, u32[]{:S(2)}) copy-start(bf16[16,384]{1,0:T(8,128)(2,1)} %constant.29.clone.picks_ref) | copy-start | bytes 36868
  64.0 1.6 %copy-start.10 = (f32[23,76,384]{2,1,0:T(8,128)}, f32[23,76,384]{2,1,0:T(8,128)S(1)}, u32[]{:S(2)}) copy-start(f32[23,76,384]{2,1,0:T(8,128)S(1)} %get-tuple-element.25.forcing_ref) | copy-start | bytes 8054788
  67.8 12.2 %collective-permute-start.2 = (bf16[3,76,192]{2,1,0:T(8,128)(2,1)S(1)}, bf16[3,76,192]{2,1,0:T(8,128)(2,1)S(1)}, u32[]{:S(2)}, u32[]{:S(2)}) collective-permute-start(bf16[3,76,192]{2,1,0:T(8,128)(2,1)S(1)} %get-tuple-element.21), channel_id=1, source_target_pairs={{0,8},{8,16},{16,24},{24,32},{32,40},{40,48},{48,56},{56,64},{64,7... | collective-permute-start | bytes 262664 | tf_op jit(solution)/shard_map/ppermute | solution.py:641
  70.4 9.7 %collective-permute-start.3 = (bf16[3,76,192]{2,1,0:T(8,128)(2,1)S(1)}, bf16[3,76,192]{2,1,0:T(8,128)(2,1)S(1)}, u32[]{:S(2)}, u32[]{:S(2)}) collective-permute-start(bf16[3,76,192]{2,1,0:T(8,128)(2,1)S(1)} %get-tuple-element.20), channel_id=1, source_target_pairs={{8,0},{16,8},{24,16},{32,24},{40,32},{48,40},{56,48},{64,56},{72,6... | collective-permute-start | bytes 262664 | tf_op jit(solution)/shard_map/ppermute | solution.py:641
  80.1 21.8 %copy-start.16 = (bf16[76,304]{1,0:T(8,128)(2,1)S(1)}, bf16[76,304]{1,0:T(8,128)(2,1)}, u32[]{:S(2)}) copy-start(bf16[76,304]{1,0:T(8,128)(2,1)} %contract_ref.1) | copy-start | bytes 138628
  80.1 54.0 %all-to-all-start.2 = ((bf16[128,24,384]{2,1,0:T(8,128)(2,1)}), bf16[128,24,384]{2,1,0:T(8,128)(2,1)}, u32[]{:S(2)}, u32[]{:S(2)}) async-start(bf16[128,24,384]{2,1,0:T(8,128)(2,1)} %bitcast.46), calls=%async_computation.2 | async-start | bytes 4718592 | tf_op jit(solution)/shard_map/all_to_all | solution.py:678
  101.9 1.8 %copy-start.11 = (f32[23,76,384]{2,1,0:T(8,128)S(1)}, f32[23,76,384]{2,1,0:T(8,128)}, u32[]{:S(2)}) copy-start(f32[23,76,384]{2,1,0:T(8,128)} %copy-done.10) | copy-start | bytes 8054788
  (6 other events, 7.0 us)

commit v3 on v2

--- a/solution.py
+++ b/solution.py
@@ -64,15 +64,35 @@
     return dot(rows.astype(BF), first.astype(F32).astype(BF), (((0,), (0,)), ((), ())))
 
 
+def pieces_of(rows):
+    return [(0, BLOCK), (BLOCK, 3 * BLOCK), (4 * BLOCK, rows - 4 * BLOCK)]
+
+
+def copy_pieces(source, target, pieces, sems):
+    copies = {}
+    for k, (at, size) in enumerate(pieces):
+        span = pl.ds(at, size)
+        copies[at] = pltpu.make_async_copy(source.at[span], target.at[span], sems.at[k])
+        copies[at].start()
+    return copies
+
+
 def forward_kernel(
-    at_ref, x, sea_ref, gain_ref, table, swap_ref, out_ref, sea, held, out, out_sems, sems
+    at_ref, x_ref, sea_ref, gain_ref, table_ref, swap_ref, out_ref,
+    x, sea, table, held, out, x_sems, out_sems, sems
 ):
     rows, ch, lon = x.shape
     peers = held.shape[1]
     groups = row_groups(rows)
+    table_copy = pltpu.make_async_copy(table_ref, table, sems.at[1])
+    table_copy.start()
+    x_copies = copy_pieces(x_ref, x, pieces_of(rows), x_sems)
     sea_copy = pltpu.make_async_copy(sea_ref.at[:, pl.ds(0, 16), :], sea, sems.at[0])
     sea_copy.start()
+    table_copy.wait()
     for at, size in groups:
+        if at in x_copies:
+            x_copies[at].wait()
         y = dot(x[at : at + size].reshape(size * ch, lon), table[...]).astype(BF)
         for a in range(0, size, 2):
             pieces = []
@@ -89,7 +109,7 @@
     own = jnp.concatenate([own, jnp.zeros((ch - rows, own.shape[1]), F32)], axis=0)
     wide = pl.cdiv(lon, 128) * 128
     own = jnp.concatenate([own, jnp.zeros((ch, wide - own.shape[1]), F32)], axis=1)
-    own = pltpu.roll(own, at_ref[0], 1)[:, :lon].astype(BF)
+    own = pltpu.roll(own, at_ref[0] * sea.shape[2], 1)[:, :lon].astype(BF)
     y = dot(own, table[...]).astype(BF)
     pieces = [y[:, q * peers : (q + 1) * peers] for q in range(4)]
     pieces.append(column(gain_ref).astype(BF))
@@ -97,12 +117,16 @@
     held[HALF - 1] = jnp.concatenate(pieces, axis=0).T
 
     out_copies = []
+    half = peers * HALF // 2
     for b in range(peers // 16):
         part = held[:, b * 16 : (b + 1) * 16, :].reshape(HALF * 16, held.shape[2])
         span = pl.ds(b * 16 * HALF, 16 * HALF)
         out[span, :] = dot(swap_ref[...], part).astype(BF)
-        out_copies.append(pltpu.make_async_copy(out.at[span], out_ref.at[span], out_sems.at[b]))
-        out_copies[-1].start()
+        if (b + 1) * 16 * HALF % half == 0:
+            k = len(out_copies)
+            span = pl.ds(k * half, half)
+            out_copies.append(pltpu.make_async_copy(out.at[span], out_ref.at[span], out_sems.at[k]))
+            out_copies[-1].start()
     for copy in out_copies:
         copy.wait()
 
@@ -113,16 +137,19 @@
     return pl.pallas_call(
         forward_kernel,
         out_shape=pltpu.HBM((peers * HALF, 8 * ch), BF),
-        in_specs=[SMEM, VMEM, HBM, VMEM, VMEM, VMEM],
+        in_specs=[SMEM, ANY, ANY, VMEM, ANY, VMEM],
         out_specs=ANY,
         scratch_shapes=[
+            pltpu.VMEM(x.shape, BF),
             pltpu.VMEM((rows, 16, sea.shape[2]), BF),
+            pltpu.VMEM(table.shape, BF),
             pltpu.VMEM((HALF, peers, 8 * ch), BF),
             pltpu.VMEM((peers * HALF, 8 * ch), BF),
-            pltpu.SemaphoreType.DMA((peers // 16,)),
-            pltpu.SemaphoreType.DMA((1,)),
+            pltpu.SemaphoreType.DMA((3,)),
+            pltpu.SemaphoreType.DMA((2,)),
+            pltpu.SemaphoreType.DMA((2,)),
         ],
-        compiler_params=pltpu.CompilerParams(vmem_limit_bytes=24 << 20),
+        compiler_params=pltpu.CompilerParams(vmem_limit_bytes=58 << 20),
         cost_estimate=pl.CostEstimate(
             flops=2 * rows * ch * lon * peers * 4, bytes_accessed=14 << 20, transcendentals=0
         ),
@@ -150,18 +177,15 @@
         (analysis_hbm, analysis_ref), (spread_hbm, spread_ref), (mix_hbm, mix_ref), (synthesis_hbm, synthesis_ref)
     )
     tables = [pltpu.make_async_copy(a, b, in_sems.at[k]) for k, (a, b) in enumerate(pairs)]
-    wires = []
-    for j in range(groups):
-        span = pl.ds(j * size, size)
-        wires.append(pltpu.make_async_copy(wire_hbm.at[span], wire_ref.at[span], wire_sems.at[j]))
-    wires[0].start()
     tables[0].start()
-    for copy in wires[1:] + tables[1:]:
+    wires = copy_pieces(wire_hbm, wire_ref, [(0, 2 * size), (2 * size, (groups - 2) * size)], wire_sems)
+    for copy in tables[1:]:
         copy.start()
     tables[0].wait()
     lines = 0.0
     for j in range(groups):
-        wires[j].wait()
+        if j * size in wires:
+            wires[j * size].wait()
         turned = wire_ref[j * size : (j + 1) * size, :].T
         for m in range(2):
             total = sum(
@@ -208,10 +232,11 @@
             for m in range(2):
                 both = [mixed[m, k, j * ch : (j + 1) * ch, :] for k in range(2)]
                 pieces.append(dot(synthesis_ref[m, rh], jnp.concatenate(both, axis=0), NT).astype(BF))
-        span = pl.ds(j * size, size)
-        out[span, :] = jnp.concatenate(pieces, axis=1)
-        copies.append(pltpu.make_async_copy(out.at[span], out_ref.at[span], sems.at[j]))
-        copies[-1].start()
+        out[j * size : (j + 1) * size, :] = jnp.concatenate(pieces, axis=1)
+        if j % 4 == 3:
+            span = pl.ds((j - 3) * size, 4 * size)
+            copies.append(pltpu.make_async_copy(out.at[span], out_ref.at[span], sems.at[j // 4]))
+            copies[-1].start()
     for copy in copies:
         copy.wait()
 
@@ -248,27 +273,21 @@
     rows, ch, lon = x.shape
     peers = held.shape[1]
     groups = row_groups(rows)
-    wire_copies = []
-    for b in range(peers // 16):
-        span = pl.ds(b * 16 * HALF, 16 * HALF)
-        wire_copies.append(pltpu.make_async_copy(wire_ref.at[span], wire.at[span], wire_sems.at[b]))
-        wire_copies[-1].start()
+    turn = 16 * HALF
+    wires = copy_pieces(wire_ref, wire, [(0, 2 * turn), (2 * turn, peers * HALF - 2 * turn)], wire_sems)
     table_copy = pltpu.make_async_copy(table_ref, table, sems.at[0])
     table_copy.start()
-    x_copies = []
-    for g, (at, size) in enumerate(groups):
-        span = pl.ds(at, size)
-        x_copies.append(pltpu.make_async_copy(x_ref.at[span], x.at[span], x_sems.at[g]))
-        x_copies[-1].start()
+    x_copies = copy_pieces(x_ref, x, pieces_of(rows), x_sems)
     for b in range(peers // 16):
-        wire_copies[b].wait()
-        part = dot(swap_ref[...], wire[b * 16 * HALF : (b + 1) * 16 * HALF, :]).astype(BF)
+        if b * turn in wires:
+            wires[b * turn].wait()
+        part = dot(swap_ref[...], wire[b * turn : (b + 1) * turn, :]).astype(BF)
         held[:, b * 16 : (b + 1) * 16, :] = part.reshape(HALF, 16, held.shape[2])
-    chans, end, _ = parts_ref.shape
+    chans = parts_ref.shape[0]
     for half in range(2):
         lines[half] = jnp.concatenate(
             [
-                parts_ref[j, end - 32 :, half * PITCH : half * PITCH + lon // chans].astype(F32)
+                parts_ref[j, SURFACE:EDGES, half * PITCH : half * PITCH + lon // chans].astype(F32)
                 for j in range(chans)
             ],
             axis=1,
@@ -288,15 +307,17 @@
     out_copies = []
     wave = wave_of(*groups[0])
     for g, (at, size) in enumerate(groups):
-        x_copies[g].wait()
+        if at in x_copies:
+            x_copies[at].wait()
         later = wave_of(*groups[g + 1]) if g + 1 < len(groups) else None
         for a in range(size):
             line = lines[a % 2, (at + a) // 2 : (at + a) // 2 + 1, :]
             forced = x[at + a].astype(F32) + gain * line
             out[at + a] = (forced + wave[a * ch : (a + 1) * ch, :]).astype(BF)
-        span = pl.ds(at, size)
-        out_copies.append(pltpu.make_async_copy(out.at[span], out_ref.at[span], out_sems.at[g]))
-        out_copies[-1].start()
+        if g % 2 or g + 1 == len(groups):
+            span = pl.ds(BLOCK * (g - g % 2), at + size - BLOCK * (g - g % 2))
+            out_copies.append(pltpu.make_async_copy(out.at[span], out_ref.at[span], out_sems.at[g]))
+            out_copies[-1].start()
         wave = later
     for copy in out_copies:
         copy.wait()
@@ -317,7 +338,7 @@
             pltpu.VMEM((HALF, peers, 8 * ch), BF),
             pltpu.VMEM(x.shape, BF),
             pltpu.VMEM(x.shape, BF),
-            pltpu.VMEM((2, 32, lon), F32),
+            pltpu.VMEM((2, HALF, lon), F32),
             pltpu.SemaphoreType.DMA((peers // 16,)),
             pltpu.SemaphoreType.DMA((groups,)),
             pltpu.SemaphoreType.DMA((groups,)),
@@ -334,19 +355,61 @@
 PITCH = 192
 
 
-def flux_kernel(reach, x_ref, sea_ref, weight_ref, out_ref, x, sea, x_sems, sems):
+SURFACE = 4 * HALF
+EDGES = SURFACE + HALF
+PILE = 5
+
+
+def flux_kernel(reach, at_ref, x_ref, sea_ref, weight_ref, out_ref, x, sea, x_sems, sems):
     rows, ch, lon = x.shape
+    _, oc, cols = sea.shape
     peers = out_ref.shape[0]
     tile = lon // peers
     block = 8
-    groups = [(at, min(block, rows - at)) for at in range(0, rows, block)]
-    copies = []
-    for g, (at, size) in enumerate(groups):
+    x_copies = {}
+    for k, (at, size) in enumerate([(0, 2 * block), (2 * block, 2 * block), (4 * block, rows - 4 * block)]):
         span = pl.ds(at, size)
-        copies.append(pltpu.make_async_copy(x_ref.at[span], x.at[span], x_sems.at[g]))
-        copies[-1].start()
-    sea_copy = pltpu.make_async_copy(sea_ref.at[:, pl.ds(0, 16), :], sea, sems.at[0])
+        x_copies[at] = pltpu.make_async_copy(x_ref.at[span], x.at[span], x_sems.at[k])
+    sea_copy = pltpu.make_async_copy(sea_ref, sea, sems.at[0])
     sea_copy.start()
+    for copy in x_copies.values():
+        copy.start()
+
+    sea_copy.wait()
+    own = jnp.concatenate([sea[:, 0, :].astype(F32), jnp.zeros((ch - rows, tile), F32)], axis=0)
+    halves = []
+    for half in range(2):
+        pick = lax.broadcasted_iota(jnp.int32, (HALF, ch), 1) == (
+            2 * lax.broadcasted_iota(jnp.int32, (HALF, ch), 0) + half
+        )
+        halves.append(dot(pick.astype(F32).astype(BF), own.astype(BF)))
+        halves.append(jnp.zeros((HALF, PITCH - tile), F32))
+    own = jnp.concatenate(halves, axis=1)
+
+    row = lax.broadcasted_iota(jnp.int32, (16, cols), 0)
+    col = lax.broadcasted_iota(jnp.int32, (16, cols), 1)
+    want = jnp.where(row % 8 < 2 * reach, row % 8 % reach + row // 8 * (cols - reach), -1)
+    picks = [
+        ((col == want) & (row % 8 // reach == half)).astype(F32).astype(BF) for half in range(2)
+    ]
+    piles = [[], []]
+    for s in range(pl.cdiv(rows, 2)):
+        value = dot(picks[0], sea[2 * s], NT)
+        if 2 * s + 1 < rows:
+            value = value + dot(picks[1], sea[2 * s + 1], NT)
+        piles[0].append(value[:8])
+        piles[1].append(value[8:])
+    edges = []
+    for pile in piles:
+        pile = pile + [jnp.zeros((8, oc), F32)] * (-len(pile) % PILE)
+        wide = [jnp.concatenate(pile[k : k + PILE], axis=0) for k in range(0, len(pile), PILE)]
+        wide.append(jnp.zeros((8 * PILE, 2 * PITCH - oc * len(wide)), F32))
+        edges.append(jnp.concatenate(wide, axis=1))
+    no_edge = jnp.zeros_like(edges[0])
+    for j in range(peers):
+        edge = jnp.where(at_ref[0] == j + 1, edges[0], jnp.where(at_ref[0] == j - 1, edges[1], no_edge))
+        out_ref[j, SURFACE:, :] = jnp.concatenate([own, edge], axis=0).astype(BF)
+
     weight = weight_ref[...].astype(F32)
     weight = jnp.concatenate([weight] * block, axis=1)
     weight = jnp.concatenate([weight] * block, axis=0)
@@ -356,78 +419,34 @@
     weight = jnp.where(keep, weight, 0.0).astype(BF)
     before = jnp.zeros((4 * block, reach), F32)
     after = jnp.zeros((4 * block, PITCH - tile - reach), F32)
-    for g, (at, size) in enumerate(groups):
-        copies[g].wait()
+    for g, at in enumerate(range(0, rows, block)):
+        size = min(block, rows - at)
+        if at in x_copies:
+            x_copies[at].wait()
         y = dot(weight[:, : size * ch], x[at : at + size].reshape(size * ch, lon))
         y = jnp.concatenate([before, y, after], axis=1)
         for j in range(peers):
             part = y[:, tile * j : tile * j + PITCH]
             part = jnp.concatenate([part[: 2 * block], part[2 * block :]], axis=1)
             out_ref[j, 2 * block * g : 2 * block * (g + 1), :] = part.astype(BF)
-    sea_copy.wait()
-    own = jnp.concatenate([sea[:, 0, :].astype(F32), jnp.zeros((ch - rows, tile), F32)], axis=0)
-    halves = []
-    for half in range(2):
-        pick = lax.broadcasted_iota(jnp.int32, (32, ch), 1) == (
-            2 * lax.broadcasted_iota(jnp.int32, (32, ch), 0) + half
-        )
-        halves.append(dot(pick.astype(F32).astype(BF), own.astype(BF)))
-        halves.append(jnp.zeros((32, PITCH - tile), F32))
-    own = jnp.concatenate(halves, axis=1).astype(BF)
-    for j in range(peers):
-        out_ref[j, out_ref.shape[1] - 32 :, :] = own
-
-
-def flux_parts(x, sea, weight, reach, peers):
-    rows, ch, lon = x.shape
-    groups = pl.cdiv(rows, 8)
+
+
+def flux_parts(at, x, sea, weight, reach, peers):
     return pl.pallas_call(
         functools.partial(flux_kernel, reach),
-        out_shape=jax.ShapeDtypeStruct((peers, groups * 16 + 32, 2 * PITCH), BF),
-        in_specs=[HBM, HBM, VMEM],
+        out_shape=jax.ShapeDtypeStruct((peers, EDGES + 8 * PILE, 2 * PITCH), BF),
+        in_specs=[SMEM, ANY, ANY, VMEM],
         out_specs=VMEM,
         scratch_shapes=[
             pltpu.VMEM(x.shape, BF),
-            pltpu.VMEM((rows, 16, sea.shape[2]), BF),
-            pltpu.SemaphoreType.DMA((groups,)),
+            pltpu.VMEM(sea.shape, BF),
+            pltpu.SemaphoreType.DMA((3,)),
             pltpu.SemaphoreType.DMA((1,)),
         ],
-        compiler_params=pltpu.CompilerParams(vmem_limit_bytes=24 << 20),
+        compiler_params=pltpu.CompilerParams(vmem_limit_bytes=58 << 20),
         cost_estimate=pl.CostEstimate(flops=1 << 30, bytes_accessed=7 << 20, transcendentals=0),
         name="flux_parts",
-    )(x, sea, weight)
-
-
-def column_kernel(reach, center_ref, first_ref, last_ref):
-    rows, ch, cols = center_ref.shape
-    shape = (16, cols)
-    row = lax.broadcasted_iota(jnp.int32, shape, 0)
-    col = lax.broadcasted_iota(jnp.int32, shape, 1)
-    want = jnp.where(row % 8 < 2 * reach, row % 8 % reach + row // 8 * (cols - reach), -1)
-    picks = []
-    for half in range(2):
-        pick = (col == want) & (row % 8 // reach == half)
-        picks.append(pick.astype(F32).astype(BF))
-    for s in range((rows + 1) // 2):
-        value = dot(picks[0], center_ref[2 * s], NT)
-        if 2 * s + 1 < rows:
-            value = value + dot(picks[1], center_ref[2 * s + 1], NT)
-        first_ref[s] = value[:8].astype(BF)
-        last_ref[s] = value[8:].astype(BF)
-
-
-def edge_columns(center, reach):
-    rows, ch, _ = center.shape
-    out = jax.ShapeDtypeStruct(((rows + 1) // 2, 8, ch), BF)
-    return pl.pallas_call(
-        functools.partial(column_kernel, reach),
-        out_shape=(out, out),
-        in_specs=[VMEM],
-        out_specs=(VMEM, VMEM),
-        compiler_params=pltpu.CompilerParams(vmem_limit_bytes=16 << 20),
-        cost_estimate=pl.CostEstimate(flops=1 << 20, bytes_accessed=1 << 20, transcendentals=0),
-        name="edge_columns",
-    )(center)
+    )(at, x, sea, weight)
 
 
 def edge_picks(reach, span):
@@ -443,7 +462,7 @@
     high = flux.astype(BF).astype(F32)
     low = flux - high
     flux = jnp.concatenate([high, low, high, jnp.zeros_like(high)], axis=0).astype(BF)
-    edge = jnp.concatenate([left_ref[s].astype(F32), right_ref[s].astype(F32)], axis=0).astype(BF)
+    edge = jnp.concatenate([left_ref[s], right_ref[s]], axis=0).astype(BF)
     return dot(
         jnp.concatenate([edge, force], axis=0),
         jnp.concatenate([picks, flux], axis=0),
@@ -460,17 +479,24 @@
 
 
 def wet_kernel(
-    reach, center_ref, left_ref, right_ref, picks_ref, parts_ref, force_ref,
-    odd_ref, even_ref, forcing_ref, first_ref, last_ref, flux
+    reach, at_ref, center_ref, picks_ref, parts_ref, force_ref,
+    odd_ref, even_ref, forcing_ref, first_ref, last_ref, flux, left_ref, right_ref
 ):
-    rows = center_ref.shape[0]
+    rows, ch, _ = center_ref.shape
     own_pairs = odd_ref.shape[0]
+    peers = parts_ref.shape[0]
     picks, force = picks_ref[...], force_ref[...]
-    total = parts_ref[0].astype(F32)
-    for j in range(1, parts_ref.shape[0]):
-        total = total + parts_ref[j].astype(F32)
+    total = parts_ref[0, :SURFACE, :].astype(F32)
+    for j in range(1, peers):
+        total = total + parts_ref[j, :SURFACE, :].astype(F32)
+    at = at_ref[0]
+    left = parts_ref[jnp.maximum(at - 1, 0), EDGES:, :].astype(F32)
+    right = parts_ref[jnp.minimum(at + 1, peers - 1), EDGES:, :].astype(F32)
     for s in range(own_pairs):
         flux[s] = total[4 * s : 4 * s + 4, :]
+        span, lanes = slice(8 * (s % PILE), 8 * (s % PILE) + 8), slice(ch * (s // PILE), ch * (s // PILE) + ch)
+        left_ref[s] = left[span, lanes]
+        right_ref[s] = right[span, lanes]
 
     def fill(s, second):
         more = pair_forcing(s, left_ref, right_ref, picks, flux[s], force)
@@ -495,7 +521,7 @@
             ref[d] = odd_ref[(at + d) // 2][:, half * PITCH : (half + 1) * PITCH]
 
 
-def wet_rows(center, left, right, picks, parts, force, reach):
+def wet_rows(at, center, picks, parts, force, reach):
     rows, ch, _ = center.shape
     edge = jax.ShapeDtypeStruct((reach, ch, PITCH), BF)
     pairs = (rows + 1) // 2
@@ -503,13 +529,17 @@
     return pl.pallas_call(
         functools.partial(wet_kernel, reach),
         out_shape=(own, own, jax.ShapeDtypeStruct(own.shape, F32), edge, edge),
-        in_specs=[VMEM] * 6,
+        in_specs=[SMEM] + [VMEM] * 4,
         out_specs=(VMEM,) * 5,
-        scratch_shapes=[pltpu.VMEM((pairs, 4, 2 * PITCH), F32)],
+        scratch_shapes=[
+            pltpu.VMEM((pairs, 4, 2 * PITCH), F32),
+            pltpu.VMEM((pairs, 8, ch), F32),
+            pltpu.VMEM((pairs, 8, ch), F32),
+        ],
         compiler_params=pltpu.CompilerParams(vmem_limit_bytes=24 << 20),
         cost_estimate=pl.CostEstimate(flops=1 << 20, bytes_accessed=1 << 20, transcendentals=0),
         name="wet_rows",
-    )(center, left, right, picks, parts, force)
+    )(at, center, picks, parts, force)
 
 
 def ocean_kernel(
@@ -679,23 +709,22 @@
             wire.reshape(peers, HALF, 8 * ch), ("chan", "lat"), 0, 0, tiled=True
         ).reshape(wire.shape)
 
-    parts = flux_parts(x, sea, surface_flux_weight, reach, chan_parts)
+    at = jnp.reshape(chan_at, (1,)).astype(jnp.int32)
+    parts = flux_parts(at, x, sea, surface_flux_weight, reach, chan_parts)
     parts = lax.all_to_all(parts, "chan", 0, 0, tiled=True)
 
     gain = sea_temp_gain[None]
-    at = jnp.reshape(chan_at * cols, (1,)).astype(jnp.int32)
     wire = forward(at, x, sea, gain, table_fwd, swap_out)
     gathered = exchange(wire)
     sea, legendre_analysis, legendre_synthesis, wire = lax.optimization_barrier(
         (sea, legendre_analysis, legendre_synthesis, wire)
     )
-    left, right = shift(*edge_columns(sea, reach), "chan")
     force = flux_ocean_forcing.T
     force_high = force.astype(BF)
     force_low = (force - force_high.astype(F32)).astype(BF)
     force = jnp.concatenate([force_high, force_high, force_low, jnp.zeros_like(force_low)], axis=0)
     picks = jnp.asarray(edge_picks(reach, cols + 2 * reach))
-    odd, even, forcing, first, last = wet_rows(sea, left, right, picks, parts, force, reach)
+    odd, even, forcing, first, last = wet_rows(at, sea, picks, parts, force, reach)
     low, high = shift(first, last, "lat")
 
     def banded(table):

time: 149 us -> 128 us (0.86)
  starting transfers between devices: 46.6 us -> 25 us
  local copies, waits for them, and re-layouts: 23.4 us -> 13 us
  waiting for transfers between devices: 11.6 us -> 20.6 us
  Pallas kernels: 65.6 us -> 67.7 us
    all_to_all x2, starting transfers between devices: 30.1 us -> 13.4 us  [exchange(): lax.all_to_all(wire.reshape(peers, HALF, 8 * ch), ('chan', 'lat'), 0, 0,...]
    all_to_all x2, waiting for transfers between devices: 5.84 us -> 16.1 us  [exchange(): lax.all_to_all(wire.reshape(peers, HALF, 8 * ch), ('chan', 'lat'), 0, 0,...]
    unnamed x49 -> x37, local copies, waits for them, and re-layouts: 18 us -> 8.7 us
    ppermute x4 -> x2, starting transfers between devices: 9.6 us -> 4.76 us  [shift(): return (lax.ppermute(last, axis, up), lax.ppermute(first, axis, down))]
    ppermute x4 -> x2, waiting for transfers between devices: 4.23 us -> 0.01 us  [shift(): return (lax.ppermute(last, axis, up), lax.ppermute(first, axis, down))]
    pallas_call x1, Pallas kernels: 6.47 us -> 9.96 us  [forward(): pl.pallas_call(forward_kernel, out_shape=pltpu.HBM((peers * HALF, 8 * ch)...]
    all_to_all x1, waiting for transfers between devices: 1.54 us -> 4.43 us  [body(): parts = lax.all_to_all(parts, 'chan', 0, 0, tiled=True)]
    pallas_call x1, Pallas kernels: 14.1 us -> 11.9 us  [inverse(): pl.pallas_call(inverse_kernel, out_shape=pltpu.HBM(x.shape, BF), in_specs...]
  transfers between devices with their start and end apart: 7 -> 5, of which waited for: 3 -> 3; matrix products, arithmetic and copies ran while one was open for 4% -> 4% of each run, Pallas kernels for 31% -> 38%
where the time goes in v3:
time: 128 us; the launch traced here: 127 us
  Pallas kernels  67.7 us (53%)
  starting transfers between devices  25 us (20%)
  waiting for transfers between devices  20.6 us (16%)
  local copies, waits for them, and re-layouts  13 us (10%)
    pallas_call x1, Pallas kernels, ocean_block(): pl.pallas_call(functools.partial(ocean_kernel, reach, mask_tiles), out_sh...  21.9 us
    all_to_all x2, waiting for transfers between devices, exchange(): lax.all_to_all(wire.reshape(peers, HALF, 8 * ch), ('chan', 'lat'), 0, 0,...  16.1 us
    all_to_all x2, starting transfers between devices, exchange(): lax.all_to_all(wire.reshape(peers, HALF, 8 * ch), ('chan', 'lat'), 0, 0,...  13.4 us
    pallas_call x1, Pallas kernels, inverse(): pl.pallas_call(inverse_kernel, out_shape=pltpu.HBM(x.shape, BF), in_specs...  11.9 us
    pallas_call x1, Pallas kernels, forward(): pl.pallas_call(forward_kernel, out_shape=pltpu.HBM((peers * HALF, 8 * ch)...  9.96 us
    pallas_call x1, Pallas kernels, wet_rows(): pl.pallas_call(functools.partial(wet_kernel, reach), out_shape=(own, own,...  9.03 us
    unnamed x37, local copies, waits for them, and re-layouts  8.7 us
    pallas_call x1, Pallas kernels, spectral(): pl.pallas_call(spectral_kernel, out_shape=pltpu.HBM(wire.shape, BF), in_s...  7.66 us
  transfers between devices with their start and end apart: 5, of which 3 were waited for; matrix products, arithmetic and copies ran while one was open for 4% of the time, Pallas kernels for 38%

profile of v3, /device:TPU:1, one launch (start us, length us, event | category | flops | bytes accessed | tf_op | source)
XLA Modules:
  0.0 127.3 jit_solution(10361231374928851940)
XLA Ops:
  0.6 7.2 %flux_parts.1 = bf16[8,160,384]{2,1,0:T(8,128)(2,1)} custom-call(s32[1]{0:T(128)} %bitcast.at_ref, bf16[45,48,1440]{2,1,0:T(8,128)(2,1)} %bitcast.34, bf16[45,76,180]{2,1,0:T(8,128)(2,1)} %bitcast.30, bf16[4,48]{1,0:T(4,128)(2,1)} %weight_ref.1), custom_call_target="tpu_custom_call" | custom-call | flops 1073741824 | bytes 7340032 | tf_op jit(solution)/shard_map/flux_parts/pallas_call | solution.py:435
  7.9 6.8 %all-to-all-start.1 = ((bf16[8,160,384]{2,1,0:T(8,128)(2,1)}), bf16[8,160,384]{2,1,0:T(8,128)(2,1)S(1)}, u32[]{:S(2)}, u32[]{:S(2)}) async-start(bf16[8,160,384]{2,1,0:T(8,128)(2,1)} %flux_parts.1), calls=%async_computation.1 | async-start | bytes 1966080 | tf_op jit(solution)/shard_map/all_to_all | solution.py:714
  14.7 10.0 %dft_forward.1 = bf16[3072,384]{1,0:T(8,128)(2,1)} custom-call(s32[1]{0:T(128)} %bitcast.at_ref, bf16[45,48,1440]{2,1,0:T(8,128)(2,1)} %bitcast.35, bf16[45,76,180]{2,1,0:T(8,128)(2,1)} %bitcast.31, bf16[1,48]{1,0:T(2,128)(2,1)} %bitcast.47, bf16[1440,512]{1,0:T(8,128)(2,1)} %constant.23.clone.table_ref, bf16[384,384]{1,0:T(8,128)(2,1)} %constant.25.clone.swap_ref), custom_call_target="tpu_custom_call" | custom-call | flops 3185049600 | bytes 14680064 | tf_op jit(solution)/shard_map/dft_forward/pallas_call | solution.py:137
  24.7 4.4 %all-to-all-done.1.parts_ref = bf16[8,160,384]{2,1,0:T(8,128)(2,1)S(1)} async-done(((bf16[8,160,384]{2,1,0:T(8,128)(2,1)}), bf16[8,160,384]{2,1,0:T(8,128)(2,1)S(1)}, u32[]{:S(2)}, u32[]{:S(2)}) %all-to-all-start.1) | async-done | bytes 983072 | tf_op jit(solution)/shard_map/all_to_all | solution.py:714
  29.1 8.4 %all-to-all-start = ((bf16[128,24,384]{2,1,0:T(8,128)(2,1)}), bf16[128,24,384]{2,1,0:T(8,128)(2,1)}, u32[]{:S(2)}, u32[]{:S(2)}) async-start(bf16[128,24,384]{2,1,0:T(8,128)(2,1)} %bitcast.37), calls=%async_computation | async-start | bytes 4718592 | tf_op jit(solution)/shard_map/all_to_all | solution.py:708
  37.5 0.6 copy.24
  38.3 1.3 %copy.26 = bf16[2,2,16,24,256]{4,3,2,1,0:T(8,128)(2,1)} copy(bf16[2,2,16,24,256]{4,2,1,3,0:T(8,128)(2,1)S(1)} %bitcast.39) | data formatting | bytes 1572864 | tf_op jit(solution)/shard_map/transpose | solution.py:733
  39.6 0.6 copy.27
  40.4 1.4 %copy.29 = bf16[2,2,16,24,256]{4,3,2,1,0:T(8,128)(2,1)} copy(bf16[2,2,16,24,256]{4,2,1,3,0:T(8,128)(2,1)S(1)} %bitcast.40) | data formatting | bytes 1572864 | tf_op jit(solution)/shard_map/transpose | solution.py:733
  42.4 9.0 %wet_rows.1 = (bf16[23,76,384]{2,1,0:T(8,128)(2,1)S(1)}, bf16[23,76,384]{2,1,0:T(8,128)(2,1)S(1)}, f32[23,76,384]{2,1,0:T(8,128)S(1)}, bf16[3,76,192]{2,1,0:T(8,128)(2,1)S(1)}, bf16[3,76,192]{2,1,0:T(8,128)(2,1)S(1)}) custom-call(s32[1]{0:T(128)} %bitcast.at_ref, bf16[45,76,180]{2,1,0:T(8,128)(2,1)S(1)} %bitcast.32, bf16[16,384]{1,0:T(8,128)(2,1)S(1)} %copy-done.2, ...), custom_call_target="tpu_custom_call" | custom-call | flops 1048576 | bytes 1048576 | tf_op jit(solution)/shard_map/wet_rows/pallas_call | solution.py:529
  51.5 1.5 %copy-done.3 = f32[23,76,384]{2,1,0:T(8,128)} copy-done((f32[23,76,384]{2,1,0:T(8,128)}, f32[23,76,384]{2,1,0:T(8,128)S(1)}, u32[]{:S(2)}) %copy-start.3) | copy-done | bytes 2684952
  53.0 1.1 copy-done.5
  54.1 1.1 copy-done.7
  55.3 3.3 %collective-permute-start = (bf16[3,76,192]{2,1,0:T(8,128)(2,1)S(1)}, bf16[3,76,192]{2,1,0:T(8,128)(2,1)S(1)}, u32[]{:S(2)}, u32[]{:S(2)}) collective-permute-start(bf16[3,76,192]{2,1,0:T(8,128)(2,1)S(1)} %get-tuple-element.17), channel_id=1, source_target_pairs={{0,8},{8,16},{16,24},{24,32},{32,40},{40,48},{48,56},{56,64},{64,7... | collective-permute-start | bytes 262664 | tf_op jit(solution)/shard_map/ppermute | solution.py:671
  58.5 1.5 %collective-permute-start.1 = (bf16[3,76,192]{2,1,0:T(8,128)(2,1)S(1)}, bf16[3,76,192]{2,1,0:T(8,128)(2,1)S(1)}, u32[]{:S(2)}, u32[]{:S(2)}) collective-permute-start(bf16[3,76,192]{2,1,0:T(8,128)(2,1)S(1)} %get-tuple-element.16), channel_id=1, source_target_pairs={{8,0},{16,8},{24,16},{32,24},{40,32},{48,40},{56,48},{64,56},{72,6... | collective-permute-start | bytes 262664 | tf_op jit(solution)/shard_map/ppermute | solution.py:671
  60.0 10.2 %all-to-all-done = bf16[128,24,384]{2,1,0:T(8,128)(2,1)} async-done(((bf16[128,24,384]{2,1,0:T(8,128)(2,1)}), bf16[128,24,384]{2,1,0:T(8,128)(2,1)}, u32[]{:S(2)}, u32[]{:S(2)}) %all-to-all-start) | async-done | bytes 2359328 | tf_op jit(solution)/shard_map/all_to_all | solution.py:708
  70.2 7.7 %spectral.1 = bf16[3072,384]{1,0:T(8,128)(2,1)} custom-call(bf16[3072,384]{1,0:T(8,128)(2,1)} %bitcast.5.wire_hbm, bf16[2,2,384,256]{3,2,1,0:T(8,128)(2,1)} %bitcast.44, bf16[2,2,384,256]{3,2,1,0:T(8,128)(2,1)} %bitcast.45, bf16[2,384,384]{2,1,0:T(8,128)(2,1)} %mix_hbm.1, bf16[384,384]{1,0:T(8,128)(2,1)} %constant.28.clone.spread_hbm), custom_call_target="tpu_custom_call" | custom-call | flops 2147483648 | bytes 9437184 | tf_op jit(solution)/shard_map/spectral/pallas_call | solution.py:248
  77.9 5.0 %all-to-all-start.2 = ((bf16[128,24,384]{2,1,0:T(8,128)(2,1)}), bf16[128,24,384]{2,1,0:T(8,128)(2,1)}, u32[]{:S(2)}, u32[]{:S(2)}) async-start(bf16[128,24,384]{2,1,0:T(8,128)(2,1)} %bitcast.43), calls=%async_computation.2 | async-start | bytes 4718592 | tf_op jit(solution)/shard_map/all_to_all | solution.py:708
  82.9 1.8 %copy-done.4 = f32[23,76,384]{2,1,0:T(8,128)S(1)} copy-done((f32[23,76,384]{2,1,0:T(8,128)S(1)}, f32[23,76,384]{2,1,0:T(8,128)}, u32[]{:S(2)}) %copy-start.4) | copy-done | bytes 2684952
  84.7 1.4 %copy-done.6 = bf16[23,76,384]{2,1,0:T(8,128)(2,1)S(1)} copy-done((bf16[23,76,384]{2,1,0:T(8,128)(2,1)S(1)}, bf16[23,76,384]{2,1,0:T(8,128)(2,1)}, u32[]{:S(2)}) %copy-start.6) | copy-done | bytes 1342488
  86.1 1.4 %copy-done.8 = bf16[23,76,384]{2,1,0:T(8,128)(2,1)S(1)} copy-done((bf16[23,76,384]{2,1,0:T(8,128)(2,1)S(1)}, bf16[23,76,384]{2,1,0:T(8,128)(2,1)}, u32[]{:S(2)}) %copy-start.8) | copy-done | bytes 1342488
  87.4 21.9 %ocean_block.1 = bf16[45,76,180]{2,1,0:T(8,128)(2,1)} custom-call(bf16[45,76,180]{2,1,0:T(8,128)(2,1)S(1)} %bitcast.33, f32[23,76,384]{2,1,0:T(8,128)S(1)} %copy-done.4, bf16[23,76,384]{2,1,0:T(8,128)(2,1)S(1)} %copy-done.6, bf16[23,76,384]{2,1,0:T(8,128)(2,1)S(1)} %copy-done.8, bf16[3,76,192]{2,1,0:T(8,128)(2,1)S(1)} %collective-permute-done.low_ref, ...), custom_call_target="tpu_custom_call" | custom-call | flops 32212254720 | bytes 8388608 | tf_op jit(solution)/shard_map/ocean_block/pallas_call | solution.py:641
  109.3 6.0 %all-to-all-done.2 = bf16[128,24,384]{2,1,0:T(8,128)(2,1)} async-done(((bf16[128,24,384]{2,1,0:T(8,128)(2,1)}), bf16[128,24,384]{2,1,0:T(8,128)(2,1)}, u32[]{:S(2)}, u32[]{:S(2)}) %all-to-all-start.2) | async-done | bytes 2359328 | tf_op jit(solution)/shard_map/all_to_all | solution.py:708
  115.3 11.9 %dft_inverse.1 = bf16[45,48,1440]{2,1,0:T(8,128)(2,1)} custom-call(bf16[3072,384]{1,0:T(8,128)(2,1)} %bitcast.17.wire_ref, bf16[512,1440]{1,0:T(8,128)(2,1)} %constant.24.clone.table_ref, bf16[384,384]{1,0:T(8,128)(2,1)} %constant.26.clone.swap_ref, bf16[45,48,1440]{2,1,0:T(8,128)(2,1)} %bitcast.36, bf16[1,48]{1,0:T(2,128)(2,1)} %bitcast.48, ...), custom_call_target="tpu_custom_call" | custom-call | flops 3185049600 | bytes 20971520 | tf_op jit(solution)/shard_map/dft_inverse/pallas_call | solution.py:330
  (44 shorter events, 1.0 us)
Async XLA Ops:
  7.9 21.2 %all-to-all-start.1 = ((bf16[8,160,384]{2,1,0:T(8,128)(2,1)}), bf16[8,160,384]{2,1,0:T(8,128)(2,1)S(1)}, u32[]{:S(2)}, u32[]{:S(2)}) async-start(bf16[8,160,384]{2,1,0:T(8,128)(2,1)} %flux_parts.1), calls=%async_computation.1 | async-start | bytes 1966080 | tf_op jit(solution)/shard_map/all_to_all | solution.py:714
  29.1 13.3 %copy-start.1 = (bf16[8,160,384]{2,1,0:T(8,128)(2,1)}, bf16[8,160,384]{2,1,0:T(8,128)(2,1)S(1)}, u32[]{:S(2)}) copy-start(bf16[8,160,384]{2,1,0:T(8,128)(2,1)S(1)} %all-to-all-done.1.parts_ref) | copy-start | bytes 2949124
  29.1 8.4 %copy-start.10 = (bf16[2,256,720]{1,2,0:T(8,128)(2,1)S(1)}, bf16[2,256,720]{1,2,0:T(8,128)(2,1)}, u32[]{:S(2)}) copy-start(bf16[2,256,720]{1,2,0:T(8,128)(2,1)} %param.21) | copy-start | bytes 2211844
  29.1 41.1 %all-to-all-start = ((bf16[128,24,384]{2,1,0:T(8,128)(2,1)}), bf16[128,24,384]{2,1,0:T(8,128)(2,1)}, u32[]{:S(2)}, u32[]{:S(2)}) async-start(bf16[128,24,384]{2,1,0:T(8,128)(2,1)} %bitcast.37), calls=%async_computation | async-start | bytes 4718592 | tf_op jit(solution)/shard_map/all_to_all | solution.py:708
  38.1 1.5 %copy-start.11 = (bf16[2,720,256]{2,1,0:T(8,128)(2,1)S(1)}, bf16[2,720,256]{2,1,0:T(8,128)(2,1)}, u32[]{:S(2)}) copy-start(bf16[2,720,256]{2,1,0:T(8,128)(2,1)} %param.22) | copy-start | bytes 2211844
  40.2 1.6 %copy-start.12 = (bf16[304,76]{0,1:T(8,128)(2,1)S(1)}, bf16[304,76]{0,1:T(8,128)(2,1)}, u32[]{:S(2)}) copy-start(bf16[304,76]{0,1:T(8,128)(2,1)} %param.30) | copy-start | bytes 138628
  40.2 1.8 %copy-start.13 = (bf16[76,1,7,7]{0,3,2,1:T(8,128)(2,1)S(1)}, bf16[76,1,7,7]{0,3,2,1:T(8,128)(2,1)}, u32[]{:S(2)}) copy-start(bf16[76,1,7,7]{0,3,2,1:T(8,128)(2,1)} %param.28) | copy-start | bytes 22348
  40.2 1.9 %copy-start.16 = (f32[76]{0:T(128)S(1)}, f32[76]{0:T(128)}, u32[]{:S(2)}) copy-start(f32[76]{0:T(128)} %param.29) | copy-start | bytes 916
  40.2 2.1 %copy-start.14 = (s32[5,5]{1,0:T(8,128)S(1)}, s32[5,5]{1,0:T(8,128)}, u32[]{:S(2)}) copy-start(s32[5,5]{1,0:T(8,128)} %param.27) | copy-start | bytes 304
  40.2 2.1 %copy-start.15 = (f32[76,4]{0,1:T(4,128)S(1)}, f32[76,4]{0,1:T(4,128)}, u32[]{:S(2)}) copy-start(f32[76,4]{0,1:T(4,128)} %param.25) | copy-start | bytes 3652
  40.2 2.2 %copy-start = (bf16[76,45,180]{2,0,1:T(8,128)(2,1)S(1)}, bf16[76,45,180]{2,0,1:T(8,128)(2,1)}, u32[]{:S(2)}) copy-start(bf16[76,45,180]{2,0,1:T(8,128)(2,1)} %param.26) | copy-start | bytes 3693604
  40.3 2.2 %copy-start.2 = (bf16[16,384]{1,0:T(8,128)(2,1)S(1)}, bf16[16,384]{1,0:T(8,128)(2,1)}, u32[]{:S(2)}) copy-start(bf16[16,384]{1,0:T(8,128)(2,1)} %constant.27.clone.picks_ref) | copy-start | bytes 36868
  51.5 1.6 %copy-start.3 = (f32[23,76,384]{2,1,0:T(8,128)}, f32[23,76,384]{2,1,0:T(8,128)S(1)}, u32[]{:S(2)}) copy-start(f32[23,76,384]{2,1,0:T(8,128)S(1)} %get-tuple-element.21.forcing_ref) | copy-start | bytes 8054788
  53.0 1.1 copy-start.5
  54.1 1.1 copy-start.7
  55.3 22.6 %collective-permute-start = (bf16[3,76,192]{2,1,0:T(8,128)(2,1)S(1)}, bf16[3,76,192]{2,1,0:T(8,128)(2,1)S(1)}, u32[]{:S(2)}, u32[]{:S(2)}) collective-permute-start(bf16[3,76,192]{2,1,0:T(8,128)(2,1)S(1)} %get-tuple-element.17), channel_id=1, source_target_pairs={{0,8},{8,16},{16,24},{24,32},{32,40},{40,48},{48,56},{56,64},{64,7... | collective-permute-start | bytes 262664 | tf_op jit(solution)/shard_map/ppermute | solution.py:671
  58.5 19.3 %collective-permute-start.1 = (bf16[3,76,192]{2,1,0:T(8,128)(2,1)S(1)}, bf16[3,76,192]{2,1,0:T(8,128)(2,1)S(1)}, u32[]{:S(2)}, u32[]{:S(2)}) collective-permute-start(bf16[3,76,192]{2,1,0:T(8,128)(2,1)S(1)} %get-tuple-element.16), channel_id=1, source_target_pairs={{8,0},{16,8},{24,16},{32,24},{40,32},{48,40},{56,48},{64,56},{72,6... | collective-permute-start | bytes 262664 | tf_op jit(solution)/shard_map/ppermute | solution.py:671
  77.9 5.0 %copy-start.9 = (bf16[76,304]{1,0:T(8,128)(2,1)S(1)}, bf16[76,304]{1,0:T(8,128)(2,1)}, u32[]{:S(2)}) copy-start(bf16[76,304]{1,0:T(8,128)(2,1)} %contract_ref.1) | copy-start | bytes 138628
  77.9 37.4 %all-to-all-start.2 = ((bf16[128,24,384]{2,1,0:T(8,128)(2,1)}), bf16[128,24,384]{2,1,0:T(8,128)(2,1)}, u32[]{:S(2)}, u32[]{:S(2)}) async-start(bf16[128,24,384]{2,1,0:T(8,128)(2,1)} %bitcast.43), calls=%async_computation.2 | async-start | bytes 4718592 | tf_op jit(solution)/shard_map/all_to_all | solution.py:708
  82.9 1.8 %copy-start.4 = (f32[23,76,384]{2,1,0:T(8,128)S(1)}, f32[23,76,384]{2,1,0:T(8,128)}, u32[]{:S(2)}) copy-start(f32[23,76,384]{2,1,0:T(8,128)} %copy-done.3) | copy-start | bytes 8054788
  84.7 1.4 %copy-start.6 = (bf16[23,76,384]{2,1,0:T(8,128)(2,1)S(1)}, bf16[23,76,384]{2,1,0:T(8,128)(2,1)}, u32[]{:S(2)}) copy-start(bf16[23,76,384]{2,1,0:T(8,128)(2,1)} %copy-done.5) | copy-start | bytes 4027396
  86.1 1.4 %copy-start.8 = (bf16[23,76,384]{2,1,0:T(8,128)(2,1)S(1)}, bf16[23,76,384]{2,1,0:T(8,128)(2,1)}, u32[]{:S(2)}) copy-start(bf16[23,76,384]{2,1,0:T(8,128)(2,1)} %copy-done.7) | copy-start | bytes 4027396

commit v4 on v3

--- a/solution.py
+++ b/solution.py
@@ -178,7 +178,7 @@
     )
     tables = [pltpu.make_async_copy(a, b, in_sems.at[k]) for k, (a, b) in enumerate(pairs)]
     tables[0].start()
-    wires = copy_pieces(wire_hbm, wire_ref, [(0, 2 * size), (2 * size, (groups - 2) * size)], wire_sems)
+    wires = copy_pieces(wire_hbm, wire_ref, [(0, size), (size, 3 * size), (4 * size, (groups - 4) * size)], wire_sems)
     for copy in tables[1:]:
         copy.start()
     tables[0].wait()
@@ -233,9 +233,9 @@
                 both = [mixed[m, k, j * ch : (j + 1) * ch, :] for k in range(2)]
                 pieces.append(dot(synthesis_ref[m, rh], jnp.concatenate(both, axis=0), NT).astype(BF))
         out[j * size : (j + 1) * size, :] = jnp.concatenate(pieces, axis=1)
-        if j % 4 == 3:
-            span = pl.ds((j - 3) * size, 4 * size)
-            copies.append(pltpu.make_async_copy(out.at[span], out_ref.at[span], sems.at[j // 4]))
+        if j % 2:
+            span = pl.ds((j - 1) * size, 2 * size)
+            copies.append(pltpu.make_async_copy(out.at[span], out_ref.at[span], sems.at[j // 2]))
             copies[-1].start()
     for copy in copies:
         copy.wait()
@@ -277,7 +277,7 @@
     wires = copy_pieces(wire_ref, wire, [(0, 2 * turn), (2 * turn, peers * HALF - 2 * turn)], wire_sems)
     table_copy = pltpu.make_async_copy(table_ref, table, sems.at[0])
     table_copy.start()
-    x_copies = copy_pieces(x_ref, x, pieces_of(rows), x_sems)
+    x_copies = copy_pieces(x_ref, x, [(0, rows)], x_sems)
     for b in range(peers // 16):
         if b * turn in wires:
             wires[b * turn].wait()
@@ -285,13 +285,9 @@
         held[:, b * 16 : (b + 1) * 16, :] = part.reshape(HALF, 16, held.shape[2])
     chans = parts_ref.shape[0]
     for half in range(2):
-        lines[half] = jnp.concatenate(
-            [
-                parts_ref[j, SURFACE:EDGES, half * PITCH : half * PITCH + lon // chans].astype(F32)
-                for j in range(chans)
-            ],
-            axis=1,
-        )
+        parts = [parts_ref[j, 80:128, :].astype(F32)[SURFACE - 80 : EDGES - 80] for j in range(chans)]
+        at = half * PITCH
+        lines[half] = jnp.concatenate([part[:, at : at + lon // chans] for part in parts], axis=1)
     gain = column(gain_ref)[:, :1]
     table_copy.wait()
 
@@ -355,93 +351,116 @@
 PITCH = 192
 
 
-SURFACE = 4 * HALF
+SURFACE = 92
 EDGES = SURFACE + HALF
-PILE = 5
-
-
-def flux_kernel(reach, at_ref, x_ref, sea_ref, weight_ref, out_ref, x, sea, x_sems, sems):
+PILE = 9
+
+
+def flux_kernel(
+    reach, at_ref, x_ref, sea_ref, weight_ref, parts_ref, x, sea, out_ref, x_sems, sems
+):
     rows, ch, lon = x.shape
     _, oc, cols = sea.shape
     peers = out_ref.shape[0]
     tile = lon // peers
-    block = 8
+    block = 16
     x_copies = {}
-    for k, (at, size) in enumerate([(0, 2 * block), (2 * block, 2 * block), (4 * block, rows - 4 * block)]):
+    for k, (at, size) in enumerate([(0, block), (block, block), (2 * block, rows - 2 * block)]):
         span = pl.ds(at, size)
         x_copies[at] = pltpu.make_async_copy(x_ref.at[span], x.at[span], x_sems.at[k])
     sea_copy = pltpu.make_async_copy(sea_ref, sea, sems.at[0])
+    x_copies[0].start()
     sea_copy.start()
-    for copy in x_copies.values():
-        copy.start()
-
-    sea_copy.wait()
-    own = jnp.concatenate([sea[:, 0, :].astype(F32), jnp.zeros((ch - rows, tile), F32)], axis=0)
-    halves = []
-    for half in range(2):
-        pick = lax.broadcasted_iota(jnp.int32, (HALF, ch), 1) == (
-            2 * lax.broadcasted_iota(jnp.int32, (HALF, ch), 0) + half
-        )
-        halves.append(dot(pick.astype(F32).astype(BF), own.astype(BF)))
-        halves.append(jnp.zeros((HALF, PITCH - tile), F32))
-    own = jnp.concatenate(halves, axis=1)
-
-    row = lax.broadcasted_iota(jnp.int32, (16, cols), 0)
-    col = lax.broadcasted_iota(jnp.int32, (16, cols), 1)
-    want = jnp.where(row % 8 < 2 * reach, row % 8 % reach + row // 8 * (cols - reach), -1)
-    picks = [
-        ((col == want) & (row % 8 // reach == half)).astype(F32).astype(BF) for half in range(2)
-    ]
-    piles = [[], []]
-    for s in range(pl.cdiv(rows, 2)):
-        value = dot(picks[0], sea[2 * s], NT)
-        if 2 * s + 1 < rows:
-            value = value + dot(picks[1], sea[2 * s + 1], NT)
-        piles[0].append(value[:8])
-        piles[1].append(value[8:])
-    edges = []
-    for pile in piles:
-        pile = pile + [jnp.zeros((8, oc), F32)] * (-len(pile) % PILE)
-        wide = [jnp.concatenate(pile[k : k + PILE], axis=0) for k in range(0, len(pile), PILE)]
-        wide.append(jnp.zeros((8 * PILE, 2 * PITCH - oc * len(wide)), F32))
-        edges.append(jnp.concatenate(wide, axis=1))
-    no_edge = jnp.zeros_like(edges[0])
-    for j in range(peers):
-        edge = jnp.where(at_ref[0] == j + 1, edges[0], jnp.where(at_ref[0] == j - 1, edges[1], no_edge))
-        out_ref[j, SURFACE:, :] = jnp.concatenate([own, edge], axis=0).astype(BF)
+    x_copies[block].start()
+    x_copies[2 * block].start()
+
+    def columns():
+        sea_copy.wait()
+        own = jnp.concatenate([sea[:, 0, :].astype(F32), jnp.zeros((ch - rows, tile), F32)], axis=0)
+        halves = []
+        for half in range(2):
+            pick = lax.broadcasted_iota(jnp.int32, (HALF, ch), 1) == (
+                2 * lax.broadcasted_iota(jnp.int32, (HALF, ch), 0) + half
+            )
+            halves.append(dot(pick.astype(F32).astype(BF), own.astype(BF)))
+            halves.append(jnp.zeros((HALF, PITCH - tile), F32))
+        own = jnp.concatenate(halves, axis=1)
+
+        row = lax.broadcasted_iota(jnp.int32, (16, cols), 0)
+        col = lax.broadcasted_iota(jnp.int32, (16, cols), 1)
+        want = jnp.where(row % 8 < 2 * reach, row % 8 % reach + row // 8 * (cols - reach), -1)
+        picks = [
+            ((col == want) & (row % 8 // reach == half)).astype(F32).astype(BF) for half in range(2)
+        ]
+        piles = [[], []]
+        for s in range(pl.cdiv(rows, 2)):
+            value = dot(picks[0], sea[2 * s], NT)
+            if 2 * s + 1 < rows:
+                value = value + dot(picks[1], sea[2 * s + 1], NT)
+            for half in range(min(2, rows - 2 * s)):
+                for k in range(2):
+                    piles[k].append(value[8 * k + half * reach : 8 * k + half * reach + reach])
+        edges = []
+        for pile in piles:
+            wide = [jnp.concatenate(pile[k : k + PILE], axis=0) for k in range(0, rows, PILE)]
+            wide.append(jnp.zeros((PILE * reach, 2 * PITCH - oc * len(wide)), F32))
+            edges.append(jnp.concatenate(wide, axis=1))
+        no_edge = jnp.zeros_like(edges[0])
+        return own, edges, no_edge
 
     weight = weight_ref[...].astype(F32)
     weight = jnp.concatenate([weight] * block, axis=1)
     weight = jnp.concatenate([weight] * block, axis=0)
     row = lax.broadcasted_iota(jnp.int32, weight.shape, 0)
     col = lax.broadcasted_iota(jnp.int32, weight.shape, 1)
-    keep = col // ch == row % 16 // 4 * 2 + row // 16
+    keep = col // ch == row % (2 * block) // 4 * 2 + row // (2 * block)
     weight = jnp.where(keep, weight, 0.0).astype(BF)
-    before = jnp.zeros((4 * block, reach), F32)
-    after = jnp.zeros((4 * block, PITCH - tile - reach), F32)
-    for g, at in enumerate(range(0, rows, block)):
+    before = jnp.zeros((4 * block, reach), BF)
+    after = jnp.zeros((4 * block, PITCH - tile - reach), BF)
+    out_copies = []
+    for at in range(0, rows, block):
         size = min(block, rows - at)
+        if at == block:
+            own, edges, no_edge = columns()
         if at in x_copies:
             x_copies[at].wait()
-        y = dot(weight[:, : size * ch], x[at : at + size].reshape(size * ch, lon))
+        y = dot(weight[:, : size * ch], x[at : at + size].reshape(size * ch, lon)).astype(BF)
         y = jnp.concatenate([before, y, after], axis=1)
         for j in range(peers):
             part = y[:, tile * j : tile * j + PITCH]
             part = jnp.concatenate([part[: 2 * block], part[2 * block :]], axis=1)
-            out_ref[j, 2 * block * g : 2 * block * (g + 1), :] = part.astype(BF)
+            if at + block < rows:
+                out_ref[j, 2 * at : 2 * at + 2 * block, :] = part
+            else:
+                edge = jnp.where(at_ref[0] == j - 1, edges[1], no_edge)
+                edge = jnp.where(at_ref[0] == j + 1, edges[0], edge)
+                end = out_ref.shape[1] - EDGES - PILE * reach
+                part = [part.astype(F32)[: SURFACE - 2 * at], own, edge, jnp.zeros((end, 2 * PITCH), F32)]
+                out_ref[j, 2 * at :, :] = jnp.concatenate(part, axis=0).astype(BF)
+        if at > 0:
+            span = pl.ds(0, 4 * block) if at == block else pl.ds(4 * block, out_ref.shape[1] - 4 * block)
+            out_copies.append(
+                pltpu.make_async_copy(
+                    out_ref.at[:, span], parts_ref.at[:, span], sems.at[1 + len(out_copies)]
+                )
+            )
+            out_copies[-1].start()
+    for copy in out_copies:
+        copy.wait()
 
 
 def flux_parts(at, x, sea, weight, reach, peers):
     return pl.pallas_call(
         functools.partial(flux_kernel, reach),
-        out_shape=jax.ShapeDtypeStruct((peers, EDGES + 8 * PILE, 2 * PITCH), BF),
+        out_shape=jax.ShapeDtypeStruct((peers, 144, 2 * PITCH), BF),
         in_specs=[SMEM, ANY, ANY, VMEM],
-        out_specs=VMEM,
+        out_specs=ANY,
         scratch_shapes=[
             pltpu.VMEM(x.shape, BF),
             pltpu.VMEM(sea.shape, BF),
+            pltpu.VMEM((peers, 144, 2 * PITCH), BF),
             pltpu.SemaphoreType.DMA((3,)),
-            pltpu.SemaphoreType.DMA((1,)),
+            pltpu.SemaphoreType.DMA((3,)),
         ],
         compiler_params=pltpu.CompilerParams(vmem_limit_bytes=58 << 20),
         cost_estimate=pl.CostEstimate(flops=1 << 30, bytes_accessed=7 << 20, transcendentals=0),
@@ -486,17 +505,22 @@
     own_pairs = odd_ref.shape[0]
     peers = parts_ref.shape[0]
     picks, force = picks_ref[...], force_ref[...]
-    total = parts_ref[0, :SURFACE, :].astype(F32)
+    total = parts_ref[0, :96, :].astype(F32)
     for j in range(1, peers):
-        total = total + parts_ref[j, :SURFACE, :].astype(F32)
+        total = total + parts_ref[j, :96, :].astype(F32)
     at = at_ref[0]
-    left = parts_ref[jnp.maximum(at - 1, 0), EDGES:, :].astype(F32)
-    right = parts_ref[jnp.minimum(at + 1, peers - 1), EDGES:, :].astype(F32)
+    left = parts_ref[jnp.maximum(at - 1, 0), 112:, :].astype(F32)[EDGES - 112 :]
+    right = parts_ref[jnp.minimum(at + 1, peers - 1), 112:, :].astype(F32)[EDGES - 112 :]
     for s in range(own_pairs):
         flux[s] = total[4 * s : 4 * s + 4, :]
-        span, lanes = slice(8 * (s % PILE), 8 * (s % PILE) + 8), slice(ch * (s // PILE), ch * (s // PILE) + ch)
-        left_ref[s] = left[span, lanes]
-        right_ref[s] = right[span, lanes]
+        for edge, ref in ((left, left_ref), (right, right_ref)):
+            both = []
+            for r in (2 * s, 2 * s + 1):
+                if r < rows:
+                    lanes = slice(ch * (r // PILE), ch * (r // PILE) + ch)
+                    both.append(edge[reach * (r % PILE) : reach * (r % PILE) + reach, lanes])
+            both.append(jnp.zeros((8 - reach * len(both), ch), F32))
+            ref[s] = jnp.concatenate(both, axis=0)
 
     def fill(s, second):
         more = pair_forcing(s, left_ref, right_ref, picks, flux[s], force)

time: 128 us -> 124 us (0.969)
  Pallas kernels: 67.7 us -> 65.1 us
    pallas_call x1, Pallas kernels: 11.9 us -> 10.5 us  [inverse(): pl.pallas_call(inverse_kernel, out_shape=pltpu.HBM(x.shape, BF), in_specs...]
  transfers between devices with their start and end apart: 5 -> 5, of which waited for: 3 -> 3; matrix products, arithmetic and copies ran while one was open for 4% -> 4% of each run, Pallas kernels for 38% -> 39%
where the time goes in v4:
time: 124 us
  Pallas kernels  65.1 us (52%)
  starting transfers between devices  25 us (20%)
  waiting for transfers between devices  19.4 us (16%)
  local copies, waits for them, and re-layouts  13 us (10%)
    pallas_call x1, Pallas kernels, ocean_block(): pl.pallas_call(functools.partial(ocean_kernel, reach, mask_tiles), out_sh...  21.9 us
    all_to_all x2, waiting for transfers between devices, exchange(): lax.all_to_all(wire.reshape(peers, HALF, 8 * ch), ('chan', 'lat'), 0, 0,...  16.1 us
    all_to_all x2, starting transfers between devices, exchange(): lax.all_to_all(wire.reshape(peers, HALF, 8 * ch), ('chan', 'lat'), 0, 0,...  13.4 us
    pallas_call x1, Pallas kernels, inverse(): pl.pallas_call(inverse_kernel, out_shape=pltpu.HBM(x.shape, BF), in_specs...  10.5 us
    pallas_call x1, Pallas kernels, forward(): pl.pallas_call(forward_kernel, out_shape=pltpu.HBM((peers * HALF, 8 * ch)...  9.96 us
    pallas_call x1, Pallas kernels, wet_rows(): pl.pallas_call(functools.partial(wet_kernel, reach), out_shape=(own, own,...  9.07 us
    unnamed x37, local copies, waits for them, and re-layouts  8.7 us
    pallas_call x1, Pallas kernels, spectral(): pl.pallas_call(spectral_kernel, out_shape=pltpu.HBM(wire.shape, BF), in_s...  7.16 us
  transfers between devices with their start and end apart: 5, of which 3 were waited for; matrix products, arithmetic and copies ran while one was open for 4% of the time, Pallas kernels for 39%

profile of v4, /device:TPU:1, one launch (start us, length us, event | category | flops | bytes accessed | tf_op | source)
XLA Modules:
  0.0 123.6 jit_solution(5937547516817996695)
XLA Ops:
  0.6 6.5 %flux_parts.1 = bf16[8,144,384]{2,1,0:T(8,128)(2,1)} custom-call(s32[1]{0:T(128)} %bitcast.at_ref, bf16[45,48,1440]{2,1,0:T(8,128)(2,1)} %bitcast.34, bf16[45,76,180]{2,1,0:T(8,128)(2,1)} %bitcast.30, bf16[4,48]{1,0:T(4,128)(2,1)} %weight_ref.1), custom_call_target="tpu_custom_call" | custom-call | flops 1073741824 | bytes 7340032 | tf_op jit(solution)/shard_map/flux_parts/pallas_call | solution.py:453
  7.1 6.8 %all-to-all-start.1 = ((bf16[8,144,384]{2,1,0:T(8,128)(2,1)}), bf16[8,144,384]{2,1,0:T(8,128)(2,1)S(1)}, u32[]{:S(2)}, u32[]{:S(2)}) async-start(bf16[8,144,384]{2,1,0:T(8,128)(2,1)} %flux_parts.1), calls=%async_computation.1 | async-start | bytes 1769472 | tf_op jit(solution)/shard_map/all_to_all | solution.py:738
  13.9 10.0 %dft_forward.1 = bf16[3072,384]{1,0:T(8,128)(2,1)} custom-call(s32[1]{0:T(128)} %bitcast.at_ref, bf16[45,48,1440]{2,1,0:T(8,128)(2,1)} %bitcast.35, bf16[45,76,180]{2,1,0:T(8,128)(2,1)} %bitcast.31, bf16[1,48]{1,0:T(2,128)(2,1)} %bitcast.47, bf16[1440,512]{1,0:T(8,128)(2,1)} %constant.23.clone.table_ref, bf16[384,384]{1,0:T(8,128)(2,1)} %constant.25.clone.swap_ref), custom_call_target="tpu_custom_call" | custom-call | flops 3185049600 | bytes 14680064 | tf_op jit(solution)/shard_map/dft_forward/pallas_call | solution.py:137
  23.9 3.4 %all-to-all-done.1.parts_ref = bf16[8,144,384]{2,1,0:T(8,128)(2,1)S(1)} async-done(((bf16[8,144,384]{2,1,0:T(8,128)(2,1)}), bf16[8,144,384]{2,1,0:T(8,128)(2,1)S(1)}, u32[]{:S(2)}, u32[]{:S(2)}) %all-to-all-start.1) | async-done | bytes 884768 | tf_op jit(solution)/shard_map/all_to_all | solution.py:738
  27.3 8.4 %all-to-all-start = ((bf16[128,24,384]{2,1,0:T(8,128)(2,1)}), bf16[128,24,384]{2,1,0:T(8,128)(2,1)}, u32[]{:S(2)}, u32[]{:S(2)}) async-start(bf16[128,24,384]{2,1,0:T(8,128)(2,1)} %bitcast.37), calls=%async_computation | async-start | bytes 4718592 | tf_op jit(solution)/shard_map/all_to_all | solution.py:732
  35.7 0.6 copy.24
  36.5 1.3 %copy.26 = bf16[2,2,16,24,256]{4,3,2,1,0:T(8,128)(2,1)} copy(bf16[2,2,16,24,256]{4,2,1,3,0:T(8,128)(2,1)S(1)} %bitcast.39) | data formatting | bytes 1572864 | tf_op jit(solution)/shard_map/transpose | solution.py:757
  37.8 0.6 copy.27
  38.6 1.4 %copy.29 = bf16[2,2,16,24,256]{4,3,2,1,0:T(8,128)(2,1)} copy(bf16[2,2,16,24,256]{4,2,1,3,0:T(8,128)(2,1)S(1)} %bitcast.40) | data formatting | bytes 1572864 | tf_op jit(solution)/shard_map/transpose | solution.py:757
  40.6 9.1 %wet_rows.1 = (bf16[23,76,384]{2,1,0:T(8,128)(2,1)S(1)}, bf16[23,76,384]{2,1,0:T(8,128)(2,1)S(1)}, f32[23,76,384]{2,1,0:T(8,128)S(1)}, bf16[3,76,192]{2,1,0:T(8,128)(2,1)S(1)}, bf16[3,76,192]{2,1,0:T(8,128)(2,1)S(1)}) custom-call(s32[1]{0:T(128)} %bitcast.at_ref, bf16[45,76,180]{2,1,0:T(8,128)(2,1)S(1)} %bitcast.32, bf16[16,384]{1,0:T(8,128)(2,1)S(1)} %copy-done.2, ...), custom_call_target="tpu_custom_call" | custom-call | flops 1048576 | bytes 1048576 | tf_op jit(solution)/shard_map/wet_rows/pallas_call | solution.py:553
  49.7 1.5 %copy-done.3 = f32[23,76,384]{2,1,0:T(8,128)} copy-done((f32[23,76,384]{2,1,0:T(8,128)}, f32[23,76,384]{2,1,0:T(8,128)S(1)}, u32[]{:S(2)}) %copy-start.3) | copy-done | bytes 2684952
  51.3 1.1 copy-done.5
  52.4 1.1 copy-done.7
  53.5 3.3 %collective-permute-start = (bf16[3,76,192]{2,1,0:T(8,128)(2,1)S(1)}, bf16[3,76,192]{2,1,0:T(8,128)(2,1)S(1)}, u32[]{:S(2)}, u32[]{:S(2)}) collective-permute-start(bf16[3,76,192]{2,1,0:T(8,128)(2,1)S(1)} %get-tuple-element.17), channel_id=1, source_target_pairs={{0,8},{8,16},{16,24},{24,32},{32,40},{40,48},{48,56},{56,64},{64,7... | collective-permute-start | bytes 262664 | tf_op jit(solution)/shard_map/ppermute | solution.py:695
  56.8 1.5 %collective-permute-start.1 = (bf16[3,76,192]{2,1,0:T(8,128)(2,1)S(1)}, bf16[3,76,192]{2,1,0:T(8,128)(2,1)S(1)}, u32[]{:S(2)}, u32[]{:S(2)}) collective-permute-start(bf16[3,76,192]{2,1,0:T(8,128)(2,1)S(1)} %get-tuple-element.16), channel_id=1, source_target_pairs={{8,0},{16,8},{24,16},{32,24},{40,32},{48,40},{56,48},{64,56},{72,6... | collective-permute-start | bytes 262664 | tf_op jit(solution)/shard_map/ppermute | solution.py:695
  58.3 10.1 %all-to-all-done = bf16[128,24,384]{2,1,0:T(8,128)(2,1)} async-done(((bf16[128,24,384]{2,1,0:T(8,128)(2,1)}), bf16[128,24,384]{2,1,0:T(8,128)(2,1)}, u32[]{:S(2)}, u32[]{:S(2)}) %all-to-all-start) | async-done | bytes 2359328 | tf_op jit(solution)/shard_map/all_to_all | solution.py:732
  68.4 7.2 %spectral.1 = bf16[3072,384]{1,0:T(8,128)(2,1)} custom-call(bf16[3072,384]{1,0:T(8,128)(2,1)} %bitcast.5.wire_hbm, bf16[2,2,384,256]{3,2,1,0:T(8,128)(2,1)} %bitcast.44, bf16[2,2,384,256]{3,2,1,0:T(8,128)(2,1)} %bitcast.45, bf16[2,384,384]{2,1,0:T(8,128)(2,1)} %mix_hbm.1, bf16[384,384]{1,0:T(8,128)(2,1)} %constant.28.clone.spread_hbm), custom_call_target="tpu_custom_call" | custom-call | flops 2147483648 | bytes 9437184 | tf_op jit(solution)/shard_map/spectral/pallas_call | solution.py:248
  75.6 5.0 %all-to-all-start.2 = ((bf16[128,24,384]{2,1,0:T(8,128)(2,1)}), bf16[128,24,384]{2,1,0:T(8,128)(2,1)}, u32[]{:S(2)}, u32[]{:S(2)}) async-start(bf16[128,24,384]{2,1,0:T(8,128)(2,1)} %bitcast.43), calls=%async_computation.2 | async-start | bytes 4718592 | tf_op jit(solution)/shard_map/all_to_all | solution.py:732
  80.6 1.8 %copy-done.4 = f32[23,76,384]{2,1,0:T(8,128)S(1)} copy-done((f32[23,76,384]{2,1,0:T(8,128)S(1)}, f32[23,76,384]{2,1,0:T(8,128)}, u32[]{:S(2)}) %copy-start.4) | copy-done | bytes 2684952
  82.4 1.4 %copy-done.6 = bf16[23,76,384]{2,1,0:T(8,128)(2,1)S(1)} copy-done((bf16[23,76,384]{2,1,0:T(8,128)(2,1)S(1)}, bf16[23,76,384]{2,1,0:T(8,128)(2,1)}, u32[]{:S(2)}) %copy-start.6) | copy-done | bytes 1342488
  83.8 1.4 %copy-done.8 = bf16[23,76,384]{2,1,0:T(8,128)(2,1)S(1)} copy-done((bf16[23,76,384]{2,1,0:T(8,128)(2,1)S(1)}, bf16[23,76,384]{2,1,0:T(8,128)(2,1)}, u32[]{:S(2)}) %copy-start.8) | copy-done | bytes 1342488
  85.1 21.9 %ocean_block.1 = bf16[45,76,180]{2,1,0:T(8,128)(2,1)} custom-call(bf16[45,76,180]{2,1,0:T(8,128)(2,1)S(1)} %bitcast.33, f32[23,76,384]{2,1,0:T(8,128)S(1)} %copy-done.4, bf16[23,76,384]{2,1,0:T(8,128)(2,1)S(1)} %copy-done.6, bf16[23,76,384]{2,1,0:T(8,128)(2,1)S(1)} %copy-done.8, bf16[3,76,192]{2,1,0:T(8,128)(2,1)S(1)} %collective-permute-done.low_ref, ...), custom_call_target="tpu_custom_call" | custom-call | flops 32212254720 | bytes 8388608 | tf_op jit(solution)/shard_map/ocean_block/pallas_call | solution.py:665
  107.0 6.0 %all-to-all-done.2 = bf16[128,24,384]{2,1,0:T(8,128)(2,1)} async-done(((bf16[128,24,384]{2,1,0:T(8,128)(2,1)}), bf16[128,24,384]{2,1,0:T(8,128)(2,1)}, u32[]{:S(2)}, u32[]{:S(2)}) %all-to-all-start.2) | async-done | bytes 2359328 | tf_op jit(solution)/shard_map/all_to_all | solution.py:732
  113.0 10.5 %dft_inverse.1 = bf16[45,48,1440]{2,1,0:T(8,128)(2,1)} custom-call(bf16[3072,384]{1,0:T(8,128)(2,1)} %bitcast.17.wire_ref, bf16[512,1440]{1,0:T(8,128)(2,1)} %constant.24.clone.table_ref, bf16[384,384]{1,0:T(8,128)(2,1)} %constant.26.clone.swap_ref, bf16[45,48,1440]{2,1,0:T(8,128)(2,1)} %bitcast.36, bf16[1,48]{1,0:T(2,128)(2,1)} %bitcast.48, ...), custom_call_target="tpu_custom_call" | custom-call | flops 3185049600 | bytes 20971520 | tf_op jit(solution)/shard_map/dft_inverse/pallas_call | solution.py:326
  (44 shorter events, 1.0 us)
Async XLA Ops:
  7.1 20.2 %all-to-all-start.1 = ((bf16[8,144,384]{2,1,0:T(8,128)(2,1)}), bf16[8,144,384]{2,1,0:T(8,128)(2,1)S(1)}, u32[]{:S(2)}, u32[]{:S(2)}) async-start(bf16[8,144,384]{2,1,0:T(8,128)(2,1)} %flux_parts.1), calls=%async_computation.1 | async-start | bytes 1769472 | tf_op jit(solution)/shard_map/all_to_all | solution.py:738
  27.3 13.3 %copy-start.1 = (bf16[8,144,384]{2,1,0:T(8,128)(2,1)}, bf16[8,144,384]{2,1,0:T(8,128)(2,1)S(1)}, u32[]{:S(2)}) copy-start(bf16[8,144,384]{2,1,0:T(8,128)(2,1)S(1)} %all-to-all-done.1.parts_ref) | copy-start | bytes 2654212
  27.3 8.4 %copy-start.10 = (bf16[2,256,720]{1,2,0:T(8,128)(2,1)S(1)}, bf16[2,256,720]{1,2,0:T(8,128)(2,1)}, u32[]{:S(2)}) copy-start(bf16[2,256,720]{1,2,0:T(8,128)(2,1)} %param.21) | copy-start | bytes 2211844
  27.3 41.1 %all-to-all-start = ((bf16[128,24,384]{2,1,0:T(8,128)(2,1)}), bf16[128,24,384]{2,1,0:T(8,128)(2,1)}, u32[]{:S(2)}, u32[]{:S(2)}) async-start(bf16[128,24,384]{2,1,0:T(8,128)(2,1)} %bitcast.37), calls=%async_computation | async-start | bytes 4718592 | tf_op jit(solution)/shard_map/all_to_all | solution.py:732
  36.3 1.5 %copy-start.11 = (bf16[2,720,256]{2,1,0:T(8,128)(2,1)S(1)}, bf16[2,720,256]{2,1,0:T(8,128)(2,1)}, u32[]{:S(2)}) copy-start(bf16[2,720,256]{2,1,0:T(8,128)(2,1)} %param.22) | copy-start | bytes 2211844
  38.4 1.7 %copy-start.12 = (bf16[304,76]{0,1:T(8,128)(2,1)S(1)}, bf16[304,76]{0,1:T(8,128)(2,1)}, u32[]{:S(2)}) copy-start(bf16[304,76]{0,1:T(8,128)(2,1)} %param.30) | copy-start | bytes 138628
  38.4 1.8 %copy-start.13 = (bf16[76,1,7,7]{0,3,2,1:T(8,128)(2,1)S(1)}, bf16[76,1,7,7]{0,3,2,1:T(8,128)(2,1)}, u32[]{:S(2)}) copy-start(bf16[76,1,7,7]{0,3,2,1:T(8,128)(2,1)} %param.28) | copy-start | bytes 22348
  38.4 1.9 %copy-start.16 = (f32[76]{0:T(128)S(1)}, f32[76]{0:T(128)}, u32[]{:S(2)}) copy-start(f32[76]{0:T(128)} %param.29) | copy-start | bytes 916
  38.4 2.1 %copy-start.14 = (s32[5,5]{1,0:T(8,128)S(1)}, s32[5,5]{1,0:T(8,128)}, u32[]{:S(2)}) copy-start(s32[5,5]{1,0:T(8,128)} %param.27) | copy-start | bytes 304
  38.4 2.1 %copy-start.15 = (f32[76,4]{0,1:T(4,128)S(1)}, f32[76,4]{0,1:T(4,128)}, u32[]{:S(2)}) copy-start(f32[76,4]{0,1:T(4,128)} %param.25) | copy-start | bytes 3652
  38.4 2.2 %copy-start = (bf16[76,45,180]{2,0,1:T(8,128)(2,1)S(1)}, bf16[76,45,180]{2,0,1:T(8,128)(2,1)}, u32[]{:S(2)}) copy-start(bf16[76,45,180]{2,0,1:T(8,128)(2,1)} %param.26) | copy-start | bytes 3693604
  38.4 2.2 %copy-start.2 = (bf16[16,384]{1,0:T(8,128)(2,1)S(1)}, bf16[16,384]{1,0:T(8,128)(2,1)}, u32[]{:S(2)}) copy-start(bf16[16,384]{1,0:T(8,128)(2,1)} %constant.27.clone.picks_ref) | copy-start | bytes 36868
  49.7 1.6 %copy-start.3 = (f32[23,76,384]{2,1,0:T(8,128)}, f32[23,76,384]{2,1,0:T(8,128)S(1)}, u32[]{:S(2)}) copy-start(f32[23,76,384]{2,1,0:T(8,128)S(1)} %get-tuple-element.21.forcing_ref) | copy-start | bytes 8054788
  51.3 1.1 copy-start.5
  52.3 1.1 copy-start.7
  53.5 22.1 %collective-permute-start = (bf16[3,76,192]{2,1,0:T(8,128)(2,1)S(1)}, bf16[3,76,192]{2,1,0:T(8,128)(2,1)S(1)}, u32[]{:S(2)}, u32[]{:S(2)}) collective-permute-start(bf16[3,76,192]{2,1,0:T(8,128)(2,1)S(1)} %get-tuple-element.17), channel_id=1, source_target_pairs={{0,8},{8,16},{16,24},{24,32},{32,40},{40,48},{48,56},{56,64},{64,7... | collective-permute-start | bytes 262664 | tf_op jit(solution)/shard_map/ppermute | solution.py:695
  56.8 18.8 %collective-permute-start.1 = (bf16[3,76,192]{2,1,0:T(8,128)(2,1)S(1)}, bf16[3,76,192]{2,1,0:T(8,128)(2,1)S(1)}, u32[]{:S(2)}, u32[]{:S(2)}) collective-permute-start(bf16[3,76,192]{2,1,0:T(8,128)(2,1)S(1)} %get-tuple-element.16), channel_id=1, source_target_pairs={{8,0},{16,8},{24,16},{32,24},{40,32},{48,40},{56,48},{64,56},{72,6... | collective-permute-start | bytes 262664 | tf_op jit(solution)/shard_map/ppermute | solution.py:695
  75.6 5.0 %copy-start.9 = (bf16[76,304]{1,0:T(8,128)(2,1)S(1)}, bf16[76,304]{1,0:T(8,128)(2,1)}, u32[]{:S(2)}) copy-start(bf16[76,304]{1,0:T(8,128)(2,1)} %contract_ref.1) | copy-start | bytes 138628
  75.6 37.4 %all-to-all-start.2 = ((bf16[128,24,384]{2,1,0:T(8,128)(2,1)}), bf16[128,24,384]{2,1,0:T(8,128)(2,1)}, u32[]{:S(2)}, u32[]{:S(2)}) async-start(bf16[128,24,384]{2,1,0:T(8,128)(2,1)} %bitcast.43), calls=%async_computation.2 | async-start | bytes 4718592 | tf_op jit(solution)/shard_map/all_to_all | solution.py:732
  80.6 1.8 %copy-start.4 = (f32[23,76,384]{2,1,0:T(8,128)S(1)}, f32[23,76,384]{2,1,0:T(8,128)}, u32[]{:S(2)}) copy-start(f32[23,76,384]{2,1,0:T(8,128)} %copy-done.3) | copy-start | bytes 8054788
  82.4 1.4 %copy-start.6 = (bf16[23,76,384]{2,1,0:T(8,128)(2,1)S(1)}, bf16[23,76,384]{2,1,0:T(8,128)(2,1)}, u32[]{:S(2)}) copy-start(bf16[23,76,384]{2,1,0:T(8,128)(2,1)} %copy-done.5) | copy-start | bytes 4027396
  83.8 1.4 %copy-start.8 = (bf16[23,76,384]{2,1,0:T(8,128)(2,1)S(1)}, bf16[23,76,384]{2,1,0:T(8,128)(2,1)}, u32[]{:S(2)}) copy-start(bf16[23,76,384]{2,1,0:T(8,128)(2,1)} %copy-done.7) | copy-start | bytes 4027396

commit v5 on v4

--- a/solution.py
+++ b/solution.py
@@ -420,11 +420,11 @@
     out_copies = []
     for at in range(0, rows, block):
         size = min(block, rows - at)
-        if at == block:
-            own, edges, no_edge = columns()
         if at in x_copies:
             x_copies[at].wait()
         y = dot(weight[:, : size * ch], x[at : at + size].reshape(size * ch, lon)).astype(BF)
+        if at == block:
+            own, edges, no_edge = columns()
         y = jnp.concatenate([before, y, after], axis=1)
         for j in range(peers):
             part = y[:, tile * j : tile * j + PITCH]

time: 124 us -> 123 us (level)
  no operation moved by 1% of the time
where the time goes in v5:
time: 123 us
  Pallas kernels  64.4 us (52%)
  starting transfers between devices  25 us (20%)
  waiting for transfers between devices  19.4 us (16%)
  local copies, waits for them, and re-layouts  13 us (11%)
    pallas_call x1, Pallas kernels, ocean_block(): pl.pallas_call(functools.partial(ocean_kernel, reach, mask_tiles), out_sh...  21.9 us
    all_to_all x2, waiting for transfers between devices, exchange(): lax.all_to_all(wire.reshape(peers, HALF, 8 * ch), ('chan', 'lat'), 0, 0,...  16.1 us
    all_to_all x2, starting transfers between devices, exchange(): lax.all_to_all(wire.reshape(peers, HALF, 8 * ch), ('chan', 'lat'), 0, 0,...  13.4 us
    pallas_call x1, Pallas kernels, inverse(): pl.pallas_call(inverse_kernel, out_shape=pltpu.HBM(x.shape, BF), in_specs...  10.5 us
    pallas_call x1, Pallas kernels, forward(): pl.pallas_call(forward_kernel, out_shape=pltpu.HBM((peers * HALF, 8 * ch)...  9.96 us
    pallas_call x1, Pallas kernels, wet_rows(): pl.pallas_call(functools.partial(wet_kernel, reach), out_shape=(own, own,...  9.07 us
    unnamed x37, local copies, waits for them, and re-layouts  8.7 us
    pallas_call x1, Pallas kernels, spectral(): pl.pallas_call(spectral_kernel, out_shape=pltpu.HBM(wire.shape, BF), in_s...  7.17 us
  transfers between devices with their start and end apart: 5, of which 3 were waited for; matrix products, arithmetic and copies ran while one was open for 4% of the time, Pallas kernels for 39%

profile of v5, /device:TPU:1, one launch (start us, length us, event | category | flops | bytes accessed | tf_op | source)
XLA Modules:
  0.0 122.9 jit_solution(15108537247029601098)
XLA Ops:
  0.6 5.8 %flux_parts.1 = bf16[8,144,384]{2,1,0:T(8,128)(2,1)} custom-call(s32[1]{0:T(128)} %bitcast.at_ref, bf16[45,48,1440]{2,1,0:T(8,128)(2,1)} %bitcast.34, bf16[45,76,180]{2,1,0:T(8,128)(2,1)} %bitcast.30, bf16[4,48]{1,0:T(4,128)(2,1)} %weight_ref.1), custom_call_target="tpu_custom_call" | custom-call | flops 1073741824 | bytes 7340032 | tf_op jit(solution)/shard_map/flux_parts/pallas_call | solution.py:453
  6.4 6.8 %all-to-all-start.1 = ((bf16[8,144,384]{2,1,0:T(8,128)(2,1)}), bf16[8,144,384]{2,1,0:T(8,128)(2,1)S(1)}, u32[]{:S(2)}, u32[]{:S(2)}) async-start(bf16[8,144,384]{2,1,0:T(8,128)(2,1)} %flux_parts.1), calls=%async_computation.1 | async-start | bytes 1769472 | tf_op jit(solution)/shard_map/all_to_all | solution.py:738
  13.3 10.0 %dft_forward.1 = bf16[3072,384]{1,0:T(8,128)(2,1)} custom-call(s32[1]{0:T(128)} %bitcast.at_ref, bf16[45,48,1440]{2,1,0:T(8,128)(2,1)} %bitcast.35, bf16[45,76,180]{2,1,0:T(8,128)(2,1)} %bitcast.31, bf16[1,48]{1,0:T(2,128)(2,1)} %bitcast.47, bf16[1440,512]{1,0:T(8,128)(2,1)} %constant.23.clone.table_ref, bf16[384,384]{1,0:T(8,128)(2,1)} %constant.25.clone.swap_ref), custom_call_target="tpu_custom_call" | custom-call | flops 3185049600 | bytes 14680064 | tf_op jit(solution)/shard_map/dft_forward/pallas_call | solution.py:137
  23.2 3.4 %all-to-all-done.1.parts_ref = bf16[8,144,384]{2,1,0:T(8,128)(2,1)S(1)} async-done(((bf16[8,144,384]{2,1,0:T(8,128)(2,1)}), bf16[8,144,384]{2,1,0:T(8,128)(2,1)S(1)}, u32[]{:S(2)}, u32[]{:S(2)}) %all-to-all-start.1) | async-done | bytes 884768 | tf_op jit(solution)/shard_map/all_to_all | solution.py:738
  26.6 8.4 %all-to-all-start = ((bf16[128,24,384]{2,1,0:T(8,128)(2,1)}), bf16[128,24,384]{2,1,0:T(8,128)(2,1)}, u32[]{:S(2)}, u32[]{:S(2)}) async-start(bf16[128,24,384]{2,1,0:T(8,128)(2,1)} %bitcast.37), calls=%async_computation | async-start | bytes 4718592 | tf_op jit(solution)/shard_map/all_to_all | solution.py:732
  35.0 0.6 copy.24
  35.8 1.3 %copy.26 = bf16[2,2,16,24,256]{4,3,2,1,0:T(8,128)(2,1)} copy(bf16[2,2,16,24,256]{4,2,1,3,0:T(8,128)(2,1)S(1)} %bitcast.39) | data formatting | bytes 1572864 | tf_op jit(solution)/shard_map/transpose | solution.py:757
  37.1 0.6 copy.27
  37.9 1.4 %copy.29 = bf16[2,2,16,24,256]{4,3,2,1,0:T(8,128)(2,1)} copy(bf16[2,2,16,24,256]{4,2,1,3,0:T(8,128)(2,1)S(1)} %bitcast.40) | data formatting | bytes 1572864 | tf_op jit(solution)/shard_map/transpose | solution.py:757
  39.9 9.1 %wet_rows.1 = (bf16[23,76,384]{2,1,0:T(8,128)(2,1)S(1)}, bf16[23,76,384]{2,1,0:T(8,128)(2,1)S(1)}, f32[23,76,384]{2,1,0:T(8,128)S(1)}, bf16[3,76,192]{2,1,0:T(8,128)(2,1)S(1)}, bf16[3,76,192]{2,1,0:T(8,128)(2,1)S(1)}) custom-call(s32[1]{0:T(128)} %bitcast.at_ref, bf16[45,76,180]{2,1,0:T(8,128)(2,1)S(1)} %bitcast.32, bf16[16,384]{1,0:T(8,128)(2,1)S(1)} %copy-done.2, ...), custom_call_target="tpu_custom_call" | custom-call | flops 1048576 | bytes 1048576 | tf_op jit(solution)/shard_map/wet_rows/pallas_call | solution.py:553
  49.0 1.5 %copy-done.3 = f32[23,76,384]{2,1,0:T(8,128)} copy-done((f32[23,76,384]{2,1,0:T(8,128)}, f32[23,76,384]{2,1,0:T(8,128)S(1)}, u32[]{:S(2)}) %copy-start.3) | copy-done | bytes 2684952
  50.6 1.1 copy-done.5
  51.7 1.1 copy-done.7
  52.8 3.3 %collective-permute-start = (bf16[3,76,192]{2,1,0:T(8,128)(2,1)S(1)}, bf16[3,76,192]{2,1,0:T(8,128)(2,1)S(1)}, u32[]{:S(2)}, u32[]{:S(2)}) collective-permute-start(bf16[3,76,192]{2,1,0:T(8,128)(2,1)S(1)} %get-tuple-element.17), channel_id=1, source_target_pairs={{0,8},{8,16},{16,24},{24,32},{32,40},{40,48},{48,56},{56,64},{64,7... | collective-permute-start | bytes 262664 | tf_op jit(solution)/shard_map/ppermute | solution.py:695
  56.1 1.5 %collective-permute-start.1 = (bf16[3,76,192]{2,1,0:T(8,128)(2,1)S(1)}, bf16[3,76,192]{2,1,0:T(8,128)(2,1)S(1)}, u32[]{:S(2)}, u32[]{:S(2)}) collective-permute-start(bf16[3,76,192]{2,1,0:T(8,128)(2,1)S(1)} %get-tuple-element.16), channel_id=1, source_target_pairs={{8,0},{16,8},{24,16},{32,24},{40,32},{48,40},{56,48},{64,56},{72,6... | collective-permute-start | bytes 262664 | tf_op jit(solution)/shard_map/ppermute | solution.py:695
  57.6 10.1 %all-to-all-done = bf16[128,24,384]{2,1,0:T(8,128)(2,1)} async-done(((bf16[128,24,384]{2,1,0:T(8,128)(2,1)}), bf16[128,24,384]{2,1,0:T(8,128)(2,1)}, u32[]{:S(2)}, u32[]{:S(2)}) %all-to-all-start) | async-done | bytes 2359328 | tf_op jit(solution)/shard_map/all_to_all | solution.py:732
  67.7 7.2 %spectral.1 = bf16[3072,384]{1,0:T(8,128)(2,1)} custom-call(bf16[3072,384]{1,0:T(8,128)(2,1)} %bitcast.5.wire_hbm, bf16[2,2,384,256]{3,2,1,0:T(8,128)(2,1)} %bitcast.44, bf16[2,2,384,256]{3,2,1,0:T(8,128)(2,1)} %bitcast.45, bf16[2,384,384]{2,1,0:T(8,128)(2,1)} %mix_hbm.1, bf16[384,384]{1,0:T(8,128)(2,1)} %constant.28.clone.spread_hbm), custom_call_target="tpu_custom_call" | custom-call | flops 2147483648 | bytes 9437184 | tf_op jit(solution)/shard_map/spectral/pallas_call | solution.py:248
  74.9 5.0 %all-to-all-start.2 = ((bf16[128,24,384]{2,1,0:T(8,128)(2,1)}), bf16[128,24,384]{2,1,0:T(8,128)(2,1)}, u32[]{:S(2)}, u32[]{:S(2)}) async-start(bf16[128,24,384]{2,1,0:T(8,128)(2,1)} %bitcast.43), calls=%async_computation.2 | async-start | bytes 4718592 | tf_op jit(solution)/shard_map/all_to_all | solution.py:732
  79.9 1.8 %copy-done.4 = f32[23,76,384]{2,1,0:T(8,128)S(1)} copy-done((f32[23,76,384]{2,1,0:T(8,128)S(1)}, f32[23,76,384]{2,1,0:T(8,128)}, u32[]{:S(2)}) %copy-start.4) | copy-done | bytes 2684952
  81.7 1.4 %copy-done.6 = bf16[23,76,384]{2,1,0:T(8,128)(2,1)S(1)} copy-done((bf16[23,76,384]{2,1,0:T(8,128)(2,1)S(1)}, bf16[23,76,384]{2,1,0:T(8,128)(2,1)}, u32[]{:S(2)}) %copy-start.6) | copy-done | bytes 1342488
  83.1 1.4 %copy-done.8 = bf16[23,76,384]{2,1,0:T(8,128)(2,1)S(1)} copy-done((bf16[23,76,384]{2,1,0:T(8,128)(2,1)S(1)}, bf16[23,76,384]{2,1,0:T(8,128)(2,1)}, u32[]{:S(2)}) %copy-start.8) | copy-done | bytes 1342488
  84.4 21.9 %ocean_block.1 = bf16[45,76,180]{2,1,0:T(8,128)(2,1)} custom-call(bf16[45,76,180]{2,1,0:T(8,128)(2,1)S(1)} %bitcast.33, f32[23,76,384]{2,1,0:T(8,128)S(1)} %copy-done.4, bf16[23,76,384]{2,1,0:T(8,128)(2,1)S(1)} %copy-done.6, bf16[23,76,384]{2,1,0:T(8,128)(2,1)S(1)} %copy-done.8, bf16[3,76,192]{2,1,0:T(8,128)(2,1)S(1)} %collective-permute-done.low_ref, ...), custom_call_target="tpu_custom_call" | custom-call | flops 32212254720 | bytes 8388608 | tf_op jit(solution)/shard_map/ocean_block/pallas_call | solution.py:665
  106.3 6.0 %all-to-all-done.2 = bf16[128,24,384]{2,1,0:T(8,128)(2,1)} async-done(((bf16[128,24,384]{2,1,0:T(8,128)(2,1)}), bf16[128,24,384]{2,1,0:T(8,128)(2,1)}, u32[]{:S(2)}, u32[]{:S(2)}) %all-to-all-start.2) | async-done | bytes 2359328 | tf_op jit(solution)/shard_map/all_to_all | solution.py:732
  112.3 10.5 %dft_inverse.1 = bf16[45,48,1440]{2,1,0:T(8,128)(2,1)} custom-call(bf16[3072,384]{1,0:T(8,128)(2,1)} %bitcast.17.wire_ref, bf16[512,1440]{1,0:T(8,128)(2,1)} %constant.24.clone.table_ref, bf16[384,384]{1,0:T(8,128)(2,1)} %constant.26.clone.swap_ref, bf16[45,48,1440]{2,1,0:T(8,128)(2,1)} %bitcast.36, bf16[1,48]{1,0:T(2,128)(2,1)} %bitcast.48, ...), custom_call_target="tpu_custom_call" | custom-call | flops 3185049600 | bytes 20971520 | tf_op jit(solution)/shard_map/dft_inverse/pallas_call | solution.py:326
  (44 shorter events, 1.0 us)
Async XLA Ops:
  6.4 20.2 %all-to-all-start.1 = ((bf16[8,144,384]{2,1,0:T(8,128)(2,1)}), bf16[8,144,384]{2,1,0:T(8,128)(2,1)S(1)}, u32[]{:S(2)}, u32[]{:S(2)}) async-start(bf16[8,144,384]{2,1,0:T(8,128)(2,1)} %flux_parts.1), calls=%async_computation.1 | async-start | bytes 1769472 | tf_op jit(solution)/shard_map/all_to_all | solution.py:738
  26.6 13.3 %copy-start.1 = (bf16[8,144,384]{2,1,0:T(8,128)(2,1)}, bf16[8,144,384]{2,1,0:T(8,128)(2,1)S(1)}, u32[]{:S(2)}) copy-start(bf16[8,144,384]{2,1,0:T(8,128)(2,1)S(1)} %all-to-all-done.1.parts_ref) | copy-start | bytes 2654212
  26.6 8.4 %copy-start.10 = (bf16[2,256,720]{1,2,0:T(8,128)(2,1)S(1)}, bf16[2,256,720]{1,2,0:T(8,128)(2,1)}, u32[]{:S(2)}) copy-start(bf16[2,256,720]{1,2,0:T(8,128)(2,1)} %param.21) | copy-start | bytes 2211844
  26.6 41.1 %all-to-all-start = ((bf16[128,24,384]{2,1,0:T(8,128)(2,1)}), bf16[128,24,384]{2,1,0:T(8,128)(2,1)}, u32[]{:S(2)}, u32[]{:S(2)}) async-start(bf16[128,24,384]{2,1,0:T(8,128)(2,1)} %bitcast.37), calls=%async_computation | async-start | bytes 4718592 | tf_op jit(solution)/shard_map/all_to_all | solution.py:732
  35.6 1.5 %copy-start.11 = (bf16[2,720,256]{2,1,0:T(8,128)(2,1)S(1)}, bf16[2,720,256]{2,1,0:T(8,128)(2,1)}, u32[]{:S(2)}) copy-start(bf16[2,720,256]{2,1,0:T(8,128)(2,1)} %param.22) | copy-start | bytes 2211844
  37.7 1.7 %copy-start.12 = (bf16[304,76]{0,1:T(8,128)(2,1)S(1)}, bf16[304,76]{0,1:T(8,128)(2,1)}, u32[]{:S(2)}) copy-start(bf16[304,76]{0,1:T(8,128)(2,1)} %param.30) | copy-start | bytes 138628
  37.7 1.8 %copy-start.13 = (bf16[76,1,7,7]{0,3,2,1:T(8,128)(2,1)S(1)}, bf16[76,1,7,7]{0,3,2,1:T(8,128)(2,1)}, u32[]{:S(2)}) copy-start(bf16[76,1,7,7]{0,3,2,1:T(8,128)(2,1)} %param.28) | copy-start | bytes 22348
  37.7 1.9 %copy-start.16 = (f32[76]{0:T(128)S(1)}, f32[76]{0:T(128)}, u32[]{:S(2)}) copy-start(f32[76]{0:T(128)} %param.29) | copy-start | bytes 916
  37.7 2.1 %copy-start.14 = (s32[5,5]{1,0:T(8,128)S(1)}, s32[5,5]{1,0:T(8,128)}, u32[]{:S(2)}) copy-start(s32[5,5]{1,0:T(8,128)} %param.27) | copy-start | bytes 304
  37.7 2.1 %copy-start.15 = (f32[76,4]{0,1:T(4,128)S(1)}, f32[76,4]{0,1:T(4,128)}, u32[]{:S(2)}) copy-start(f32[76,4]{0,1:T(4,128)} %param.25) | copy-start | bytes 3652
  37.7 2.2 %copy-start = (bf16[76,45,180]{2,0,1:T(8,128)(2,1)S(1)}, bf16[76,45,180]{2,0,1:T(8,128)(2,1)}, u32[]{:S(2)}) copy-start(bf16[76,45,180]{2,0,1:T(8,128)(2,1)} %param.26) | copy-start | bytes 3693604
  37.7 2.2 %copy-start.2 = (bf16[16,384]{1,0:T(8,128)(2,1)S(1)}, bf16[16,384]{1,0:T(8,128)(2,1)}, u32[]{:S(2)}) copy-start(bf16[16,384]{1,0:T(8,128)(2,1)} %constant.27.clone.picks_ref) | copy-start | bytes 36868
  49.0 1.6 %copy-start.3 = (f32[23,76,384]{2,1,0:T(8,128)}, f32[23,76,384]{2,1,0:T(8,128)S(1)}, u32[]{:S(2)}) copy-start(f32[23,76,384]{2,1,0:T(8,128)S(1)} %get-tuple-element.21.forcing_ref) | copy-start | bytes 8054788
  50.6 1.1 copy-start.5
  51.7 1.1 copy-start.7
  52.8 22.1 %collective-permute-start = (bf16[3,76,192]{2,1,0:T(8,128)(2,1)S(1)}, bf16[3,76,192]{2,1,0:T(8,128)(2,1)S(1)}, u32[]{:S(2)}, u32[]{:S(2)}) collective-permute-start(bf16[3,76,192]{2,1,0:T(8,128)(2,1)S(1)} %get-tuple-element.17), channel_id=1, source_target_pairs={{0,8},{8,16},{16,24},{24,32},{32,40},{40,48},{48,56},{56,64},{64,7... | collective-permute-start | bytes 262664 | tf_op jit(solution)/shard_map/ppermute | solution.py:695
  56.1 18.8 %collective-permute-start.1 = (bf16[3,76,192]{2,1,0:T(8,128)(2,1)S(1)}, bf16[3,76,192]{2,1,0:T(8,128)(2,1)S(1)}, u32[]{:S(2)}, u32[]{:S(2)}) collective-permute-start(bf16[3,76,192]{2,1,0:T(8,128)(2,1)S(1)} %get-tuple-element.16), channel_id=1, source_target_pairs={{8,0},{16,8},{24,16},{32,24},{40,32},{48,40},{56,48},{64,56},{72,6... | collective-permute-start | bytes 262664 | tf_op jit(solution)/shard_map/ppermute | solution.py:695
  74.9 5.0 %copy-start.9 = (bf16[76,304]{1,0:T(8,128)(2,1)S(1)}, bf16[76,304]{1,0:T(8,128)(2,1)}, u32[]{:S(2)}) copy-start(bf16[76,304]{1,0:T(8,128)(2,1)} %contract_ref.1) | copy-start | bytes 138628
  74.9 37.4 %all-to-all-start.2 = ((bf16[128,24,384]{2,1,0:T(8,128)(2,1)}), bf16[128,24,384]{2,1,0:T(8,128)(2,1)}, u32[]{:S(2)}, u32[]{:S(2)}) async-start(bf16[128,24,384]{2,1,0:T(8,128)(2,1)} %bitcast.43), calls=%async_computation.2 | async-start | bytes 4718592 | tf_op jit(solution)/shard_map/all_to_all | solution.py:732
  79.9 1.8 %copy-start.4 = (f32[23,76,384]{2,1,0:T(8,128)S(1)}, f32[23,76,384]{2,1,0:T(8,128)}, u32[]{:S(2)}) copy-start(f32[23,76,384]{2,1,0:T(8,128)} %copy-done.3) | copy-start | bytes 8054788
  81.7 1.4 %copy-start.6 = (bf16[23,76,384]{2,1,0:T(8,128)(2,1)S(1)}, bf16[23,76,384]{2,1,0:T(8,128)(2,1)}, u32[]{:S(2)}) copy-start(bf16[23,76,384]{2,1,0:T(8,128)(2,1)} %copy-done.5) | copy-start | bytes 4027396
  83.1 1.4 %copy-start.8 = (bf16[23,76,384]{2,1,0:T(8,128)(2,1)S(1)}, bf16[23,76,384]{2,1,0:T(8,128)(2,1)}, u32[]{:S(2)}) copy-start(bf16[23,76,384]{2,1,0:T(8,128)(2,1)} %copy-done.7) | copy-start | bytes 4027396
